TPU v7x, 128 devices: a whole 4x4x4 slice. The times are simulated.
128 devices in a mesh: shot: 2 (over y_hi), gx: 8 (over y_lo, z), gy: 8 (over x, core).
Axes of the slice: x: 4, y: 4 (y_hi: 2, y_lo: 2; y = y_hi * 2 + y_lo), z: 4, core: 2. Of those that a mesh axis runs over, the one named last changes fastest.
Arguments:
- coef: float32 [256, 256, 256], P('gx', 'gy'), may hold values from 0.1 to 0.3
- wave_now: float32 [2, 256, 256, 256], P('shot', 'gx', 'gy'), may hold values from -6 to 6
- wave_prev: float32 [2, 256, 256, 256], P('shot', 'gx', 'gy'), may hold values from -6 to 6
- adjoint_next: float32 [2, 256, 256, 256], P('shot', 'gx', 'gy'), may hold values from -1.5 to 1.5
- adjoint_after: float32 [2, 256, 256, 256], P('shot', 'gx', 'gy'), may hold values from -1.5 to 1.5
- noise: float32 [256, 256, 256], P('gx', 'gy'), may hold values from -6 to 6
- observed: float32 [2, 4096, 16], P('shot', ('gx', 'gy')), may hold values from -6 to 6
- recv_tile: int32 [4096, 1], P(('gx', 'gy')), may hold values from 0 to 63; in each aligned block of 64 rows (0 to 63, 64 to 127, ...) at most 2 rows name the same one
- recv_cell: int32 [4096], P(('gx', 'gy')), may hold values from 0 to 1023
Outputs:
- sample: float32 [256, 256, 256], P('gx', 'gy')
- gradient: float32 [256, 256, 256], P('gx', 'gy')
Inputs may be any that keep to these rules, and one draw needn't show every extreme that they name: `recv_tile`: among the receivers of one device no tile appears more than 2 times, a bound that some block reaches; every tile holds some receiver.
All inputs are finite; a program needn't handle non-finite values.
Results may differ from a plain program's by a relative error of at most 0.00025.
Values sent between devices are 32-bit elements; how exact they have to be, the bound alone decides.
No kernel may reach another device: no remote copies, remote signals or barrier semaphores. Data moves between devices by JAX's collectives and lax.ppermute only.
A program may use at most 128 MiB of HBM per device.

v0:
```python
import math

import jax
import jax.numpy as jnp
from jax import lax
from jax.sharding import PartitionSpec as P

STEPS = 16
DEPTH = 2


step_eta = 0.01
prior_prec = 4.0
prior_centre = 0.2


def extended(block, sides, width):
    for axis, dim in sides:
        count = lax.axis_size(axis)
        forward = [(i, i + 1) for i in range(count - 1)]
        backward = [(target, source) for source, target in forward]
        low = lax.ppermute(
            lax.slice_in_dim(block, block.shape[dim] - width, None, axis=dim), axis, forward
        )
        high = lax.ppermute(lax.slice_in_dim(block, 0, width, axis=dim), axis, backward)
        block = jnp.concatenate([low, block, high], axis=dim)
    return block


def lap_core(padded):
    centre = padded[1:-1, 1:-1]
    zero_face = jnp.zeros_like(centre[:, :, :1])
    shifted_up = jnp.concatenate((centre[:, :, 1:], zero_face), 2)
    shifted_down = jnp.concatenate((zero_face, centre[:, :, :-1]), 2)
    lateral = padded[2:, 1:-1] + padded[:-2, 1:-1] + padded[1:-1, 2:] + padded[1:-1, :-2]
    return lateral + shifted_up + shifted_down - 6.0 * centre


def local(
    coef, wave_now, wave_prev, adjoint_next, adjoint_after, noise, observed, recv_tile, recv_cell
):
    rows_x, rows_y, depth_cells = coef.shape
    cell_count = rows_x * rows_y
    tile_count = lax.axis_size(("gx", "gy"))
    highest = lax.Precision.HIGHEST
    depth_mask = (jnp.arange(depth_cells, dtype=jnp.int32) == DEPTH).astype(jnp.float32)

    def depth_pick(field):
        flat_field = field.reshape(field.shape[0] * field.shape[1], depth_cells)
        return jnp.dot(
            flat_field, depth_mask, precision=highest, preferred_element_type=jnp.float32
        )

    tile_of = recv_tile[:, 0]
    per_tile = max(2, 2 * observed.shape[1] // tile_count)
    slot_count = tile_count * per_tile
    owner_hot = (tile_of[:, None] == jnp.arange(tile_count, dtype=jnp.int32)[None, :]).astype(
        jnp.int32
    )
    before = jnp.cumsum(owner_hot, 0) - owner_hot
    slot_of = tile_of * per_tile + jnp.sum(before * owner_hot, 1)
    routing = slot_of[None, :] == jnp.arange(slot_count, dtype=jnp.int32)[:, None]
    outgoing = jnp.dot(
        routing.astype(jnp.float32),
        observed[0],
        precision=highest,
        preferred_element_type=jnp.float32,
    )
    cell_marks = jnp.sum(jnp.where(routing, recv_cell[None, :] + 1, 0), 1).astype(jnp.float32) - 1.0
    arrived, arrived_cells = (
        lax.all_to_all(
            outgoing.reshape(tile_count, per_tile, STEPS),
            ("gx", "gy"),
            split_axis=0,
            concat_axis=0,
            tiled=True,
        ),
        lax.all_to_all(
            cell_marks.reshape(tile_count, per_tile),
            ("gx", "gy"),
            split_axis=0,
            concat_axis=0,
            tiled=True,
        ),
    )
    obs_rows = arrived.reshape(slot_count, STEPS)
    cell_rows = arrived_cells.reshape(-1).astype(jnp.int32)
    picker = (cell_rows[:, None] == jnp.arange(cell_count, dtype=jnp.int32)[None, :]).astype(
        jnp.float32
    )

    def forward(carried, unused):
        previous, current = carried
        padded = extended(current, (("gx", 0), ("gy", 1)), 1)
        laplace = lap_core(padded)
        updated = 2.0 * current - previous + coef * laplace
        return ((current, updated), (laplace, depth_pick(updated)))

    _, (laps, surface) = lax.scan(forward, (wave_prev[0], wave_now[0]), None, length=STEPS)
    predicted = jnp.dot(surface, picker.T, precision=highest, preferred_element_type=jnp.float32)
    residual = predicted - obs_rows.T
    injected = jnp.dot(residual, picker, precision=highest, preferred_element_type=jnp.float32)

    def backward(carried, inputs):
        later_one, later_two, gradient = carried
        laplace, inject_now = inputs
        padded = extended(coef * later_one, (("gx", 0), ("gy", 1)), 1)
        source = inject_now.reshape(rows_x, rows_y)[:, :, None] * depth_mask
        adjoint = 2.0 * later_one - later_two + lap_core(padded) + source
        return ((adjoint, later_one, gradient + laplace * adjoint), None)

    zeros_field = jnp.zeros(coef.shape, jnp.float32)
    (_, _, gradient), _ = lax.scan(
        backward, (adjoint_next[0], adjoint_after[0], zeros_field), (laps, injected), reverse=True
    )
    total = lax.psum(gradient, "shot")
    sample = (
        coef
        + step_eta * (prior_prec * (prior_centre - coef) - total)
        + math.sqrt(2.0 * step_eta) * noise
    )
    return (sample, total)


def solution(mesh):
    return jax.shard_map(
        local,
        mesh=mesh,
        in_specs=(
            P("gx", "gy", None),
            P("shot", "gx", "gy", None),
            P("shot", "gx", "gy", None),
            P("shot", "gx", "gy", None),
            P("shot", "gx", "gy", None),
            P("gx", "gy", None),
            P("shot", ("gx", "gy"), None),
            P(("gx", "gy"), None),
            P(("gx", "gy")),
        ),
        out_specs=(P("gx", "gy", None), P("gx", "gy", None)),
        check_vma=False,
    )
```

profile of v0, /device:TPU:10, one launch (start us, length us, event | category | flops | bytes accessed | tf_op | source)
XLA Modules:
  0.0 865.7 jit_solution(9068362023434331601)
XLA Ops:
  12.9 9.9 %all-to-all-start = ((f32[64,1,2]{2,1,0:T(1,128)}), f32[64,1,2]{2,1,0:T(1,128)S(1)}, u32[]{:S(2)}, u32[]{:S(2)}) async-start(f32[64,1,2]{2,1,0:T(1,128)} %bitcast.5), calls=%async_computation | async-start | bytes 65536 | tf_op jit(solution)/shard_map/all_to_all | solution.py:78
  23.9 5.2 all-to-all-done
  29.1 6.4 all-to-all-start.1
  35.8 6.0 all-to-all-done.1
  41.9 394.8 %while.36 = (s32[]{:T(128)}, f32[32,32,256]{2,1,0:T(8,128)}, f32[32,32,256]{2,1,0:T(8,128)S(1)}, f32[16,32,32,256]{3,2,1,0:T(8,128)}, f32[16,1024]{1,0:T(8,128)S...) while((s32[]{:T(128)}, f32[32,32,256]{2,1,0:T(8,128)}, f32[32,32,256]{2,1,0:T(8,128)S(1)}, ...), condition=%wide.region_1.2_spmd.clone, body=%wide.region_0.0_spmd.clone.sunk | while | flops 7078402 | bytes 32860476 | solution.py:99
  44.6 5.4 collective-permute-start.1
  68.6 6.1 collective-permute-start.1
  93.3 6.1 collective-permute-start.1
  117.9 6.1 collective-permute-start.1
  142.6 6.1 collective-permute-start.1
  167.2 6.1 collective-permute-start.1
  191.9 6.1 collective-permute-start.1
  216.5 6.1 collective-permute-start.1
  241.3 6.1 collective-permute-start.1
  266.0 6.1 collective-permute-start.1
  290.7 6.1 collective-permute-start.1
  315.3 6.1 collective-permute-start.1
  340.0 6.1 collective-permute-start.1
  364.7 6.1 collective-permute-start.1
  389.3 6.1 collective-permute-start.1
  414.0 6.1 collective-permute-start.1
  437.4 371.6 %while.37 = (s32[]{:T(128)}, f32[32,32,256]{2,1,0:T(8,128)S(1)}, f32[32,32,256]{2,1,0:T(8,128)}, f32[32,32,256]{2,1,0:T(8,128)}, f32[32,32,256]{2,1,0:T(8,128)S(...) while((s32[]{:T(128)}, f32[32,32,256]{2,1,0:T(8,128)S(1)}, ...), condition=%wide.region_6.7_spmd.clone, body=%wide.region_5.6_spmd.clone.sunk | while | flops 6326788 | bytes 22960420 | solution.py:113
  437.7 6.1 collective-permute-start.4
  481.7 4.6 fusion.57
  504.7 4.6 fusion.57
  527.7 4.6 fusion.57
  550.7 4.6 fusion.57
  573.6 4.6 fusion.57
  596.6 4.6 fusion.57
  619.6 4.6 fusion.57
  711.5 4.6 fusion.57
  809.1 46.1 %all-reduce.6.cloned.1.call-done = f32[32,32,256]{2,1,0:T(8,128)} async-done(((f32[32,32,256]{2,1,0:T(8,128)}), f32[32,32,256]{2,1,0:T(8,128)}) %all-reduce.6.cloned.1.call-update) | async-done | bytes 1048592 | tf_op jit(solution)/shard_map/psum | solution.py:116
  (705 shorter events, 634.5 us)
Async XLA Ops:
  12.9 16.2 %all-to-all-start = ((f32[64,1,2]{2,1,0:T(1,128)}), f32[64,1,2]{2,1,0:T(1,128)S(1)}, u32[]{:S(2)}, u32[]{:S(2)}) async-start(f32[64,1,2]{2,1,0:T(1,128)} %bitcast.5), calls=%async_computation | async-start | bytes 65536 | tf_op jit(solution)/shard_map/all_to_all | solution.py:78
  29.1 12.7 %all-to-all-start.1 = ((f32[64,2,16]{2,1,0:T(2,128)}), f32[64,2,16]{2,1,0:T(2,128)S(1)}, u32[]{:S(2)}, u32[]{:S(2)}) async-start(f32[64,2,16]{2,1,0:T(2,128)} %copy.16), calls=%async_computation.1 | async-start | bytes 131072 | tf_op jit(solution)/shard_map/all_to_all | solution.py:71
  35.5 819.8 %all-reduce.6.cloned.1.call-start = ((), (), s32[]{:S(2)}) async-start(), calls=%async_computation.2 | async-start | bytes 2097152 | tf_op jit(solution)/shard_map/psum | solution.py:116
  41.9 9.8 %collective-permute-start = (f32[1,32,256]{2,1,0:T(8,128)S(1)}, f32[1,32,256]{2,1,0:T(8,128)S(1)}, u32[]{:S(2)}, u32[]{:S(2)}) collective-permute-start(f32[1,32,256]{2,1,0:T(8,128)S(1)} %get-tuple-element.378), channel_id=1, source_target_pairs={{0,8},{8,16},{16,24},{24,32},{32,40},{40,48},{48,56},{1,9},{9,17},... | collective-permute-start | bytes 98312 | tf_op jit(solution)/shard_map/while/body/eval_jaxpr/ppermute | solution.py:22
  66.7 9.7 %collective-permute-start = (f32[1,32,256]{2,1,0:T(8,128)S(1)}, f32[1,32,256]{2,1,0:T(8,128)S(1)}, u32[]{:S(2)}, u32[]{:S(2)}) collective-permute-start(f32[1,32,256]{2,1,0:T(8,128)S(1)} %get-tuple-element.378), channel_id=1, source_target_pairs={{0,8},{8,16},{16,24},{24,32},{32,40},{40,48},{48,56},{1,9},{9,17},... | collective-permute-start | bytes 98312 | tf_op jit(solution)/shard_map/while/body/eval_jaxpr/ppermute | solution.py:22
  91.3 9.7 %collective-permute-start = (f32[1,32,256]{2,1,0:T(8,128)S(1)}, f32[1,32,256]{2,1,0:T(8,128)S(1)}, u32[]{:S(2)}, u32[]{:S(2)}) collective-permute-start(f32[1,32,256]{2,1,0:T(8,128)S(1)} %get-tuple-element.378), channel_id=1, source_target_pairs={{0,8},{8,16},{16,24},{24,32},{32,40},{40,48},{48,56},{1,9},{9,17},... | collective-permute-start | bytes 98312 | tf_op jit(solution)/shard_map/while/body/eval_jaxpr/ppermute | solution.py:22
  116.0 9.7 %collective-permute-start = (f32[1,32,256]{2,1,0:T(8,128)S(1)}, f32[1,32,256]{2,1,0:T(8,128)S(1)}, u32[]{:S(2)}, u32[]{:S(2)}) collective-permute-start(f32[1,32,256]{2,1,0:T(8,128)S(1)} %get-tuple-element.378), channel_id=1, source_target_pairs={{0,8},{8,16},{16,24},{24,32},{32,40},{40,48},{48,56},{1,9},{9,17},... | collective-permute-start | bytes 98312 | tf_op jit(solution)/shard_map/while/body/eval_jaxpr/ppermute | solution.py:22
  140.6 9.7 %collective-permute-start = (f32[1,32,256]{2,1,0:T(8,128)S(1)}, f32[1,32,256]{2,1,0:T(8,128)S(1)}, u32[]{:S(2)}, u32[]{:S(2)}) collective-permute-start(f32[1,32,256]{2,1,0:T(8,128)S(1)} %get-tuple-element.378), channel_id=1, source_target_pairs={{0,8},{8,16},{16,24},{24,32},{32,40},{40,48},{48,56},{1,9},{9,17},... | collective-permute-start | bytes 98312 | tf_op jit(solution)/shard_map/while/body/eval_jaxpr/ppermute | solution.py:22
  165.3 9.7 %collective-permute-start = (f32[1,32,256]{2,1,0:T(8,128)S(1)}, f32[1,32,256]{2,1,0:T(8,128)S(1)}, u32[]{:S(2)}, u32[]{:S(2)}) collective-permute-start(f32[1,32,256]{2,1,0:T(8,128)S(1)} %get-tuple-element.378), channel_id=1, source_target_pairs={{0,8},{8,16},{16,24},{24,32},{32,40},{40,48},{48,56},{1,9},{9,17},... | collective-permute-start | bytes 98312 | tf_op jit(solution)/shard_map/while/body/eval_jaxpr/ppermute | solution.py:22
  190.0 9.7 %collective-permute-start = (f32[1,32,256]{2,1,0:T(8,128)S(1)}, f32[1,32,256]{2,1,0:T(8,128)S(1)}, u32[]{:S(2)}, u32[]{:S(2)}) collective-permute-start(f32[1,32,256]{2,1,0:T(8,128)S(1)} %get-tuple-element.378), channel_id=1, source_target_pairs={{0,8},{8,16},{16,24},{24,32},{32,40},{40,48},{48,56},{1,9},{9,17},... | collective-permute-start | bytes 98312 | tf_op jit(solution)/shard_map/while/body/eval_jaxpr/ppermute | solution.py:22
  214.6 9.7 %collective-permute-start = (f32[1,32,256]{2,1,0:T(8,128)S(1)}, f32[1,32,256]{2,1,0:T(8,128)S(1)}, u32[]{:S(2)}, u32[]{:S(2)}) collective-permute-start(f32[1,32,256]{2,1,0:T(8,128)S(1)} %get-tuple-element.378), channel_id=1, source_target_pairs={{0,8},{8,16},{16,24},{24,32},{32,40},{40,48},{48,56},{1,9},{9,17},... | collective-permute-start | bytes 98312 | tf_op jit(solution)/shard_map/while/body/eval_jaxpr/ppermute | solution.py:22
  239.3 9.7 %collective-permute-start = (f32[1,32,256]{2,1,0:T(8,128)S(1)}, f32[1,32,256]{2,1,0:T(8,128)S(1)}, u32[]{:S(2)}, u32[]{:S(2)}) collective-permute-start(f32[1,32,256]{2,1,0:T(8,128)S(1)} %get-tuple-element.378), channel_id=1, source_target_pairs={{0,8},{8,16},{16,24},{24,32},{32,40},{40,48},{48,56},{1,9},{9,17},... | collective-permute-start | bytes 98312 | tf_op jit(solution)/shard_map/while/body/eval_jaxpr/ppermute | solution.py:22
  264.1 9.7 %collective-permute-start = (f32[1,32,256]{2,1,0:T(8,128)S(1)}, f32[1,32,256]{2,1,0:T(8,128)S(1)}, u32[]{:S(2)}, u32[]{:S(2)}) collective-permute-start(f32[1,32,256]{2,1,0:T(8,128)S(1)} %get-tuple-element.378), channel_id=1, source_target_pairs={{0,8},{8,16},{16,24},{24,32},{32,40},{40,48},{48,56},{1,9},{9,17},... | collective-permute-start | bytes 98312 | tf_op jit(solution)/shard_map/while/body/eval_jaxpr/ppermute | solution.py:22
  288.7 9.7 %collective-permute-start = (f32[1,32,256]{2,1,0:T(8,128)S(1)}, f32[1,32,256]{2,1,0:T(8,128)S(1)}, u32[]{:S(2)}, u32[]{:S(2)}) collective-permute-start(f32[1,32,256]{2,1,0:T(8,128)S(1)} %get-tuple-element.378), channel_id=1, source_target_pairs={{0,8},{8,16},{16,24},{24,32},{32,40},{40,48},{48,56},{1,9},{9,17},... | collective-permute-start | bytes 98312 | tf_op jit(solution)/shard_map/while/body/eval_jaxpr/ppermute | solution.py:22
  313.4 9.7 %collective-permute-start = (f32[1,32,256]{2,1,0:T(8,128)S(1)}, f32[1,32,256]{2,1,0:T(8,128)S(1)}, u32[]{:S(2)}, u32[]{:S(2)}) collective-permute-start(f32[1,32,256]{2,1,0:T(8,128)S(1)} %get-tuple-element.378), channel_id=1, source_target_pairs={{0,8},{8,16},{16,24},{24,32},{32,40},{40,48},{48,56},{1,9},{9,17},... | collective-permute-start | bytes 98312 | tf_op jit(solution)/shard_map/while/body/eval_jaxpr/ppermute | solution.py:22
  338.1 9.7 %collective-permute-start = (f32[1,32,256]{2,1,0:T(8,128)S(1)}, f32[1,32,256]{2,1,0:T(8,128)S(1)}, u32[]{:S(2)}, u32[]{:S(2)}) collective-permute-start(f32[1,32,256]{2,1,0:T(8,128)S(1)} %get-tuple-element.378), channel_id=1, source_target_pairs={{0,8},{8,16},{16,24},{24,32},{32,40},{40,48},{48,56},{1,9},{9,17},... | collective-permute-start | bytes 98312 | tf_op jit(solution)/shard_map/while/body/eval_jaxpr/ppermute | solution.py:22
  362.8 9.7 %collective-permute-start = (f32[1,32,256]{2,1,0:T(8,128)S(1)}, f32[1,32,256]{2,1,0:T(8,128)S(1)}, u32[]{:S(2)}, u32[]{:S(2)}) collective-permute-start(f32[1,32,256]{2,1,0:T(8,128)S(1)} %get-tuple-element.378), channel_id=1, source_target_pairs={{0,8},{8,16},{16,24},{24,32},{32,40},{40,48},{48,56},{1,9},{9,17},... | collective-permute-start | bytes 98312 | tf_op jit(solution)/shard_map/while/body/eval_jaxpr/ppermute | solution.py:22
  387.4 9.7 %collective-permute-start = (f32[1,32,256]{2,1,0:T(8,128)S(1)}, f32[1,32,256]{2,1,0:T(8,128)S(1)}, u32[]{:S(2)}, u32[]{:S(2)}) collective-permute-start(f32[1,32,256]{2,1,0:T(8,128)S(1)} %get-tuple-element.378), channel_id=1, source_target_pairs={{0,8},{8,16},{16,24},{24,32},{32,40},{40,48},{48,56},{1,9},{9,17},... | collective-permute-start | bytes 98312 | tf_op jit(solution)/shard_map/while/body/eval_jaxpr/ppermute | solution.py:22
  412.0 9.7 %collective-permute-start = (f32[1,32,256]{2,1,0:T(8,128)S(1)}, f32[1,32,256]{2,1,0:T(8,128)S(1)}, u32[]{:S(2)}, u32[]{:S(2)}) collective-permute-start(f32[1,32,256]{2,1,0:T(8,128)S(1)} %get-tuple-element.378), channel_id=1, source_target_pairs={{0,8},{8,16},{16,24},{24,32},{32,40},{40,48},{48,56},{1,9},{9,17},... | collective-permute-start | bytes 98312 | tf_op jit(solution)/shard_map/while/body/eval_jaxpr/ppermute | solution.py:22
  437.7 9.7 %collective-permute-start.4 = (f32[1,32,256]{2,1,0:T(8,128)S(1)}, f32[1,32,256]{2,1,0:T(8,128)S(1)}, u32[]{:S(2)}, u32[]{:S(2)}) collective-permute-start(f32[1,32,256]{2,1,0:T(8,128)S(1)} %get-tuple-element.393), channel_id=1, source_target_pairs={{8,0},{16,8},{24,16},{32,24},{40,32},{48,40},{56,48},{9,1},{17,9},... | collective-permute-start | bytes 98312 | tf_op jit(solution)/shard_map/while/body/eval_jaxpr/ppermute | solution.py:25
  466.6 7.9 collective-permute-start.5
  489.6 7.9 collective-permute-start.5
  535.5 7.9 collective-permute-start.5
  558.5 7.9 collective-permute-start.5
  581.5 7.9 collective-permute-start.5
  604.4 7.9 collective-permute-start.5
  650.4 7.9 collective-permute-start.5
  673.4 7.9 collective-permute-start.5
  696.3 7.9 collective-permute-start.5
  719.3 7.9 collective-permute-start.5
  765.3 7.9 collective-permute-start.5
  788.2 7.9 collective-permute-start.5
  (140 other events, 1223.6 us)
Sparse Core Ops, SparseCore 0:
  809.2 45.9 all-reduce.5
where the time goes:
time: 871 us; the launch traced here: 866 us
  starting transfers between devices  418 us (48%)
  other arithmetic  151 us (17%)
  waiting for transfers between devices  145 us (17%)
  local copies, waits for them, and re-layouts  117 us (13%)
  matrix products  16.6 us (2%)
  between operations  14.2 us (2%)
    ppermute x64, starting transfers between devices, extended(): lax.ppermute(lax.slice_in_dim(block, 0, width, axis=dim), axis, backward)  247 us
    ppermute x64, starting transfers between devices, extended(): lax.ppermute(lax.slice_in_dim(block, block.shape[dim] - width, None, axis...  155 us
    add x16, other arithmetic, backward(): return ((adjoint, later_one, gradient + laplace * adjoint), None)  74 us
    dynamic_update_slice x16, other arithmetic, local(): lax.scan(forward, (wave_prev[0], wave_now[0]), None, length=STEPS)  63.2 us
    slice x32, local copies, waits for them, and re-layouts, lap_core(): shifted_up = jnp.concatenate((centre[:, :, 1:], zero_face), 2)  54 us
    while x160, local copies, waits for them, and re-layouts  51.6 us
    ppermute x64, waiting for transfers between devices, extended(): lax.ppermute(lax.slice_in_dim(block, 0, width, axis=dim), axis, backward)  48.9 us
    psum x1, waiting for transfers between devices, local(): total = lax.psum(gradient, 'shot')  46.1 us
  transfers between devices with their start and end apart: 131, of which 51 were waited for; matrix products, arithmetic and copies ran while one was open for 7% of the time, Pallas kernels for 0%

commit v1 on v0

v1 whole, which is shorter than its diff:
```python
import functools
import math

import jax
import jax.numpy as jnp
from jax import lax
from jax.experimental import pallas as pl
from jax.experimental.pallas import tpu as pltpu
from jax.sharding import PartitionSpec as P

STEPS = 16
DEPTH = 2
K = 8
VMEM_LIMIT = 48 * 1024 * 1024

step_eta = 0.01
prior_prec = 4.0
prior_centre = 0.2


def pairs(count, odd):
    found = []
    for low in range(1 if odd else 0, count - 1, 2):
        found += [(low, low + 1), (low + 1, low)]
    return found


def swap(axis, even, low, high):
    count = lax.axis_size(axis)
    first = lax.ppermute(jnp.where(even, high, low), axis, pairs(count, False))
    second = lax.ppermute(jnp.where(even, low, high), axis, pairs(count, True))
    return first, second


def exchange(even_x, even_y, fields):
    rows, cols = fields.shape[1], fields.shape[2]
    x_first, x_second = swap("gx", even_x, fields[:, :K], fields[:, rows - K :])
    below = jnp.where(even_x, x_second, x_first)
    above = jnp.where(even_x, x_first, x_second)
    low = jnp.concatenate([below[:, :, :K], fields[:, :, :K], above[:, :, :K]], 1)
    high = jnp.concatenate(
        [below[:, :, cols - K :], fields[:, :, cols - K :], above[:, :, cols - K :]], 1
    )
    y_first, y_second = swap("gy", even_y, low, high)
    return x_first, x_second, y_first, y_second


def block_kernel(shape, adjoint, initial, base, parity, *refs):
    rows, cols, depth = shape
    own_refs, refs = refs[:3], refs[3:]
    halo_refs, refs = refs[:8], refs[8:]
    if adjoint:
        laps, inject, grad_in, newest, older, grad, first, second, coef, sems, out_sems = refs
    else:
        newest, older, laps, surface, first, second, coef, sems, out_sems = refs
    turn_of = pl.program_id(0)
    groups = cols // 8 + 2
    halves = depth // 128
    edge = K + 1
    lane = lax.broadcasted_iota(jnp.int32, (8, 128), 1)
    line = lax.broadcasted_iota(jnp.int32, (8, 128), 0)
    last_lane, first_lane = lane == 127, lane == 0
    last_line, first_line = line == 7, line == 0
    zero = jnp.zeros((8, 128), jnp.float32)

    @pl.when(turn_of == 0)
    def _():
        x_first = jnp.where(parity[0] == 0, rows + K, 0) + 1
        x_second = jnp.where(parity[0] == 0, 0, rows + K) + 1
        y_first = pl.multiple_of(jnp.where(parity[1] == 0, cols + K, 0), 8)
        y_second = pl.multiple_of(jnp.where(parity[1] == 0, 0, cols + K), 8)
        copies = []
        for index, (own, target) in enumerate(zip(own_refs, (first, second, coef))):
            halos = halo_refs[4:] if index == 2 else halo_refs[:4]
            inner = pl.ds(K, cols)
            for source, place in (
                (own, target.at[pl.ds(edge, rows), inner]),
                (halos[0].at[index], target.at[pl.ds(x_first, K), inner]),
                (halos[1].at[index], target.at[pl.ds(x_second, K), inner]),
                (halos[2].at[index], target.at[pl.ds(1, rows + 2 * K), pl.ds(y_first, K)]),
                (halos[3].at[index], target.at[pl.ds(1, rows + 2 * K), pl.ds(y_second, K)]),
            ):
                copies.append(pltpu.make_async_copy(source, place, sems.at[len(copies)]))
        for copy in copies:
            copy.start()
        for field in (first, second, coef):
            field[0] = jnp.zeros(field.shape[1:], jnp.float32)
            field[rows + 2 * K + 1] = jnp.zeros(field.shape[1:], jnp.float32)
        for copy in copies:
            copy.wait()
        if adjoint and initial:

            def weigh(x, carried):
                first[x] = first[x] * coef[x]
                second[x] = second[x] * coef[x]
                return carried

            lax.fori_loop(1, rows + 2 * K + 1, weigh, 0)
        if adjoint:
            grad[...] = grad_in[...]
        else:
            surface[...] = jnp.zeros(surface.shape, jnp.float32)

    def row(x, source, target, half, inside):
        step = 2 * turn_of + half
        if adjoint:
            turn = lax.rem(128 + DEPTH - (base - step), 128)
            slot = 1 - half
        else:
            turn = lax.rem(128 - DEPTH + base + step, 128)
            mark = lane == base + step
            slot = half

        def read(at_x, g, h):
            return source[at_x, pl.ds(8 * g, 8), pl.ds(128 * h, 128)]

        centre = [[read(x, g, h) for h in range(halves)] for g in range(groups)]
        ups = [[pltpu.roll(c, 7, 0) for c in line_of] for line_of in centre]
        downs = [[pltpu.roll(c, 1, 0) for c in line_of] for line_of in centre]
        done = []
        for g in range(groups):
            lefts = [pltpu.roll(c, 127, 1) for c in centre[g]]
            rights = [pltpu.roll(c, 1, 1) for c in centre[g]]
            for h in range(halves):
                c = centre[g][h]
                at = (x, pl.ds(8 * g, 8), pl.ds(128 * h, 128))
                up = jnp.where(last_line, ups[g + 1][h], ups[g][h]) if g + 1 < groups else ups[g][h]
                down = jnp.where(first_line, downs[g - 1][h], downs[g][h]) if g > 0 else downs[g][h]
                left = jnp.where(last_lane, lefts[h + 1] if h + 1 < halves else zero, lefts[h])
                right = jnp.where(first_lane, rights[h - 1] if h > 0 else zero, rights[h])
                lateral = (read(x + 1, g, h) + read(x - 1, g, h)) + (up + down)
                laplace = lateral + (left + right) - 6.0 * c
                forced = laplace
                if adjoint and h == 0:
                    moved = pltpu.roll(inject[x - 1, pl.ds(8 * g, 8), :], turn, 1)
                    forced = laplace + jnp.where(lane == DEPTH, moved, 0.0)
                fresh = (2.0 * c - target[at]) + coef[at] * forced
                done.append((g, h, at, laplace, fresh))
        for g, h, at, laplace, fresh in done:
            target[at] = fresh
            if inside and 0 < g < groups - 1:
                mine = (x - edge, pl.ds(8 * g - 8, 8), pl.ds(128 * h, 128))
                if adjoint:
                    grad[mine] = grad[mine] + laps[(slot,) + mine] * fresh
                else:
                    laps[(slot,) + mine] = laplace
                    if h == 0:
                        seen = pltpu.roll(fresh, turn, 1)
                        flat = (x - edge, pl.ds(8 * g - 8, 8), slice(None))
                        surface[flat] = jnp.where(mark, seen, surface[flat])

    def sweep(source, target, half):
        def rows_from(begin, count, unroll, inside):
            def body(index, carried):
                for offset in range(unroll):
                    row(begin + index * unroll + offset, source, target, half, inside)
                return carried

            lax.fori_loop(0, count, body, 0)

        count = K // 2 - turn_of - half
        rows_from(edge - 2 * count, count, 2, False)
        rows_from(edge, rows // 4, 4, True)
        rows_from(edge + rows, count, 2, False)

    sweep(first, second, 0)
    sweep(second, first, 1)

    @pl.when(turn_of == K // 2 - 1)
    def _():
        inner = (pl.ds(edge, rows), pl.ds(K, cols))
        out_new = pltpu.make_async_copy(first.at[inner], newest, out_sems.at[0])
        out_old = pltpu.make_async_copy(second.at[inner], older, out_sems.at[1])
        out_new.start()
        out_old.start()
        out_new.wait()
        out_old.wait()


def run_block(parity, current, previous, coef, halos, coef_halos, adjoint=None, base=0):
    rows, cols, depth = coef.shape
    extended = (rows + 2 * K + 2, cols + 2 * K)
    any_spec = pl.BlockSpec(memory_space=pl.ANY)
    field = jax.ShapeDtypeStruct(coef.shape, jnp.float32)
    whole = lambda shape: pl.BlockSpec(shape, lambda step: (0,) * len(shape))
    in_specs = [pl.BlockSpec(memory_space=pltpu.SMEM)] + [any_spec] * 11
    operands = [parity, current, previous, coef, *halos, *coef_halos]
    if adjoint is None:
        out_shape = [
            field,
            field,
            jax.ShapeDtypeStruct((K,) + coef.shape, jnp.float32),
            jax.ShapeDtypeStruct((rows, cols, 128), jnp.float32),
        ]
        out_specs = [
            any_spec,
            any_spec,
            pl.BlockSpec((2,) + coef.shape, lambda step: (step, 0, 0, 0)),
            whole((rows, cols, 128)),
        ]
        initial = False
    else:
        laps, inject, gradient, initial = adjoint
        operands += [laps, inject, gradient]
        in_specs += [
            pl.BlockSpec((2,) + coef.shape, lambda step: (K // 2 - 1 - step, 0, 0, 0)),
            whole(inject.shape),
            whole(coef.shape),
        ]
        out_shape = [field, field, field]
        out_specs = [any_spec, any_spec, whole(coef.shape)]
    return pl.pallas_call(
        functools.partial(block_kernel, coef.shape, adjoint is not None, initial, base),
        grid=(K // 2,),
        in_specs=in_specs,
        out_specs=out_specs,
        out_shape=out_shape,
        scratch_shapes=[
            pltpu.VMEM(extended + (depth,), jnp.float32),
            pltpu.VMEM(extended + (depth,), jnp.float32),
            pltpu.VMEM(extended + (depth,), jnp.float32),
            pltpu.SemaphoreType.DMA((15,)),
            pltpu.SemaphoreType.DMA((2,)),
        ],
        compiler_params=pltpu.CompilerParams(vmem_limit_bytes=VMEM_LIMIT),
    )(*operands)


def receivers(observed, recv_tile, recv_cell, cell_count):
    tile_count = lax.axis_size(("gx", "gy"))
    highest = lax.Precision.HIGHEST
    tile_of = recv_tile[:, 0]
    per_tile = max(2, 2 * observed.shape[1] // tile_count)
    slot_count = tile_count * per_tile
    owner_hot = (tile_of[:, None] == jnp.arange(tile_count, dtype=jnp.int32)[None, :]).astype(
        jnp.int32
    )
    before = jnp.cumsum(owner_hot, 0) - owner_hot
    slot_of = tile_of * per_tile + jnp.sum(before * owner_hot, 1)
    routing = (slot_of[None, :] == jnp.arange(slot_count, dtype=jnp.int32)[:, None]).astype(
        jnp.float32
    )
    marks = (recv_cell + 1).astype(jnp.float32)[:, None]
    outgoing = jnp.dot(
        routing,
        jnp.concatenate([observed[0], marks], 1),
        precision=highest,
        preferred_element_type=jnp.float32,
    )
    arrived = lax.all_to_all(
        outgoing.reshape(tile_count, per_tile, STEPS + 1),
        ("gx", "gy"),
        split_axis=0,
        concat_axis=0,
        tiled=True,
    ).reshape(slot_count, STEPS + 1)
    cells = arrived[:, STEPS].astype(jnp.int32) - 1
    picker = (jnp.arange(cell_count, dtype=jnp.int32)[:, None] == cells[None, :]).astype(
        jnp.float32
    )
    seen = jnp.dot(
        picker, arrived[:, :STEPS], precision=highest, preferred_element_type=jnp.float32
    )
    return jnp.sum(picker, 1, keepdims=True), seen


def local(
    coef, wave_now, wave_prev, adjoint_next, adjoint_after, noise, observed, recv_tile, recv_cell
):
    rows, cols, depth = coef.shape
    odd_x, odd_y = lax.axis_index("gx") % 2, lax.axis_index("gy") % 2
    parity = jnp.stack([odd_x, odd_y]).astype(jnp.int32)
    even = (odd_x == 0, odd_y == 0)
    trade = functools.partial(exchange, *even)

    wave_halos = trade(jnp.stack([wave_now[0], wave_prev[0], coef]))
    coef_halos = wave_halos
    adjoint_halos = trade(jnp.stack([adjoint_next[0], adjoint_after[0]]))
    counts, seen = receivers(observed, recv_tile, recv_cell, rows * cols)

    now, then, laps_early, surface_early = run_block(
        parity, wave_now[0], wave_prev[0], coef, wave_halos, coef_halos, base=0
    )
    _, _, laps_late, surface_late = run_block(
        parity, now, then, coef, trade(jnp.stack([now, then])), coef_halos, base=K
    )
    surface = (surface_early + surface_late)[:, :, :STEPS].reshape(rows * cols, STEPS)
    inject = (counts * surface - seen).reshape(1, rows, cols, STEPS)
    x_first, x_second, y_first, y_second = trade(inject)
    below, above = jnp.where(even[0], x_second, x_first), jnp.where(even[0], x_first, x_second)
    left, right = jnp.where(even[1], y_second, y_first), jnp.where(even[1], y_first, y_second)
    middle = jnp.concatenate([below[0], inject[0], above[0]], 0)
    inject = jnp.concatenate([left[0], middle, right[0]], 1)
    inject = jnp.pad(inject, ((0, 0), (0, 0), (0, 128 - STEPS)))

    now, then, gradient = run_block(
        parity,
        adjoint_next[0],
        adjoint_after[0],
        coef,
        adjoint_halos,
        coef_halos,
        adjoint=(laps_late, inject, jnp.zeros(coef.shape, jnp.float32), True),
        base=STEPS - 1,
    )
    _, _, gradient = run_block(
        parity,
        now,
        then,
        coef,
        trade(jnp.stack([now, then])),
        coef_halos,
        adjoint=(laps_early, inject, gradient, False),
        base=K - 1,
    )
    other = lax.ppermute(gradient, "shot", pairs(lax.axis_size("shot"), False))
    total = (gradient + other) / coef
    sample = (
        coef
        + step_eta * (prior_prec * (prior_centre - coef) - total)
        + math.sqrt(2.0 * step_eta) * noise
    )
    return (sample, total)


def solution(mesh):
    return jax.shard_map(
        local,
        mesh=mesh,
        in_specs=(
            P("gx", "gy", None),
            P("shot", "gx", "gy", None),
            P("shot", "gx", "gy", None),
            P("shot", "gx", "gy", None),
            P("shot", "gx", "gy", None),
            P("gx", "gy", None),
            P("shot", ("gx", "gy"), None),
            P(("gx", "gy"), None),
            P(("gx", "gy")),
        ),
        out_specs=(P("gx", "gy", None), P("gx", "gy", None)),
        check_vma=False,
    )
```

time: 871 us -> 268 us (0.31)
  starting transfers between devices: 418 us -> 44.8 us
  other arithmetic: 151 us -> 18.6 us
  local copies, waits for them, and re-layouts: 117 us -> 8.41 us
  Pallas kernels: 0 us -> 95.5 us
  waiting for transfers between devices: 145 us -> 97 us
  matrix products: 16.6 us -> 1.8 us
  between operations: 14.2 us -> 1.27 us
    ppermute x128 -> x21, starting transfers between devices: 402 us -> 37.2 us  [the longest x10 31 us: swap(): second = lax.ppermute(jnp.where(even, low, high), axis, pairs(count, True))]
    pallas_call x0 -> x4, Pallas kernels: none -> 95.5 us  [run_block(): pl.pallas_call(functools.partial(block_kernel, coef.shape, adjoint is not...]
    add x33 -> x2, other arithmetic: 80.9 us -> 0.09 us  [the longest x1 0.08 us: local(): surface_early + surface_late]
    dynamic_update_slice x16 -> x0, other arithmetic: 63.2 us -> none  [local(): lax.scan(forward, (wave_prev[0], wave_now[0]), None, length=STEPS)]
    slice x80 -> x11, local copies, waits for them, and re-layouts: 55 us -> 2.81 us  [the longest x2 2.58 us: exchange(): fields[:, :, cols - K:]]
    while x160 -> x0, local copies, waits for them, and re-layouts: 51.6 us -> none
    psum x1 -> x0, waiting for transfers between devices: 46.1 us -> none  [local(): total = lax.psum(gradient, 'shot')]
    dot_general x19 -> x2, matrix products: 16.6 us -> 1.8 us  [the longest x1 1 us: receivers(): jnp.dot(picker, arrived[:, :STEPS], precision=highest, preferred_element_...]
  transfers between devices with their start and end apart: 131 -> 22, of which waited for: 51 -> 15; matrix products, arithmetic and copies ran while one was open for 7% -> 6% of each run, Pallas kernels for 0% -> 17%
where the time goes in v1:
time: 268 us; the launch traced here: 267 us
  waiting for transfers between devices  97 us (36%)
  Pallas kernels  95.5 us (36%)
  starting transfers between devices  44.8 us (17%)
  other arithmetic  18.6 us (7%)
  local copies, waits for them, and re-layouts  8.41 us (3%)
    pallas_call x4, Pallas kernels, run_block(): pl.pallas_call(functools.partial(block_kernel, coef.shape, adjoint is not...  95.5 us
    ppermute x10, waiting for transfers between devices, swap(): second = lax.ppermute(jnp.where(even, low, high), axis, pairs(count, True))  42.9 us
    ppermute x10, starting transfers between devices, swap(): second = lax.ppermute(jnp.where(even, low, high), axis, pairs(count, True))  31 us
    ppermute x10, waiting for transfers between devices, swap(): first = lax.ppermute(jnp.where(even, high, low), axis, pairs(count, False))  29.5 us
    ppermute x1, waiting for transfers between devices, local(): other = lax.ppermute(gradient, 'shot', pairs(lax.axis_size('shot'), False))  24.7 us
    all_to_all x1, starting transfers between devices, receivers(): lax.all_to_all(outgoing.reshape(tile_count, per_tile, STEPS + 1), ('gx',...  7.62 us
    select_n x10, other arithmetic, swap(): second = lax.ppermute(jnp.where(even, low, high), axis, pairs(count, True))  7.4 us
  transfers between devices with their start and end apart: 22, of which 15 were waited for; matrix products, arithmetic and copies ran while one was open for 6% of the time, Pallas kernels for 17%

profile of v1, /device:TPU:10, one launch (start us, length us, event | category | flops | bytes accessed | tf_op | source)
XLA Modules:
  0.0 267.4 jit_solution(10234483881922637426)
XLA Ops:
  0.6 2.2 pad_maximum_fusion
  4.5 1.9 collective-permute-start.4
  6.4 4.3 %collective-permute-start.5 = (f32[3,8,32,256]{3,2,1,0:T(8,128)S(1)}, f32[3,8,32,256]{3,2,1,0:T(8,128)S(1)}, u32[]{:S(2)}, u32[]{:S(2)}) collective-permute-start(f32[3,8,32,256]{3,2,1,0:T(8,128)S(1)} %get-tuple-element.30), channel_id=1, source_target_pairs={{8,16},{16,8},{24,32},{32,24},{40,48},{48,40},{9,17},{17,9},{25,33... | collective-permute-start | bytes 2359304 | tf_op jit(solution)/shard_map/ppermute | solution.py:31
  12.2 11.7 %collective-permute-done.4.refs_3_.refs_7_ = f32[3,8,32,256]{3,2,1,0:T(8,128)S(1)} collective-permute-done((f32[3,8,32,256]{3,2,1,0:T(8,128)S(1)}, f32[3,8,32,256]{3,2,1,0:T(8,128)S(1)}, u32[]{:S(2)}, u32[]{:S(2)}) %collective-permute-start.4) | collective-permute-done | bytes 786464 | tf_op jit(solution)/shard_map/ppermute | solution.py:30
  24.0 5.5 %collective-permute-done.5.refs_4_.refs_8_ = f32[3,8,32,256]{3,2,1,0:T(8,128)S(1)} collective-permute-done((f32[3,8,32,256]{3,2,1,0:T(8,128)S(1)}, f32[3,8,32,256]{3,2,1,0:T(8,128)S(1)}, u32[]{:S(2)}, u32[]{:S(2)}) %collective-permute-start.5) | collective-permute-done | bytes 786464 | tf_op jit(solution)/shard_map/ppermute | solution.py:31
  31.2 2.5 collective-permute-start.7
  35.0 7.6 %all-to-all-start = ((f32[64,2,17]{2,1,0:T(2,128)}), f32[64,2,17]{2,1,0:T(2,128)S(1)}, u32[]{:S(2)}, u32[]{:S(2)}) async-start(f32[64,2,17]{2,1,0:T(2,128)} %bitcast.12), calls=%async_computation | async-start | bytes 131072 | tf_op jit(solution)/shard_map/all_to_all | solution.py:250
  44.3 5.1 %collective-permute-done.7.refs_6_.refs_10_ = f32[3,48,8,256]{3,2,1,0:T(8,128)} collective-permute-done((f32[3,48,8,256]{3,2,1,0:T(8,128)}, f32[3,48,8,256]{3,2,1,0:T(8,128)}, u32[]{:S(2)}, u32[]{:S(2)}) %collective-permute-start.7) | collective-permute-done | bytes 1179680 | tf_op jit(solution)/shard_map/ppermute | solution.py:31
  49.4 22.2 %shard_map.104 = (f32[32,32,256]{2,1,0:T(8,128)S(1)}, f32[32,32,256]{2,1,0:T(8,128)S(1)}, f32[8,32,32,256]{3,2,1,0:T(8,128)}, f32[32,32,128]{2,1,0:T(8,128)S(1)}) custom-call(s32[2]{0:T(128)S(1)} %pad_add_fusion.parity, f32[32,32,256]{2,1,0:T(8,128)S(1)} %bitcast.36, f32[32,32,256]{2,1,0:T(8,128)} %bitcast.46, f32[32,32,256]{2,1,0:T(8,128)} %refs_2_.7, ...), custom_call_target="tpu_custom_call" | custom-call | tf_op jit(solution)/shard_map/pallas_call | solution.py:212
  73.1 4.3 %collective-permute-start.9 = (f32[2,8,32,256]{3,2,1,0:T(8,128)}, f32[2,8,32,256]{3,2,1,0:T(8,128)}, u32[]{:S(2)}, u32[]{:S(2)}) collective-permute-start(f32[2,8,32,256]{3,2,1,0:T(8,128)} %get-tuple-element.36), channel_id=1, source_target_pairs={{8,16},{16,8},{24,32},{32,24},{40,48},{48,40},{9,17},{17,9},{25,33... | collective-permute-start | bytes 1572872 | tf_op jit(solution)/shard_map/ppermute | solution.py:31
  78.5 3.9 %collective-permute-start.1 = (f32[2,8,32,256]{3,2,1,0:T(8,128)}, f32[2,8,32,256]{3,2,1,0:T(8,128)}, u32[]{:S(2)}, u32[]{:S(2)}) collective-permute-start(f32[2,8,32,256]{3,2,1,0:T(8,128)} %get-tuple-element.40), channel_id=1, source_target_pairs={{8,16},{16,8},{24,32},{32,24},{40,48},{48,40},{9,17},{17,9},{25,33... | collective-permute-start | bytes 1572872 | tf_op jit(solution)/shard_map/ppermute | solution.py:31
  84.8 3.5 %collective-permute-done.8.refs_3_ = f32[2,8,32,256]{3,2,1,0:T(8,128)} collective-permute-done((f32[2,8,32,256]{3,2,1,0:T(8,128)}, f32[2,8,32,256]{3,2,1,0:T(8,128)}, u32[]{:S(2)}, u32[]{:S(2)}) %collective-permute-start.8) | collective-permute-done | bytes 524320 | tf_op jit(solution)/shard_map/ppermute | solution.py:30
  88.2 4.0 %collective-permute-done.9.refs_4_ = f32[2,8,32,256]{3,2,1,0:T(8,128)} collective-permute-done((f32[2,8,32,256]{3,2,1,0:T(8,128)}, f32[2,8,32,256]{3,2,1,0:T(8,128)}, u32[]{:S(2)}, u32[]{:S(2)}) %collective-permute-start.9) | collective-permute-done | bytes 524320 | tf_op jit(solution)/shard_map/ppermute | solution.py:31
  93.9 2.0 collective-permute-start.11
  96.0 3.1 %collective-permute-done.refs_3_ = f32[2,8,32,256]{3,2,1,0:T(8,128)S(1)} collective-permute-done((f32[2,8,32,256]{3,2,1,0:T(8,128)}, f32[2,8,32,256]{3,2,1,0:T(8,128)S(1)}, u32[]{:S(2)}, u32[]{:S(2)}) %collective-permute-start) | collective-permute-done | bytes 524320 | tf_op jit(solution)/shard_map/ppermute | solution.py:30
  99.1 4.1 %collective-permute-done.1.refs_4_ = f32[2,8,32,256]{3,2,1,0:T(8,128)} collective-permute-done((f32[2,8,32,256]{3,2,1,0:T(8,128)}, f32[2,8,32,256]{3,2,1,0:T(8,128)}, u32[]{:S(2)}, u32[]{:S(2)}) %collective-permute-start.1) | collective-permute-done | bytes 524320 | tf_op jit(solution)/shard_map/ppermute | solution.py:31
  105.8 2.0 collective-permute-start.3
  107.8 23.4 %shard_map.105 = (f32[32,32,256]{2,1,0:T(8,128)}, f32[32,32,256]{2,1,0:T(8,128)}, f32[8,32,32,256]{3,2,1,0:T(8,128)}, f32[32,32,128]{2,1,0:T(8,128)S(1)}) custom-call(s32[2]{0:T(128)S(1)} %pad_add_fusion.parity, f32[32,32,256]{2,1,0:T(8,128)} %copy-done, f32[32,32,256]{2,1,0:T(8,128)} %copy-done.1, f32[32,32,256]{2,1,0:T(8,128)} %refs_2_.7, ...), custom_call_target="tpu_custom_call" | custom-call | tf_op jit(solution)/shard_map/pallas_call | solution.py:212
  133.6 4.3 %collective-permute-start.12 = (f32[1,8,32,16]{3,2,1,0:T(8,128)S(1)}, f32[1,8,32,16]{3,2,1,0:T(8,128)S(1)}, u32[]{:S(2)}, u32[]{:S(2)}) collective-permute-start(f32[1,8,32,16]{3,2,1,0:T(8,128)S(1)} %get-tuple-element.62), channel_id=1, source_target_pairs={{8,16},{16,8},{24,32},{32,24},{40,48},{48,40},{9,17},{17,9},{25,33... | collective-permute-start | bytes 49160 | tf_op jit(solution)/shard_map/ppermute | solution.py:31
  138.0 5.4 %collective-permute-done.12 = f32[1,8,32,16]{3,2,1,0:T(8,128)S(1)} collective-permute-done((f32[1,8,32,16]{3,2,1,0:T(8,128)S(1)}, f32[1,8,32,16]{3,2,1,0:T(8,128)S(1)}, u32[]{:S(2)}, u32[]{:S(2)}) %collective-permute-start.12) | collective-permute-done | bytes 16416 | tf_op jit(solution)/shard_map/ppermute | solution.py:31
  144.1 1.9 collective-permute-start.14
  147.3 3.8 %collective-permute-done.14 = f32[1,48,8,16]{3,2,1,0:T(8,128)S(1)} collective-permute-done((f32[1,48,8,16]{3,2,1,0:T(8,128)S(1)}, f32[1,48,8,16]{3,2,1,0:T(8,128)S(1)}, u32[]{:S(2)}, u32[]{:S(2)}) %collective-permute-start.14) | collective-permute-done | bytes 24608 | tf_op jit(solution)/shard_map/ppermute | solution.py:31
  153.5 25.1 %shard_map.106 = (f32[32,32,256]{2,1,0:T(8,128)S(1)}, f32[32,32,256]{2,1,0:T(8,128)}, f32[32,32,256]{2,1,0:T(8,128)}) custom-call(s32[2]{0:T(128)S(1)} %pad_add_fusion.parity, f32[32,32,256]{2,1,0:T(8,128)} %bitcast.44, f32[32,32,256]{2,1,0:T(8,128)} %bitcast.45, f32[32,32,256]{2,1,0:T(8,128)} %refs_2_.7, ...), custom_call_target="tpu_custom_call" | custom-call | tf_op jit(solution)/shard_map/pallas_call | solution.py:212
  180.4 3.7 %collective-permute-start.17 = (f32[2,8,32,256]{3,2,1,0:T(8,128)S(1)}, f32[2,8,32,256]{3,2,1,0:T(8,128)S(1)}, u32[]{:S(2)}, u32[]{:S(2)}) collective-permute-start(f32[2,8,32,256]{3,2,1,0:T(8,128)S(1)} %get-tuple-element.34), channel_id=1, source_target_pairs={{8,16},{16,8},{24,32},{32,24},{40,48},{48,40},{9,17},{17,9},{25,33... | collective-permute-start | bytes 1572872 | tf_op jit(solution)/shard_map/ppermute | solution.py:31
  184.2 10.2 %collective-permute-done.16.refs_3_ = f32[2,8,32,256]{3,2,1,0:T(8,128)S(1)} collective-permute-done((f32[2,8,32,256]{3,2,1,0:T(8,128)S(1)}, f32[2,8,32,256]{3,2,1,0:T(8,128)S(1)}, u32[]{:S(2)}, u32[]{:S(2)}) %collective-permute-start.16) | collective-permute-done | bytes 524320 | tf_op jit(solution)/shard_map/ppermute | solution.py:30
  194.4 4.0 %collective-permute-done.17.refs_4_ = f32[2,8,32,256]{3,2,1,0:T(8,128)S(1)} collective-permute-done((f32[2,8,32,256]{3,2,1,0:T(8,128)S(1)}, f32[2,8,32,256]{3,2,1,0:T(8,128)S(1)}, u32[]{:S(2)}, u32[]{:S(2)}) %collective-permute-start.17) | collective-permute-done | bytes 524320 | tf_op jit(solution)/shard_map/ppermute | solution.py:31
  198.9 1.9 collective-permute-start.19
  201.1 11.0 %collective-permute-done.19.refs_6_ = f32[2,48,8,256]{3,2,1,0:T(8,128)S(1)} collective-permute-done((f32[2,48,8,256]{3,2,1,0:T(8,128)S(1)}, f32[2,48,8,256]{3,2,1,0:T(8,128)S(1)}, u32[]{:S(2)}, u32[]{:S(2)}) %collective-permute-start.19) | collective-permute-done | bytes 786464 | tf_op jit(solution)/shard_map/ppermute | solution.py:31
  212.2 24.8 %shard_map.107 = (f32[32,32,256]{2,1,0:T(8,128)}, f32[32,32,256]{2,1,0:T(8,128)}, f32[32,32,256]{2,1,0:T(8,128)}) custom-call(s32[2]{0:T(128)S(1)} %pad_add_fusion.parity, f32[32,32,256]{2,1,0:T(8,128)} %copy-done.3, f32[32,32,256]{2,1,0:T(8,128)} %get-tuple-element.18.refs_1_, f32[32,32,256]{2,1,0:T(8,128)} %refs_2_.7, ...), custom_call_target="tpu_custom_call" | custom-call | tf_op jit(solution)/shard_map/pallas_call | solution.py:212
  236.9 2.7 collective-permute-start.20
  239.6 24.7 %collective-permute-done.20 = f32[32,32,256]{2,1,0:T(8,128)S(1)} collective-permute-done((f32[32,32,256]{2,1,0:T(8,128)}, f32[32,32,256]{2,1,0:T(8,128)S(1)}, u32[]{:S(2)}, u32[]{:S(2)}) %collective-permute-start.20) | collective-permute-done | bytes 1048608 | tf_op jit(solution)/shard_map/ppermute | solution.py:316
  264.3 3.1 %multiply_add_fusion = (f32[32,32,256]{2,1,0:T(8,128)}, f32[32,32,256]{2,1,0:T(8,128)}) fusion(f32[32,32,256]{2,1,0:T(8,128)S(1)} %copy-done.14, f32[32,32,256]{2,1,0:T(8,128)S(1)} %copy-done.7, f32[32,32,256]{2,1,0:T(8,128)} %get-tuple-element.21, f32[32,32,256]{2,1,0:T(8,128)S(1)} %collective-permute-done.20), kind=kLoop, calls=%fused_computation.24 | loop fusion | flops 2359296 | bytes 6291456 | tf_op jit(solution)/shard_map/add | solution.py:319
  (100 shorter events, 26.1 us)
Async XLA Ops:
  4.5 19.5 %collective-permute-start.4 = (f32[3,8,32,256]{3,2,1,0:T(8,128)S(1)}, f32[3,8,32,256]{3,2,1,0:T(8,128)S(1)}, u32[]{:S(2)}, u32[]{:S(2)}) collective-permute-start(f32[3,8,32,256]{3,2,1,0:T(8,128)S(1)} %get-tuple-element.31), channel_id=1, source_target_pairs={{0,8},{8,0},{16,24},{24,16},{32,40},{40,32},{48,56},{56,48},{1,9},... | collective-permute-start | bytes 2359304 | tf_op jit(solution)/shard_map/ppermute | solution.py:30
  6.4 23.0 %collective-permute-start.5 = (f32[3,8,32,256]{3,2,1,0:T(8,128)S(1)}, f32[3,8,32,256]{3,2,1,0:T(8,128)S(1)}, u32[]{:S(2)}, u32[]{:S(2)}) collective-permute-start(f32[3,8,32,256]{3,2,1,0:T(8,128)S(1)} %get-tuple-element.30), channel_id=1, source_target_pairs={{8,16},{16,8},{24,32},{32,24},{40,48},{48,40},{9,17},{17,9},{25,33... | collective-permute-start | bytes 2359304 | tf_op jit(solution)/shard_map/ppermute | solution.py:31
  31.2 13.0 %collective-permute-start.6 = (f32[3,48,8,256]{3,2,1,0:T(8,128)}, f32[3,48,8,256]{3,2,1,0:T(8,128)S(1)}, u32[]{:S(2)}, u32[]{:S(2)}) collective-permute-start(f32[3,48,8,256]{3,2,1,0:T(8,128)} %get-tuple-element.33), channel_id=1, source_target_pairs={{0,1},{1,0},{2,3},{3,2},{4,5},{5,4},{6,7},{7,6},{8,9},{9,8},{10,11... | collective-permute-start | bytes 3538952 | tf_op jit(solution)/shard_map/ppermute | solution.py:30
  31.2 18.2 %collective-permute-start.7 = (f32[3,48,8,256]{3,2,1,0:T(8,128)}, f32[3,48,8,256]{3,2,1,0:T(8,128)}, u32[]{:S(2)}, u32[]{:S(2)}) collective-permute-start(f32[3,48,8,256]{3,2,1,0:T(8,128)} %get-tuple-element.32), channel_id=1, source_target_pairs={{1,2},{2,1},{3,4},{4,3},{5,6},{6,5},{9,10},{10,9},{11,12},{12,11},... | collective-permute-start | bytes 3538952 | tf_op jit(solution)/shard_map/ppermute | solution.py:31
  35.0 48.6 %all-to-all-start = ((f32[64,2,17]{2,1,0:T(2,128)}), f32[64,2,17]{2,1,0:T(2,128)S(1)}, u32[]{:S(2)}, u32[]{:S(2)}) async-start(f32[64,2,17]{2,1,0:T(2,128)} %bitcast.12), calls=%async_computation | async-start | bytes 131072 | tf_op jit(solution)/shard_map/all_to_all | solution.py:250
  44.1 5.3 %copy-start.4 = (f32[1,32,32,256]{3,2,1,0:T(8,128)S(1)}, f32[1,32,32,256]{3,2,1,0:T(8,128)}, u32[]{:S(2)}) copy-start(f32[1,32,32,256]{3,2,1,0:T(8,128)} %param.10) | copy-start | bytes 3145732
  71.6 22.0 %copy-start = (f32[32,32,256]{2,1,0:T(8,128)}, f32[32,32,256]{2,1,0:T(8,128)S(1)}, u32[]{:S(2)}) copy-start(f32[32,32,256]{2,1,0:T(8,128)S(1)} %get-tuple-element.12.refs_0_) | copy-start | bytes 3145732
  73.1 15.1 %collective-permute-start.8 = (f32[2,8,32,256]{3,2,1,0:T(8,128)}, f32[2,8,32,256]{3,2,1,0:T(8,128)}, u32[]{:S(2)}, u32[]{:S(2)}) collective-permute-start(f32[2,8,32,256]{3,2,1,0:T(8,128)} %get-tuple-element.37), channel_id=1, source_target_pairs={{0,8},{8,0},{16,24},{24,16},{32,40},{40,32},{48,56},{56,48},{1,9},... | collective-permute-start | bytes 1572872 | tf_op jit(solution)/shard_map/ppermute | solution.py:30
  73.1 19.1 %collective-permute-start.9 = (f32[2,8,32,256]{3,2,1,0:T(8,128)}, f32[2,8,32,256]{3,2,1,0:T(8,128)}, u32[]{:S(2)}, u32[]{:S(2)}) collective-permute-start(f32[2,8,32,256]{3,2,1,0:T(8,128)} %get-tuple-element.36), channel_id=1, source_target_pairs={{8,16},{16,8},{24,32},{32,24},{40,48},{48,40},{9,17},{17,9},{25,33... | collective-permute-start | bytes 1572872 | tf_op jit(solution)/shard_map/ppermute | solution.py:31
  78.5 20.6 %collective-permute-start = (f32[2,8,32,256]{3,2,1,0:T(8,128)}, f32[2,8,32,256]{3,2,1,0:T(8,128)S(1)}, u32[]{:S(2)}, u32[]{:S(2)}) collective-permute-start(f32[2,8,32,256]{3,2,1,0:T(8,128)} %get-tuple-element.41), channel_id=1, source_target_pairs={{0,8},{8,0},{16,24},{24,16},{32,40},{40,32},{48,56},{56,48},{1,9},... | collective-permute-start | bytes 1572872 | tf_op jit(solution)/shard_map/ppermute | solution.py:30
  78.5 24.7 %collective-permute-start.1 = (f32[2,8,32,256]{3,2,1,0:T(8,128)}, f32[2,8,32,256]{3,2,1,0:T(8,128)}, u32[]{:S(2)}, u32[]{:S(2)}) collective-permute-start(f32[2,8,32,256]{3,2,1,0:T(8,128)} %get-tuple-element.40), channel_id=1, source_target_pairs={{8,16},{16,8},{24,32},{32,24},{40,48},{48,40},{9,17},{17,9},{25,33... | collective-permute-start | bytes 1572872 | tf_op jit(solution)/shard_map/ppermute | solution.py:31
  84.8 8.8 %copy-start.2 = (f32[32,32,256]{2,1,0:T(8,128)S(1)}, f32[32,32,256]{2,1,0:T(8,128)}, u32[]{:S(2)}) copy-start(f32[32,32,256]{2,1,0:T(8,128)} %copy-done.1) | copy-start | bytes 3145732
  93.8 14.0 %collective-permute-start.10 = (f32[2,48,8,256]{3,2,1,0:T(8,128)S(1)}, f32[2,48,8,256]{3,2,1,0:T(8,128)S(1)}, u32[]{:S(2)}, u32[]{:S(2)}) collective-permute-start(f32[2,48,8,256]{3,2,1,0:T(8,128)S(1)} %get-tuple-element.27), channel_id=1, source_target_pairs={{0,1},{1,0},{2,3},{3,2},{4,5},{5,4},{6,7},{7,6},{8,9},{9,8},{10,11... | collective-permute-start | bytes 2359304 | tf_op jit(solution)/shard_map/ppermute | solution.py:30
  93.9 14.0 %collective-permute-start.11 = (f32[2,48,8,256]{3,2,1,0:T(8,128)S(1)}, f32[2,48,8,256]{3,2,1,0:T(8,128)S(1)}, u32[]{:S(2)}, u32[]{:S(2)}) collective-permute-start(f32[2,48,8,256]{3,2,1,0:T(8,128)S(1)} %get-tuple-element.26), channel_id=1, source_target_pairs={{1,2},{2,1},{3,4},{4,3},{5,6},{6,5},{9,10},{10,9},{11,12},{12,11},... | collective-permute-start | bytes 2359304 | tf_op jit(solution)/shard_map/ppermute | solution.py:31
  96.0 8.5 %copy-start.12 = (f32[2,32,8,256]{3,2,1,0:T(8,128)S(1)}, f32[2,32,8,256]{3,2,1,0:T(8,128)}, u32[]{:S(2)}) copy-start(f32[2,32,8,256]{3,2,1,0:T(8,128)} %get-tuple-element.38) | copy-start | bytes 1572868
  96.0 8.5 %copy-start.13 = (f32[2,32,8,256]{3,2,1,0:T(8,128)S(1)}, f32[2,32,8,256]{3,2,1,0:T(8,128)}, u32[]{:S(2)}) copy-start(f32[2,32,8,256]{3,2,1,0:T(8,128)} %get-tuple-element.39) | copy-start | bytes 1572868
  105.7 46.6 %collective-permute-start.2 = (f32[2,48,8,256]{3,2,1,0:T(8,128)}, f32[2,48,8,256]{3,2,1,0:T(8,128)S(1)}, u32[]{:S(2)}, u32[]{:S(2)}) collective-permute-start(f32[2,48,8,256]{3,2,1,0:T(8,128)} %get-tuple-element.45), channel_id=1, source_target_pairs={{0,1},{1,0},{2,3},{3,2},{4,5},{5,4},{6,7},{7,6},{8,9},{9,8},{10,11... | collective-permute-start | bytes 2359304 | tf_op jit(solution)/shard_map/ppermute | solution.py:30
  105.7 25.5 %copy-start.6 = (f32[32,32,128]{2,1,0:T(8,128)S(1)}, f32[32,32,128]{2,1,0:T(8,128)}, u32[]{:S(2)}) copy-start(f32[32,32,128]{2,1,0:T(8,128)} %copy-done.5) | copy-start | bytes 1572868
  105.8 46.6 %collective-permute-start.3 = (f32[2,48,8,256]{3,2,1,0:T(8,128)}, f32[2,48,8,256]{3,2,1,0:T(8,128)}, u32[]{:S(2)}, u32[]{:S(2)}) collective-permute-start(f32[2,48,8,256]{3,2,1,0:T(8,128)} %get-tuple-element.44), channel_id=1, source_target_pairs={{1,2},{2,1},{3,4},{4,3},{5,6},{6,5},{9,10},{10,9},{11,12},{12,11},... | collective-permute-start | bytes 2359304 | tf_op jit(solution)/shard_map/ppermute | solution.py:31
  133.6 9.8 %collective-permute-start.12 = (f32[1,8,32,16]{3,2,1,0:T(8,128)S(1)}, f32[1,8,32,16]{3,2,1,0:T(8,128)S(1)}, u32[]{:S(2)}, u32[]{:S(2)}) collective-permute-start(f32[1,8,32,16]{3,2,1,0:T(8,128)S(1)} %get-tuple-element.62), channel_id=1, source_target_pairs={{8,16},{16,8},{24,32},{32,24},{40,48},{48,40},{9,17},{17,9},{25,33... | collective-permute-start | bytes 49160 | tf_op jit(solution)/shard_map/ppermute | solution.py:31
  137.9 6.1 %collective-permute-start.13 = (f32[1,8,32,16]{3,2,1,0:T(8,128)S(1)}, f32[1,8,32,16]{3,2,1,0:T(8,128)S(1)}, u32[]{:S(2)}, u32[]{:S(2)}) collective-permute-start(f32[1,8,32,16]{3,2,1,0:T(8,128)S(1)} %get-tuple-element.63), channel_id=1, source_target_pairs={{0,8},{8,0},{16,24},{24,16},{32,40},{40,32},{48,56},{56,48},{1,9},... | collective-permute-start | bytes 49160 | tf_op jit(solution)/shard_map/ppermute | solution.py:30
  144.1 7.0 %collective-permute-start.14 = (f32[1,48,8,16]{3,2,1,0:T(8,128)S(1)}, f32[1,48,8,16]{3,2,1,0:T(8,128)S(1)}, u32[]{:S(2)}, u32[]{:S(2)}) collective-permute-start(f32[1,48,8,16]{3,2,1,0:T(8,128)S(1)} %get-tuple-element.74), channel_id=1, source_target_pairs={{1,2},{2,1},{3,4},{4,3},{5,6},{6,5},{9,10},{10,9},{11,12},{12,11},... | collective-permute-start | bytes 73736 | tf_op jit(solution)/shard_map/ppermute | solution.py:31
  146.0 5.1 %collective-permute-start.15 = (f32[1,48,8,16]{3,2,1,0:T(8,128)S(1)}, f32[1,48,8,16]{3,2,1,0:T(8,128)S(1)}, u32[]{:S(2)}, u32[]{:S(2)}) collective-permute-start(f32[1,48,8,16]{3,2,1,0:T(8,128)S(1)} %get-tuple-element.75), channel_id=1, source_target_pairs={{0,1},{1,0},{2,3},{3,2},{4,5},{5,4},{6,7},{7,6},{8,9},{9,8},{10,11... | collective-permute-start | bytes 73736 | tf_op jit(solution)/shard_map/ppermute | solution.py:30
  178.6 20.0 %copy-start.3 = (f32[32,32,256]{2,1,0:T(8,128)}, f32[32,32,256]{2,1,0:T(8,128)S(1)}, u32[]{:S(2)}) copy-start(f32[32,32,256]{2,1,0:T(8,128)S(1)} %get-tuple-element.17.refs_0_) | copy-start | bytes 3145732
  178.6 5.6 %copy-start.9 = (f32[32,32,256]{2,1,0:T(8,128)S(1)}, f32[32,32,256]{2,1,0:T(8,128)}, u32[]{:S(2)}) copy-start(f32[32,32,256]{2,1,0:T(8,128)} %get-tuple-element.18.refs_1_) | copy-start | bytes 3145732
  180.4 14.1 %collective-permute-start.16 = (f32[2,8,32,256]{3,2,1,0:T(8,128)S(1)}, f32[2,8,32,256]{3,2,1,0:T(8,128)S(1)}, u32[]{:S(2)}, u32[]{:S(2)}) collective-permute-start(f32[2,8,32,256]{3,2,1,0:T(8,128)S(1)} %get-tuple-element.35), channel_id=1, source_target_pairs={{0,8},{8,0},{16,24},{24,16},{32,40},{40,32},{48,56},{56,48},{1,9},... | collective-permute-start | bytes 1572872 | tf_op jit(solution)/shard_map/ppermute | solution.py:30
  180.4 18.0 %collective-permute-start.17 = (f32[2,8,32,256]{3,2,1,0:T(8,128)S(1)}, f32[2,8,32,256]{3,2,1,0:T(8,128)S(1)}, u32[]{:S(2)}, u32[]{:S(2)}) collective-permute-start(f32[2,8,32,256]{3,2,1,0:T(8,128)S(1)} %get-tuple-element.34), channel_id=1, source_target_pairs={{8,16},{16,8},{24,32},{32,24},{40,48},{48,40},{9,17},{17,9},{25,33... | collective-permute-start | bytes 1572872 | tf_op jit(solution)/shard_map/ppermute | solution.py:31
  198.8 2.4 collective-permute-start.18
  198.9 13.3 %collective-permute-start.19 = (f32[2,48,8,256]{3,2,1,0:T(8,128)S(1)}, f32[2,48,8,256]{3,2,1,0:T(8,128)S(1)}, u32[]{:S(2)}, u32[]{:S(2)}) collective-permute-start(f32[2,48,8,256]{3,2,1,0:T(8,128)S(1)} %get-tuple-element.24), channel_id=1, source_target_pairs={{1,2},{2,1},{3,4},{4,3},{5,6},{6,5},{9,10},{10,9},{11,12},{12,11},... | collective-permute-start | bytes 2359304 | tf_op jit(solution)/shard_map/ppermute | solution.py:31
  212.2 52.1 %copy-start.7 = (f32[32,32,256]{2,1,0:T(8,128)S(1)}, f32[32,32,256]{2,1,0:T(8,128)}, u32[]{:S(2)}) copy-start(f32[32,32,256]{2,1,0:T(8,128)} %refs_2_.7) | copy-start | bytes 3145732
  212.2 52.1 %copy-start.14 = (f32[32,32,256]{2,1,0:T(8,128)S(1)}, f32[32,32,256]{2,1,0:T(8,128)}, u32[]{:S(2)}) copy-start(f32[32,32,256]{2,1,0:T(8,128)} %param.14) | copy-start | bytes 3145732
  236.9 27.3 %collective-permute-start.20 = (f32[32,32,256]{2,1,0:T(8,128)}, f32[32,32,256]{2,1,0:T(8,128)S(1)}, u32[]{:S(2)}, u32[]{:S(2)}) collective-permute-start(f32[32,32,256]{2,1,0:T(8,128)} %get-tuple-element.21), channel_id=1, source_target_pairs={{0,64},{64,0},{1,65},{65,1},{2,66},{66,2},{3,67},{67,3},{4,68},{68... | collective-permute-start | bytes 3145736 | tf_op jit(solution)/shard_map/ppermute | solution.py:316
  (8 other events, 24.3 us)

commit v2 on v1

v2 whole, which is shorter than its diff:
```python
import functools
import math

import jax
import jax.numpy as jnp
from jax import lax
from jax.experimental import pallas as pl
from jax.experimental.pallas import tpu as pltpu
from jax.sharding import PartitionSpec as P

STEPS = 16
DEPTH = 2
K = 8
UNROLL = 8
THIN = 32
MARK = 64
THIN_UNROLL = 4
VMEM_LIMIT = 48 * 1024 * 1024
STRIP_VMEM_LIMIT = 16 * 1024 * 1024

step_eta = 0.01
prior_prec = 4.0
prior_centre = 0.2


def pairs(count, odd):
    found = []
    for low in range(1 if odd else 0, count - 1, 2):
        found += [(low, low + 1), (low + 1, low)]
    return found


def swap(axis, first, second):
    count = lax.axis_size(axis)
    return (
        lax.ppermute(first, axis, pairs(count, False)),
        lax.ppermute(second, axis, pairs(count, True)),
    )


def strip_kernel(axis, width, count, parity, *refs):
    fields, refs = refs[:count], refs[count:]
    received, refs = refs[: 2 * axis], refs[2 * axis :]
    sends, sems = refs[:2], refs[2]
    rows, cols = fields[0].shape[:2]
    far = (rows, cols)[axis] - width
    even = parity[axis] == 0
    copies = []

    def copy(source, target):
        copies.append(pltpu.make_async_copy(source, target, sems.at[len(copies)]))

    for send, start in zip(sends, (jnp.where(even, far, 0), jnp.where(even, 0, far))):
        if axis == 1:
            part = pl.ds(pl.multiple_of(start, 8), width)
            above, below = rows + width, 0
            places = [jnp.where(parity[0] == 0, *pair) for pair in ((above, below), (below, above))]
        for index, field in enumerate(fields):
            if axis == 0:
                copy(field.at[pl.ds(start, width)], send.at[index])
            else:
                copy(field.at[:, part], send.at[index, pl.ds(width, rows)])
                for strip, place in zip(received, places):
                    copy(strip.at[index, :, part], send.at[index, pl.ds(place, width)])
    run_copies(copies)


def strips(parity, fields, axis, width, received=()):
    rows, cols, depth = fields[0].shape
    count = len(fields)
    shape = (count, width, cols, depth) if axis == 0 else (count, rows + 2 * width, width, depth)
    send = jax.ShapeDtypeStruct(shape, jnp.float32)
    anywhere = pl.BlockSpec(memory_space=pl.ANY)
    return pl.pallas_call(
        functools.partial(strip_kernel, axis, width, count),
        in_specs=[pl.BlockSpec(memory_space=pltpu.SMEM)] + [anywhere] * (count + len(received)),
        out_specs=[anywhere, anywhere],
        out_shape=[send, send],
        scratch_shapes=[pltpu.SemaphoreType.DMA(((2 + 4 * axis) * count,))],
        compiler_params=pltpu.CompilerParams(vmem_limit_bytes=STRIP_VMEM_LIMIT),
    )(parity, *fields, *received)


def halo_places(parity, shape, width, pad):
    rows, cols = shape[:2]
    x_first = jnp.where(parity[0] == 0, rows + width, 0) + pad
    x_second = jnp.where(parity[0] == 0, 0, rows + width) + pad
    y_first = pl.multiple_of(jnp.where(parity[1] == 0, cols + width, 0), 8)
    y_second = pl.multiple_of(jnp.where(parity[1] == 0, 0, cols + width), 8)
    inner, every = pl.ds(width, cols), pl.ds(pad, rows + 2 * width)
    return (
        (pl.ds(width + pad, rows), inner),
        (pl.ds(x_first, width), inner),
        (pl.ds(x_second, width), inner),
        (every, pl.ds(y_first, width)),
        (every, pl.ds(y_second, width)),
    )


def run_copies(copies, between=None):
    for copy in copies:
        copy.start()
    if between is not None:
        between()
    for copy in copies:
        copy.wait()


def block_kernel(shape, adjoint, gather, parity, *refs):
    rows, cols, depth = shape
    own_refs, refs = refs[:3], refs[3:]
    halo_refs, refs = refs[:8], refs[8:]
    if gather:
        factor, grad_in, refs = refs[0], refs[1], refs[2:]
    if gather and not adjoint:
        surface_in, refs = refs[0], refs[1:]
    if gather:
        grad, refs = refs[0], refs[1:]
    else:
        newest, older, send_first, send_second, kept = refs[:5]
        refs = refs[5:]
    if gather and not adjoint:
        kept, refs = refs[0], refs[1:]
    if not adjoint:
        surface, refs = refs[0], refs[1:]
    first, second, coef, sems, out_sems = refs
    turn_of = pl.program_id(0)
    groups = cols // 8 + 2
    halves = depth // 128
    edge = K + 1
    lane = lax.broadcasted_iota(jnp.int32, (8, 128), 1)
    line = lax.broadcasted_iota(jnp.int32, (8, 128), 0)
    last_lane, first_lane = lane == 127, lane == 0
    last_line, first_line = line == 7, line == 0
    zero = jnp.zeros((8, 128), jnp.float32)

    @pl.when(turn_of == 0)
    def _():
        places = halo_places(parity, shape, K, 1)
        copies = []
        for index, (own, target) in enumerate(zip(own_refs, (first, second, coef))):
            halos = halo_refs[4:] if index == 2 else halo_refs[:4]
            sources = [own] + [halo.at[index] for halo in halos]
            for source, place in zip(sources, places):
                copies.append(
                    pltpu.make_async_copy(source, target.at[place], sems.at[len(copies)])
                )

        def pads():
            for field in (first, second, coef):
                field[0] = jnp.zeros(field.shape[1:], jnp.float32)
                field[rows + 2 * K + 1] = jnp.zeros(field.shape[1:], jnp.float32)
            if gather:
                grad[...] = grad_in[...]
            if not adjoint:
                surface[...] = surface_in[...] if gather else jnp.zeros_like(surface)

        run_copies(copies, pads)
        if adjoint and not gather:

            def weigh(x, carried):
                first[x] = first[x] * coef[x]
                second[x] = second[x] * coef[x]
                return carried

            lax.fori_loop(1, rows + 2 * K + 1, weigh, 0)

    def load(source, x):
        return [
            [source[x, pl.ds(8 * g, 8), pl.ds(128 * h, 128)] for h in range(halves)]
            for g in range(groups)
        ]

    def row(x, target, half, inside, below, centre, above):
        ups = [[pltpu.roll(c, 7, 0) for c in line_of] for line_of in centre]
        downs = [[pltpu.roll(c, 1, 0) for c in line_of] for line_of in centre]
        done = []
        for g in range(groups):
            lefts = [pltpu.roll(c, 127, 1) for c in centre[g]]
            rights = [pltpu.roll(c, 1, 1) for c in centre[g]]
            for h in range(halves):
                c = centre[g][h]
                at = (x, pl.ds(8 * g, 8), pl.ds(128 * h, 128))
                up = jnp.where(last_line, ups[g + 1][h], ups[g][h]) if g + 1 < groups else ups[g][h]
                down = jnp.where(first_line, downs[g - 1][h], downs[g][h]) if g > 0 else downs[g][h]
                left = jnp.where(last_lane, lefts[h + 1] if h + 1 < halves else zero, lefts[h])
                right = jnp.where(first_lane, rights[h - 1] if h > 0 else zero, rights[h])
                lateral = (above[g][h] + below[g][h]) + (up + down)
                laplace = lateral + (left + right) - 6.0 * c
                fresh = (2.0 * c - target[at]) + coef[at] * laplace
                done.append((g, h, at, laplace, fresh))
        for g, h, at, laplace, fresh in done:
            target[at] = fresh
            if inside and 0 < g < groups - 1:
                mine = (x - edge, pl.ds(8 * g - 8, 8), pl.ds(128 * h, 128))
                term = fresh if adjoint else laplace
                if gather:
                    grad[mine] = grad[mine] + factor[(1 - half,) + mine] * term
                if not gather or (not adjoint and h == 0):
                    kept[(half,) + mine] = term
                if not adjoint and h == 0:
                    surface[mine] = jnp.where(lane == DEPTH, fresh, pltpu.roll(surface[mine], 1, 1))

    def sweep(source, target, half):
        def rows_from(begin, count, unroll, inside):
            def body(index, carried):
                below, centre = carried
                for offset in range(unroll):
                    x = begin + index * unroll + offset
                    above = load(source, x + 1)
                    row(x, target, half, inside, below, centre, above)
                    below, centre = centre, above
                return below, centre

            lax.fori_loop(0, count, body, (load(source, begin - 1), load(source, begin)))

        count = K // 2 - turn_of - half
        rows_from(edge - 2 * count, count, 2, False)
        rows_from(edge, rows // UNROLL, UNROLL, True)
        rows_from(edge + rows, count, 2, False)

    sweep(first, second, 0)
    sweep(second, first, 1)

    if not gather:

        @pl.when(turn_of == K // 2 - 1)
        def _():
            inner = pl.ds(K, cols)
            low, high = edge, edge + rows - K
            copies = []
            for index, (field, out) in enumerate(((first, newest), (second, older))):
                for source, target in (
                    (pl.ds(edge, rows), out),
                    (pl.ds(jnp.where(parity[0] == 0, high, low), K), send_first.at[index]),
                    (pl.ds(jnp.where(parity[0] == 0, low, high), K), send_second.at[index]),
                ):
                    copies.append(
                        pltpu.make_async_copy(
                            field.at[source, inner], target, out_sems.at[len(copies)]
                        )
                    )
            run_copies(copies)


def whole(shape):
    return pl.BlockSpec(shape, lambda step: (0,) * len(shape))


def run_block(parity, current, previous, coef, halos, coef_halos, adjoint, gather=None):
    rows, cols, depth = coef.shape
    extended = (rows + 2 * K + 2, cols + 2 * K, depth)
    any_spec = pl.BlockSpec(memory_space=pltpu.HBM)
    field = jax.ShapeDtypeStruct(coef.shape, jnp.float32)
    strips = jax.ShapeDtypeStruct((2, K, cols, depth), jnp.float32)
    flat = (rows, cols, 128)
    in_specs = [pl.BlockSpec(memory_space=pltpu.SMEM)] + [any_spec] * 11
    operands = [parity, current, previous, coef, *halos, *coef_halos]
    if gather is not None:
        operands += gather
        in_specs += [
            pl.BlockSpec((2,) + coef.shape, lambda step: (K // 2 - 1 - step, 0, 0, 0)),
            whole(coef.shape),
        ]
        if not adjoint:
            in_specs += [whole(flat)]
        out_shape, out_specs = [field], [whole(coef.shape)]
    else:
        out_shape = [field, field, strips, strips]
        out_specs = [any_spec] * 4
    if gather is None or not adjoint:
        kept = flat if gather is not None else coef.shape
        out_shape += [jax.ShapeDtypeStruct((K,) + kept, jnp.float32)]
        out_specs += [pl.BlockSpec((2,) + kept, lambda step: (step, 0, 0, 0))]
    if not adjoint:
        out_shape += [jax.ShapeDtypeStruct(flat, jnp.float32)]
        out_specs += [whole(flat)]
    return pl.pallas_call(
        functools.partial(block_kernel, coef.shape, adjoint, gather is not None),
        grid=(K // 2,),
        in_specs=in_specs,
        out_specs=out_specs,
        out_shape=out_shape,
        scratch_shapes=[pltpu.VMEM(extended, jnp.float32)] * 3
        + [pltpu.SemaphoreType.DMA((15,)), pltpu.SemaphoreType.DMA((6,))],
        cost_estimate=pl.CostEstimate(flops=10**8, bytes_accessed=6 * 10**7, transcendentals=0),
        compiler_params=pltpu.CompilerParams(vmem_limit_bytes=VMEM_LIMIT),
    )(*operands)


def thin_kernel(shape, parity, own, *refs):
    halo_refs, refs = refs[:4], refs[4:]
    laps_early, laps_late, packed_out, tile, first, second, coef, inject, grad, sems = refs
    rows, cols = shape[:2]
    turn_of = pl.program_id(0)
    blocks = 128 // THIN
    span = (rows + 2 * STEPS) // blocks
    groups = (cols + 2 * STEPS) // 8
    margin = STEPS // 8
    lane = lax.broadcasted_iota(jnp.int32, (8, 128), 1)
    line = lax.broadcasted_iota(jnp.int32, (8, 128), 0)
    in_block = lane % THIN
    last_lane, first_lane = in_block == THIN - 1, in_block == 0
    last_line, first_line = line == 7, line == 0

    def rows8(g):
        return pl.ds(8 * g, 8)

    @pl.when(turn_of == 0)
    def _():
        places = halo_places(parity, shape, STEPS, 0)
        sources = [own] + [halo.at[0] for halo in halo_refs]
        run_copies(
            [
                pltpu.make_async_copy(source, tile.at[place], sems.at[index])
                for index, (source, place) in enumerate(zip(sources, places))
            ]
        )
        first[...] = jnp.zeros_like(first)
        second[...] = jnp.zeros_like(second)
        grad[...] = jnp.zeros_like(grad)

        def pack(i, carried):
            for g in range(groups):
                forces, speeds = jnp.zeros((8, 128), jnp.float32), jnp.zeros((8, 128), jnp.float32)
                for block in range(blocks):
                    value = tile[block * span + i, rows8(g), :]
                    here = lane // THIN == block
                    forces = jnp.where(here, pltpu.roll(value, THIN * block, 1), forces)
                    speeds = jnp.where(
                        here, pltpu.roll(value, (THIN * block - THIN) % 128, 1), speeds
                    )
                inject[i, rows8(g), :] = forces
                coef[i, rows8(g), :] = speeds
            return carried

        lax.fori_loop(0, span, pack, 0)

    def sweep(source, target, half, laps):
        def load(i):
            return [source[i, rows8(g), :] for g in range(groups)]

        def body(index, carried):
            below, centre = carried
            for offset in range(THIN_UNROLL):
                i = index * THIN_UNROLL + offset
                above = load(i + 2)
                ups = [pltpu.roll(c, 7, 0) for c in centre]
                downs = [pltpu.roll(c, 1, 0) for c in centre]
                done = []
                for g, c in enumerate(centre):
                    up = jnp.where(last_line, ups[g + 1], ups[g]) if g + 1 < groups else ups[g]
                    down = jnp.where(first_line, downs[g - 1], downs[g]) if g > 0 else downs[g]
                    left = jnp.where(last_lane, 0.0, pltpu.roll(c, 127, 1))
                    right = jnp.where(first_lane, 0.0, pltpu.roll(c, 1, 1))
                    laplace = (above[g] + below[g]) + (up + down) + (left + right) - 6.0 * c
                    force = inject[i, rows8(g), :]
                    forced = laplace + jnp.where(in_block == DEPTH, force, 0.0)
                    fresh = (2.0 * c - target[i + 1, rows8(g), :]) + coef[i, rows8(g), :] * forced
                    done.append((g, pltpu.roll(force, 127, 1), fresh))
                for g, force, fresh in done:
                    inject[i, rows8(g), :] = force
                    target[i + 1, rows8(g), :] = fresh
                for g, _, fresh in done[margin : groups - margin]:
                    for block in range(rows // span):
                        moved = pltpu.roll(fresh, 128 - THIN * (block + STEPS // span), 1)
                        at = (block * span + i, rows8(g - margin), slice(None))
                        grad[at] = grad[at] + laps[(1 - half,) + at] * moved
                below, centre = centre, above
            return below, centre

        lax.fori_loop(0, span // THIN_UNROLL, body, (load(0), load(1)))
        for g in range(groups):
            target[0, rows8(g), :] = pltpu.roll(target[span, rows8(g), :], THIN, 1)
            target[span + 1, rows8(g), :] = pltpu.roll(target[1, rows8(g), :], 128 - THIN, 1)

    @pl.when(turn_of < STEPS // 4)
    def _():
        sweep(first, second, 0, laps_late)
        sweep(second, first, 1, laps_late)

    @pl.when(turn_of >= STEPS // 4)
    def _():
        sweep(first, second, 0, laps_early)
        sweep(second, first, 1, laps_early)

    @pl.when(turn_of == STEPS // 2 - 1)
    def _():
        height = rows // blocks
        for p in range(height):
            for g in range(cols // 8):
                value = jnp.zeros((8, 128), jnp.float32)
                for block in range(blocks):
                    moved = pltpu.roll(grad[block * height + p, rows8(g), :], THIN * block, 1)
                    value = jnp.where(lane // THIN == block, moved, value)
                packed_out[p, rows8(g), :] = value


def run_thin(parity, own, halos, laps_early, laps_late):
    rows, cols = own.shape[:2]
    extended = (rows + 2 * STEPS, cols + 2 * STEPS, 128)
    span = extended[0] * THIN // 128
    packed = (rows * THIN // 128, cols, 128)
    half = STEPS // 4
    any_spec = pl.BlockSpec(memory_space=pltpu.HBM)
    return pl.pallas_call(
        functools.partial(thin_kernel, own.shape),
        grid=(STEPS // 2,),
        in_specs=[pl.BlockSpec(memory_space=pltpu.SMEM)]
        + [any_spec] * 5
        + [
            pl.BlockSpec(
                (2, rows, cols, 128), lambda step: (jnp.minimum(half - 1, 2 * half - 1 - step), 0, 0, 0)
            ),
            pl.BlockSpec(
                (2, rows, cols, 128), lambda step: (jnp.maximum(0, half - 1 - step), 0, 0, 0)
            ),
        ],
        out_specs=whole(packed),
        out_shape=jax.ShapeDtypeStruct(packed, jnp.float32),
        scratch_shapes=[
            pltpu.VMEM(extended, jnp.float32),
            pltpu.VMEM((span + 2, extended[1], 128), jnp.float32),
            pltpu.VMEM((span + 2, extended[1], 128), jnp.float32),
            pltpu.VMEM((span, extended[1], 128), jnp.float32),
            pltpu.VMEM((span, extended[1], 128), jnp.float32),
            pltpu.VMEM((rows, cols, 128), jnp.float32),
            pltpu.SemaphoreType.DMA((5,)),
        ],
        cost_estimate=pl.CostEstimate(flops=10**8, bytes_accessed=5 * 10**7, transcendentals=0),
        compiler_params=pltpu.CompilerParams(vmem_limit_bytes=VMEM_LIMIT),
    )(parity, own, *halos, laps_early, laps_late)


def final_kernel(ours, theirs, thin_ours, thin_theirs, coef, noise, sample, total):
    block = pl.program_id(0)
    lane = lax.broadcasted_iota(jnp.int32, (8, 128), 1)
    for p in range(coef.shape[0]):
        for g in range(coef.shape[1] // 8):
            lines = pl.ds(8 * g, 8)
            thin = thin_ours[p, lines, :] + thin_theirs[p, lines, :]
            thin = jnp.where(lane < THIN, pltpu.roll(thin, lax.rem(128 - THIN * block, 128), 1), 0.0)
            for h in range(coef.shape[2] // 128):
                at = (p, lines, pl.ds(128 * h, 128))
                summed = ours[at] + theirs[at]
                if h == 0:
                    summed = summed + thin
                speed = coef[at]
                gradient = summed / speed
                total[at] = gradient
                sample[at] = (
                    speed
                    + step_eta * (prior_prec * (prior_centre - speed) - gradient)
                    + math.sqrt(2.0 * step_eta) * noise[at]
                )


def run_final(ours, theirs, thin_ours, thin_theirs, coef, noise):
    blocks = 128 // THIN
    part = pl.BlockSpec((coef.shape[0] // blocks,) + coef.shape[1:], lambda step: (step, 0, 0))
    thin = whole(thin_ours.shape)
    field = jax.ShapeDtypeStruct(coef.shape, jnp.float32)
    return pl.pallas_call(
        final_kernel,
        grid=(blocks,),
        in_specs=[part, part, thin, thin, part, part],
        out_specs=[part, part],
        out_shape=[field, field],
        compiler_params=pltpu.CompilerParams(vmem_limit_bytes=VMEM_LIMIT),
    )(ours, theirs, thin_ours, thin_theirs, coef, noise)


def receivers(observed, recv_tile, recv_cell, cell_count):
    tile_count = lax.axis_size(("gx", "gy"))
    highest = lax.Precision.HIGHEST
    tile_of = recv_tile[:, 0]
    per_tile = max(2, 2 * observed.shape[1] // tile_count)
    slot_count = tile_count * per_tile
    owner_hot = (tile_of[:, None] == jnp.arange(tile_count, dtype=jnp.int32)[None, :]).astype(
        jnp.int32
    )
    before = jnp.cumsum(owner_hot, 0) - owner_hot
    slot_of = tile_of * per_tile + jnp.sum(before * owner_hot, 1)
    routing = (slot_of[None, :] == jnp.arange(slot_count, dtype=jnp.int32)[:, None]).astype(
        jnp.float32
    )
    traces = jnp.pad(-observed[0][:, ::-1], ((0, 0), (DEPTH, 128 - DEPTH - STEPS)))
    marks = (recv_cell + 1).astype(jnp.float32)[:, None]
    lanes = jnp.arange(128, dtype=jnp.int32)[None, :]
    outgoing = jnp.dot(
        routing,
        jnp.where(lanes == MARK, marks, traces),
        precision=highest,
        preferred_element_type=jnp.float32,
    )
    arrived = lax.all_to_all(
        outgoing.reshape(tile_count, per_tile, 128),
        ("gx", "gy"),
        split_axis=0,
        concat_axis=0,
        tiled=True,
    ).reshape(slot_count, 128)
    cells = arrived[:, MARK].astype(jnp.int32) - 1
    picker = (jnp.arange(cell_count, dtype=jnp.int32)[:, None] == cells[None, :]).astype(
        jnp.float32
    )
    seen = jnp.dot(
        picker,
        jnp.where(lanes < THIN, arrived, 0.0),
        precision=highest,
        preferred_element_type=jnp.float32,
    )
    return jnp.sum(picker, 1, keepdims=True), seen


def local(
    coef, wave_now, wave_prev, adjoint_next, adjoint_after, noise, observed, recv_tile, recv_cell
):
    rows, cols, depth = coef.shape
    odd_x, odd_y = lax.axis_index("gx") % 2, lax.axis_index("gy") % 2
    parity = jnp.stack([odd_x, odd_y]).astype(jnp.int32)
    after = lambda value, *earlier: lax.optimization_barrier((value, earlier))[0]

    wave_fields = [wave_now[0], wave_prev[0], coef]
    adjoint_fields = [adjoint_next[0], adjoint_after[0]]
    sends = strips(parity, wave_fields, 0, K)
    wave_halos = swap("gx", *sends)
    counts, seen = receivers(after(observed, sends), recv_tile, recv_cell, rows * cols)
    speeds = jnp.pad(coef[:, :, :THIN], ((0, 0), (0, 0), (THIN, 128 - 2 * THIN)))
    sends = strips(parity, wave_fields, 1, K, wave_halos)
    wave_halos += swap("gy", *sends)
    sends = strips(after(parity, sends, counts, seen, speeds), adjoint_fields, 0, K)
    adjoint_halos = swap("gx", *sends)
    sends = strips(parity, adjoint_fields, 1, K, adjoint_halos)
    adjoint_halos += swap("gy", *sends)

    wave = (after(parity, sends), *wave_fields, wave_halos, wave_halos)
    now, then, *sends, laps_early, surface = run_block(*wave, False)
    wave_mid = swap("gx", *sends)
    adjoint = (after(parity, sends), *adjoint_fields, coef, adjoint_halos, wave_halos)
    later, latest, *late_sends, fields = run_block(*adjoint, True)
    sends = strips(after(parity, late_sends), [now, then], 1, K, wave_mid)
    wave_mid += swap("gy", *sends)
    adjoint_mid = swap("gx", *after(late_sends, sends))
    sends = strips(parity, [later, latest], 1, K, adjoint_mid)
    adjoint_mid += swap("gy", *sends)
    gradient = jnp.zeros(coef.shape, jnp.float32)
    wave = (after(parity, sends), now, then, coef, wave_mid, wave_halos)
    gradient, laps_late, surface = run_block(*wave, False, (fields, gradient, surface))
    thin = counts * surface.reshape(rows * cols, 128) + seen
    thin = thin.reshape(rows, cols, 128) + speeds
    sends = strips(parity, [thin], 0, STEPS)
    thin_halos = swap("gx", *sends)
    adjoint = (after(parity, sends), later, latest, coef, adjoint_mid, wave_halos)
    (gradient,) = run_block(*adjoint, True, (laps_early, gradient))
    shots = pairs(lax.axis_size("shot"), False)
    other = lax.ppermute(after(gradient, thin_halos), "shot", shots)
    sends = strips(after(parity, gradient), [thin], 1, STEPS, thin_halos)
    thin_halos += swap("gy", *sends)
    thin_gradient = run_thin(parity, thin, thin_halos, laps_early, laps_late)
    thin_other = lax.ppermute(thin_gradient, "shot", shots)
    return tuple(run_final(gradient, other, thin_gradient, thin_other, coef, noise))


def solution(mesh):
    return jax.shard_map(
        local,
        mesh=mesh,
        in_specs=(
            P("gx", "gy", None),
            P("shot", "gx", "gy", None),
            P("shot", "gx", "gy", None),
            P("shot", "gx", "gy", None),
            P("shot", "gx", "gy", None),
            P("gx", "gy", None),
            P("shot", ("gx", "gy"), None),
            P(("gx", "gy"), None),
            P(("gx", "gy")),
        ),
        out_specs=(P("gx", "gy", None), P("gx", "gy", None)),
        check_vma=False,
    )
```

time: 268 us -> 225 us (0.84)
  waiting for transfers between devices: 97 us -> 54.4 us
  other arithmetic: 18.6 us -> 1.16 us
  Pallas kernels: 95.5 us -> 108 us
    ppermute x21 -> x22, waiting for transfers between devices: 97 us -> 54.4 us  [the longest x10 26.6 us: swap(): lax.ppermute(first, axis, pairs(count, False))]
    pallas_call x4 -> x14, Pallas kernels: 95.5 us -> 108 us  [the longest x4 76.7 us: run_block(): pl.pallas_call(functools.partial(block_kernel, coef.shape, adjoint, gathe...]
    select_n x15 -> x0, other arithmetic: 10.1 us -> none  [the longest x10 7.4 us: swap(): second = lax.ppermute(jnp.where(even, low, high), axis, pairs(count, True))]
    unnamed x37 -> x34, local copies, waits for them, and re-layouts: 3.21 us -> 8.61 us
    another operation x3 -> x0, other arithmetic: 3.3 us -> none  [the longest x1 2.23 us: local(): wave_halos = trade(jnp.stack([wave_now[0], wave_prev[0], coef]))]
    ppermute x21 -> x22, starting transfers between devices: 37.2 us -> 40.3 us  [the longest x10 31.8 us: swap(): lax.ppermute(second, axis, pairs(count, True))]
    add x3 -> x2, other arithmetic: 3.2 us -> 0.4 us  [the longest x1 0.2 us: local(): thin = counts * surface.reshape(rows * cols, 128) + seen]
  transfers between devices with their start and end apart: 22 -> 23, of which waited for: 15 -> 8; matrix products, arithmetic and copies ran while one was open for 6% -> 2% of each run, Pallas kernels for 17% -> 46%
where the time goes in v2:
time: 225 us; the launch traced here: 224 us
  Pallas kernels  108 us (48%)
  waiting for transfers between devices  54.4 us (24%)
  starting transfers between devices  47.3 us (21%)
  local copies, waits for them, and re-layouts  10.5 us (5%)
    pallas_call x4, Pallas kernels, run_block(): pl.pallas_call(functools.partial(block_kernel, coef.shape, adjoint, gathe...  76.7 us
    ppermute x10, starting transfers between devices, swap(): lax.ppermute(second, axis, pairs(count, True))  31.8 us
    ppermute x10, waiting for transfers between devices, swap(): lax.ppermute(first, axis, pairs(count, False))  26.6 us
    ppermute x10, waiting for transfers between devices, swap(): lax.ppermute(second, axis, pairs(count, True))  21.6 us
    pallas_call x1, Pallas kernels, run_thin(): pl.pallas_call(functools.partial(thin_kernel, own.shape), grid=(STEPS //...  20.9 us
    unnamed x34, local copies, waits for them, and re-layouts  8.61 us
    pallas_call x8, Pallas kernels, strips(): pl.pallas_call(functools.partial(strip_kernel, axis, width, count), in_sp...  8.15 us
    all_to_all x1, starting transfers between devices, receivers(): lax.all_to_all(outgoing.reshape(tile_count, per_tile, 128), ('gx', 'gy'),...  7.02 us
  transfers between devices with their start and end apart: 23, of which 8 were waited for; matrix products, arithmetic and copies ran while one was open for 2% of the time, Pallas kernels for 46%

profile of v2, /device:TPU:10, one launch (start us, length us, event | category | flops | bytes accessed | tf_op | source)
XLA Modules:
  0.0 223.6 jit_solution(3174597455352899174)
XLA Ops:
  0.7 1.2 copy-done
  2.0 1.2 copy-done.5
  4.4 1.5 shard_map.104
  5.9 2.0 collective-permute-start
  7.9 4.3 %collective-permute-start.1 = (f32[3,8,32,256]{3,2,1,0:T(8,128)S(1)}, f32[3,8,32,256]{3,2,1,0:T(8,128)S(1)}, u32[]{:S(2)}, u32[]{:S(2)}) collective-permute-start(f32[3,8,32,256]{3,2,1,0:T(8,128)S(1)} %get-tuple-element.44), channel_id=1, source_target_pairs={{8,16},{16,8},{24,32},{32,24},{40,48},{48,40},{9,17},{17,9},{25,33... | collective-permute-start | bytes 2359304 | tf_op jit(solution)/shard_map/ppermute | solution.py:37
  13.5 7.0 %all-to-all-start = ((f32[64,2,128]{2,1,0:T(2,128)}), f32[64,2,128]{2,1,0:T(2,128)S(1)}, u32[]{:S(2)}, u32[]{:S(2)}) async-start(f32[64,2,128]{2,1,0:T(2,128)} %bitcast.6), calls=%async_computation | async-start | bytes 131072 | tf_op jit(solution)/shard_map/all_to_all | solution.py:496
  20.6 5.7 %collective-permute-done.refs_3_.refs_7_ = f32[3,8,32,256]{3,2,1,0:T(8,128)S(1)} collective-permute-done((f32[3,8,32,256]{3,2,1,0:T(8,128)}, f32[3,8,32,256]{3,2,1,0:T(8,128)S(1)}, u32[]{:S(2)}, u32[]{:S(2)}) %collective-permute-start) | collective-permute-done | bytes 786464 | tf_op jit(solution)/shard_map/ppermute | solution.py:36
  26.3 5.3 %collective-permute-done.1.refs_4_.refs_8_ = f32[3,8,32,256]{3,2,1,0:T(8,128)S(1)} collective-permute-done((f32[3,8,32,256]{3,2,1,0:T(8,128)S(1)}, f32[3,8,32,256]{3,2,1,0:T(8,128)S(1)}, u32[]{:S(2)}, u32[]{:S(2)}) %collective-permute-start.1) | collective-permute-done | bytes 786464 | tf_op jit(solution)/shard_map/ppermute | solution.py:37
  31.6 1.2 copy-done.6
  34.1 2.1 shard_map.105
  36.3 2.5 %collective-permute-start.5 = (f32[3,48,8,256]{3,2,1,0:T(8,128)}, f32[3,48,8,256]{3,2,1,0:T(8,128)}, u32[]{:S(2)}, u32[]{:S(2)}) collective-permute-start(f32[3,48,8,256]{3,2,1,0:T(8,128)} %get-tuple-element.47), channel_id=1, source_target_pairs={{1,2},{2,1},{3,4},{4,3},{5,6},{6,5},{9,10},{10,9},{11,12},{12,11},... | collective-permute-start | bytes 3538952 | tf_op jit(solution)/shard_map/ppermute | solution.py:37
  42.6 4.3 %collective-permute-start.3 = (f32[2,8,32,256]{3,2,1,0:T(8,128)S(1)}, f32[2,8,32,256]{3,2,1,0:T(8,128)S(1)}, u32[]{:S(2)}, u32[]{:S(2)}) collective-permute-start(f32[2,8,32,256]{3,2,1,0:T(8,128)S(1)} %get-tuple-element.50), channel_id=1, source_target_pairs={{8,16},{16,8},{24,32},{32,24},{40,48},{48,40},{9,17},{17,9},{25,33... | collective-permute-start | bytes 1572872 | tf_op jit(solution)/shard_map/ppermute | solution.py:37
  47.0 10.3 %collective-permute-done.2.refs_2_.refs_3_ = f32[2,8,32,256]{3,2,1,0:T(8,128)S(1)} collective-permute-done((f32[2,8,32,256]{3,2,1,0:T(8,128)S(1)}, f32[2,8,32,256]{3,2,1,0:T(8,128)S(1)}, u32[]{:S(2)}, u32[]{:S(2)}) %collective-permute-start.2) | collective-permute-done | bytes 524320 | tf_op jit(solution)/shard_map/ppermute | solution.py:36
  57.3 4.0 %collective-permute-done.3.refs_3_.refs_4_ = f32[2,8,32,256]{3,2,1,0:T(8,128)S(1)} collective-permute-done((f32[2,8,32,256]{3,2,1,0:T(8,128)S(1)}, f32[2,8,32,256]{3,2,1,0:T(8,128)S(1)}, u32[]{:S(2)}, u32[]{:S(2)}) %collective-permute-start.3) | collective-permute-done | bytes 524320 | tf_op jit(solution)/shard_map/ppermute | solution.py:37
  62.3 1.9 collective-permute-start.7
  64.3 19.1 %shard_map.108 = (f32[32,32,256]{2,1,0:T(8,128)S(1)}, f32[32,32,256]{2,1,0:T(8,128)S(1)}, f32[2,8,32,256]{3,2,1,0:T(8,128)S(1)}, f32[2,8,32,256]{3,2,1,0:T(8,128...) custom-call(s32[2]{0:T(128)S(1)} %pad_add_fusion.parity, f32[32,32,256]{2,1,0:T(8,128)} %bitcast.22, ...), custom_call_target="tpu_custom_call" | custom-call | flops 100000000 | bytes 60000000 | tf_op jit(solution)/shard_map/pallas_call | solution.py:278
  83.5 4.4 %collective-permute-start.9 = (f32[2,8,32,256]{3,2,1,0:T(8,128)S(1)}, f32[2,8,32,256]{3,2,1,0:T(8,128)S(1)}, u32[]{:S(2)}, u32[]{:S(2)}) collective-permute-start(f32[2,8,32,256]{3,2,1,0:T(8,128)S(1)} %get-tuple-element.55), channel_id=1, source_target_pairs={{8,16},{16,8},{24,32},{32,24},{40,48},{48,40},{9,17},{17,9},{25,33... | collective-permute-start | bytes 1572872 | tf_op jit(solution)/shard_map/ppermute | solution.py:37
  87.9 19.5 %shard_map.109 = (f32[32,32,256]{2,1,0:T(8,128)}, f32[32,32,256]{2,1,0:T(8,128)}, f32[2,8,32,256]{3,2,1,0:T(8,128)S(1)}, f32[2,8,32,256]{3,2,1,0:T(8,128)S(1)}, f32[8,32,32,256]{3,2,1,0:T(8,128)}) custom-call(s32[2]{0:T(128)S(1)} %pad_add_fusion.parity, f32[32,32,256]{2,1,0:T(8,128)} %bitcast.16, f32[32,32,256]{2,1,0:T(8,128)} %bitcast.19, ...), custom_call_target="tpu_custom_call" | custom-call | flops 100000000 | bytes 60000000 | tf_op jit(solution)/shard_map/pallas_call | solution.py:278
  109.4 2.5 %collective-permute-start.13 = (f32[2,48,8,256]{3,2,1,0:T(8,128)S(1)}, f32[2,48,8,256]{3,2,1,0:T(8,128)S(1)}, u32[]{:S(2)}, u32[]{:S(2)}) collective-permute-start(f32[2,48,8,256]{3,2,1,0:T(8,128)S(1)} %get-tuple-element.65), channel_id=1, source_target_pairs={{1,2},{2,1},{3,4},{4,3},{5,6},{6,5},{9,10},{10,9},{11,12},{12,11},... | collective-permute-start | bytes 2359304 | tf_op jit(solution)/shard_map/ppermute | solution.py:37
  112.0 3.9 %collective-permute-start.11 = (f32[2,8,32,256]{3,2,1,0:T(8,128)S(1)}, f32[2,8,32,256]{3,2,1,0:T(8,128)S(1)}, u32[]{:S(2)}, u32[]{:S(2)}) collective-permute-start(f32[2,8,32,256]{3,2,1,0:T(8,128)S(1)} %get-tuple-element.67), channel_id=1, source_target_pairs={{8,16},{16,8},{24,32},{32,24},{40,48},{48,40},{9,17},{17,9},{25,33... | collective-permute-start | bytes 1572872 | tf_op jit(solution)/shard_map/ppermute | solution.py:37
  116.0 10.6 %collective-permute-done.10.refs_2_.refs_3_ = f32[2,8,32,256]{3,2,1,0:T(8,128)S(1)} collective-permute-done((f32[2,8,32,256]{3,2,1,0:T(8,128)S(1)}, f32[2,8,32,256]{3,2,1,0:T(8,128)S(1)}, u32[]{:S(2)}, u32[]{:S(2)}) %collective-permute-start.10) | collective-permute-done | bytes 524320 | tf_op jit(solution)/shard_map/ppermute | solution.py:36
  126.5 4.0 %collective-permute-done.11.refs_3_.refs_4_ = f32[2,8,32,256]{3,2,1,0:T(8,128)S(1)} collective-permute-done((f32[2,8,32,256]{3,2,1,0:T(8,128)S(1)}, f32[2,8,32,256]{3,2,1,0:T(8,128)S(1)}, u32[]{:S(2)}, u32[]{:S(2)}) %collective-permute-start.11) | collective-permute-done | bytes 524320 | tf_op jit(solution)/shard_map/ppermute | solution.py:37
  131.5 1.9 collective-permute-start.15
  134.7 19.9 %shard_map.112 = (f32[32,32,256]{2,1,0:T(8,128)}, f32[8,32,32,128]{3,2,1,0:T(8,128)}, f32[32,32,128]{2,1,0:T(8,128)S(1)}) custom-call(s32[2]{0:T(128)S(1)} %pad_add_fusion.parity, f32[32,32,256]{2,1,0:T(8,128)} %copy-done.11, f32[32,32,256]{2,1,0:T(8,128)} %copy-done.12, f32[32,32,256]{2,1,0:T(8,128)} %coef.1, ...), custom_call_target="tpu_custom_call" | custom-call | flops 100000000 | bytes 60000000 | tf_op jit(solution)/shard_map/pallas_call | solution.py:278
  156.6 3.8 %collective-permute-start.17 = (f32[1,16,32,128]{3,2,1,0:T(8,128)S(1)}, f32[1,16,32,128]{3,2,1,0:T(8,128)S(1)}, u32[]{:S(2)}, u32[]{:S(2)}) collective-permute-start(f32[1,16,32,128]{3,2,1,0:T(8,128)S(1)} %get-tuple-element.75), channel_id=1, source_target_pairs={{8,16},{16,8},{24,32},{32,24},{40,48},{48,40},{9,17},{17,9},{25,33... | collective-permute-start | bytes 786440 | tf_op jit(solution)/shard_map/ppermute | solution.py:37
  160.4 18.1 %shard_map.114.ours = f32[32,32,256]{2,1,0:T(8,128)S(1)} custom-call(s32[2]{0:T(128)S(1)} %pad_add_fusion.parity, f32[32,32,256]{2,1,0:T(8,128)} %get-tuple-element.57.refs_0_, f32[32,32,256]{2,1,0:T(8,128)} %get-tuple-element.58.refs_1_, f32[32,32,256]{2,1,0:T(8,128)} %coef.1, f32[2,8,32,256]{3,2,1,0:T(8,128)S(1)} %collective-permute-done.10.refs_2_.refs_3_, ...), custom_call_target="tpu_custom_call" | custom-call | flops 100000000 | bytes 60000000 | tf_op jit(solution)/shard_map/pallas_call | solution.py:278
  178.6 2.7 %collective-permute-start.18 = (f32[32,32,256]{2,1,0:T(8,128)S(1)}, f32[32,32,256]{2,1,0:T(8,128)S(1)}, u32[]{:S(2)}, u32[]{:S(2)}) collective-permute-start(f32[32,32,256]{2,1,0:T(8,128)S(1)} %shard_map.114.ours), channel_id=1, source_target_pairs={{0,64},{64,0},{1,65},{65,1},{2,66},{66,2},{3,67},{67,3},{4,68},{68... | collective-permute-start | bytes 3145736 | tf_op jit(solution)/shard_map/ppermute | solution.py:557
  182.9 2.3 %collective-permute-start.20 = (f32[1,64,16,128]{3,2,1,0:T(8,128)S(1)}, f32[1,64,16,128]{3,2,1,0:T(8,128)S(1)}, u32[]{:S(2)}, u32[]{:S(2)}) collective-permute-start(f32[1,64,16,128]{3,2,1,0:T(8,128)S(1)} %get-tuple-element.82), channel_id=1, source_target_pairs={{1,2},{2,1},{3,4},{4,3},{5,6},{6,5},{9,10},{10,9},{11,12},{12,11},... | collective-permute-start | bytes 1572872 | tf_op jit(solution)/shard_map/ppermute | solution.py:37
  185.2 8.2 %collective-permute-done.20.refs_3_ = f32[1,64,16,128]{3,2,1,0:T(8,128)S(1)} collective-permute-done((f32[1,64,16,128]{3,2,1,0:T(8,128)S(1)}, f32[1,64,16,128]{3,2,1,0:T(8,128)S(1)}, u32[]{:S(2)}, u32[]{:S(2)}) %collective-permute-start.20) | collective-permute-done | bytes 524320 | tf_op jit(solution)/shard_map/ppermute | solution.py:37
  193.4 20.9 %shard_map.116.thin_ours = f32[8,32,128]{2,1,0:T(8,128)S(1)} custom-call(s32[2]{0:T(128)S(1)} %pad_add_fusion.parity, f32[32,32,128]{2,1,0:T(8,128)S(1)} %pad_add_fusion.1.refs_0_.own, f32[1,16,32,128]{3,2,1,0:T(8,128)S(1)} %collective-permute-done.16.refs_1_.refs_0_, f32[1,16,32,128]{3,2,1,0:T(8,128)S(1)} %collective-permute-done.17.refs_2_.refs_1_, ...), custom_call_target="tpu_custom_call" | custom-call | flops 100000000 | bytes 50000000 | tf_op jit(solution)/shard_map/pallas_call | solution.py:406
  215.4 6.2 %collective-permute-done.21.thin_theirs = f32[8,32,128]{2,1,0:T(8,128)S(1)} collective-permute-done((f32[8,32,128]{2,1,0:T(8,128)S(1)}, f32[8,32,128]{2,1,0:T(8,128)S(1)}, u32[]{:S(2)}, u32[]{:S(2)}) %collective-permute-start.21) | collective-permute-done | bytes 131104 | tf_op jit(solution)/shard_map/ppermute | solution.py:561
  221.6 2.0 shard_map.117
  (80 shorter events, 17.7 us)
Async XLA Ops:
  4.4 7.9 %copy-start.14 = (f32[1,64,16]{1,2,0:T(8,128)S(1)}, f32[1,64,16]{1,2,0:T(8,128)}, u32[]{:S(2)}) copy-start(f32[1,64,16]{1,2,0:T(8,128)} %param.15) | copy-start | bytes 12292
  4.4 8.2 %copy-start.16 = (s32[64]{0:T(128)S(1)}, s32[64]{0:T(128)}, u32[]{:S(2)}) copy-start(s32[64]{0:T(128)} %param.17) | copy-start | bytes 772
  4.4 27.2 %copy-start.1 = (f32[32,32,256]{2,1,0:T(8,128)S(1)}, f32[32,32,256]{2,1,0:T(8,128)}, u32[]{:S(2)}) copy-start(f32[32,32,256]{2,1,0:T(8,128)} %coef.1) | copy-start | bytes 3145732
  5.9 20.4 %collective-permute-start = (f32[3,8,32,256]{3,2,1,0:T(8,128)}, f32[3,8,32,256]{3,2,1,0:T(8,128)S(1)}, u32[]{:S(2)}, u32[]{:S(2)}) collective-permute-start(f32[3,8,32,256]{3,2,1,0:T(8,128)} %get-tuple-element.43), channel_id=1, source_target_pairs={{0,8},{8,0},{16,24},{24,16},{32,40},{40,32},{48,56},{56,48},{1,9},... | collective-permute-start | bytes 2359304 | tf_op jit(solution)/shard_map/ppermute | solution.py:36
  7.9 23.7 %collective-permute-start.1 = (f32[3,8,32,256]{3,2,1,0:T(8,128)S(1)}, f32[3,8,32,256]{3,2,1,0:T(8,128)S(1)}, u32[]{:S(2)}, u32[]{:S(2)}) collective-permute-start(f32[3,8,32,256]{3,2,1,0:T(8,128)S(1)} %get-tuple-element.44), channel_id=1, source_target_pairs={{8,16},{16,8},{24,32},{32,24},{40,48},{48,40},{9,17},{17,9},{25,33... | collective-permute-start | bytes 2359304 | tf_op jit(solution)/shard_map/ppermute | solution.py:37
  13.5 25.3 %all-to-all-start = ((f32[64,2,128]{2,1,0:T(2,128)}), f32[64,2,128]{2,1,0:T(2,128)S(1)}, u32[]{:S(2)}, u32[]{:S(2)}) async-start(f32[64,2,128]{2,1,0:T(2,128)} %bitcast.6), calls=%async_computation | async-start | bytes 131072 | tf_op jit(solution)/shard_map/all_to_all | solution.py:496
  36.2 28.0 %collective-permute-start.4 = (f32[3,48,8,256]{3,2,1,0:T(8,128)}, f32[3,48,8,256]{3,2,1,0:T(8,128)}, u32[]{:S(2)}, u32[]{:S(2)}) collective-permute-start(f32[3,48,8,256]{3,2,1,0:T(8,128)} %get-tuple-element.46), channel_id=1, source_target_pairs={{0,1},{1,0},{2,3},{3,2},{4,5},{5,4},{6,7},{7,6},{8,9},{9,8},{10,11... | collective-permute-start | bytes 3538952 | tf_op jit(solution)/shard_map/ppermute | solution.py:36
  36.3 27.9 %collective-permute-start.5 = (f32[3,48,8,256]{3,2,1,0:T(8,128)}, f32[3,48,8,256]{3,2,1,0:T(8,128)}, u32[]{:S(2)}, u32[]{:S(2)}) collective-permute-start(f32[3,48,8,256]{3,2,1,0:T(8,128)} %get-tuple-element.47), channel_id=1, source_target_pairs={{1,2},{2,1},{3,4},{4,3},{5,6},{6,5},{9,10},{10,9},{11,12},{12,11},... | collective-permute-start | bytes 3538952 | tf_op jit(solution)/shard_map/ppermute | solution.py:37
  42.5 14.7 %collective-permute-start.2 = (f32[2,8,32,256]{3,2,1,0:T(8,128)S(1)}, f32[2,8,32,256]{3,2,1,0:T(8,128)S(1)}, u32[]{:S(2)}, u32[]{:S(2)}) collective-permute-start(f32[2,8,32,256]{3,2,1,0:T(8,128)S(1)} %get-tuple-element.49), channel_id=1, source_target_pairs={{0,8},{8,0},{16,24},{24,16},{32,40},{40,32},{48,56},{56,48},{1,9},... | collective-permute-start | bytes 1572872 | tf_op jit(solution)/shard_map/ppermute | solution.py:36
  42.6 18.7 %collective-permute-start.3 = (f32[2,8,32,256]{3,2,1,0:T(8,128)S(1)}, f32[2,8,32,256]{3,2,1,0:T(8,128)S(1)}, u32[]{:S(2)}, u32[]{:S(2)}) collective-permute-start(f32[2,8,32,256]{3,2,1,0:T(8,128)S(1)} %get-tuple-element.50), channel_id=1, source_target_pairs={{8,16},{16,8},{24,32},{32,24},{40,48},{48,40},{9,17},{17,9},{25,33... | collective-permute-start | bytes 1572872 | tf_op jit(solution)/shard_map/ppermute | solution.py:37
  62.1 25.7 %collective-permute-start.6 = (f32[2,48,8,256]{3,2,1,0:T(8,128)S(1)}, f32[2,48,8,256]{3,2,1,0:T(8,128)S(1)}, u32[]{:S(2)}, u32[]{:S(2)}) collective-permute-start(f32[2,48,8,256]{3,2,1,0:T(8,128)S(1)} %get-tuple-element.51), channel_id=1, source_target_pairs={{0,1},{1,0},{2,3},{3,2},{4,5},{5,4},{6,7},{7,6},{8,9},{9,8},{10,11... | collective-permute-start | bytes 2359304 | tf_op jit(solution)/shard_map/ppermute | solution.py:36
  62.3 25.5 %collective-permute-start.7 = (f32[2,48,8,256]{3,2,1,0:T(8,128)S(1)}, f32[2,48,8,256]{3,2,1,0:T(8,128)S(1)}, u32[]{:S(2)}, u32[]{:S(2)}) collective-permute-start(f32[2,48,8,256]{3,2,1,0:T(8,128)S(1)} %get-tuple-element.52), channel_id=1, source_target_pairs={{1,2},{2,1},{3,4},{4,3},{5,6},{6,5},{9,10},{10,9},{11,12},{12,11},... | collective-permute-start | bytes 2359304 | tf_op jit(solution)/shard_map/ppermute | solution.py:37
  83.3 24.1 %copy-start.11 = (f32[32,32,256]{2,1,0:T(8,128)}, f32[32,32,256]{2,1,0:T(8,128)S(1)}, u32[]{:S(2)}) copy-start(f32[32,32,256]{2,1,0:T(8,128)S(1)} %get-tuple-element.62.refs_0_) | copy-start | bytes 3145732
  83.4 24.1 %copy-start.12 = (f32[32,32,256]{2,1,0:T(8,128)}, f32[32,32,256]{2,1,0:T(8,128)S(1)}, u32[]{:S(2)}) copy-start(f32[32,32,256]{2,1,0:T(8,128)S(1)} %get-tuple-element.63.refs_1_) | copy-start | bytes 3145732
  83.4 24.1 %collective-permute-start.8 = (f32[2,8,32,256]{3,2,1,0:T(8,128)S(1)}, f32[2,8,32,256]{3,2,1,0:T(8,128)S(1)}, u32[]{:S(2)}, u32[]{:S(2)}) collective-permute-start(f32[2,8,32,256]{3,2,1,0:T(8,128)S(1)} %get-tuple-element.54), channel_id=1, source_target_pairs={{0,8},{8,0},{16,24},{24,16},{32,40},{40,32},{48,56},{56,48},{1,9},... | collective-permute-start | bytes 1572872 | tf_op jit(solution)/shard_map/ppermute | solution.py:36
  83.5 24.0 %collective-permute-start.9 = (f32[2,8,32,256]{3,2,1,0:T(8,128)S(1)}, f32[2,8,32,256]{3,2,1,0:T(8,128)S(1)}, u32[]{:S(2)}, u32[]{:S(2)}) collective-permute-start(f32[2,8,32,256]{3,2,1,0:T(8,128)S(1)} %get-tuple-element.55), channel_id=1, source_target_pairs={{8,16},{16,8},{24,32},{32,24},{40,48},{48,40},{9,17},{17,9},{25,33... | collective-permute-start | bytes 1572872 | tf_op jit(solution)/shard_map/ppermute | solution.py:37
  107.5 23.1 %copy-start.10 = (f32[32,32,256]{2,1,0:T(8,128)S(1)}, f32[32,32,256]{2,1,0:T(8,128)}, u32[]{:S(2)}) copy-start(f32[32,32,256]{2,1,0:T(8,128)} %get-tuple-element.58.refs_1_) | copy-start | bytes 3145732
  108.3 22.2 %copy-start.9 = (f32[32,32,256]{2,1,0:T(8,128)S(1)}, f32[32,32,256]{2,1,0:T(8,128)}, u32[]{:S(2)}) copy-start(f32[32,32,256]{2,1,0:T(8,128)} %get-tuple-element.57.refs_0_) | copy-start | bytes 3145732
  108.4 25.2 %collective-permute-start.12 = (f32[2,48,8,256]{3,2,1,0:T(8,128)S(1)}, f32[2,48,8,256]{3,2,1,0:T(8,128)S(1)}, u32[]{:S(2)}, u32[]{:S(2)}) collective-permute-start(f32[2,48,8,256]{3,2,1,0:T(8,128)S(1)} %get-tuple-element.64), channel_id=1, source_target_pairs={{0,1},{1,0},{2,3},{3,2},{4,5},{5,4},{6,7},{7,6},{8,9},{9,8},{10,11... | collective-permute-start | bytes 2359304 | tf_op jit(solution)/shard_map/ppermute | solution.py:36
  109.4 24.1 %collective-permute-start.13 = (f32[2,48,8,256]{3,2,1,0:T(8,128)S(1)}, f32[2,48,8,256]{3,2,1,0:T(8,128)S(1)}, u32[]{:S(2)}, u32[]{:S(2)}) collective-permute-start(f32[2,48,8,256]{3,2,1,0:T(8,128)S(1)} %get-tuple-element.65), channel_id=1, source_target_pairs={{1,2},{2,1},{3,4},{4,3},{5,6},{6,5},{9,10},{10,9},{11,12},{12,11},... | collective-permute-start | bytes 2359304 | tf_op jit(solution)/shard_map/ppermute | solution.py:37
  112.0 14.6 %collective-permute-start.10 = (f32[2,8,32,256]{3,2,1,0:T(8,128)S(1)}, f32[2,8,32,256]{3,2,1,0:T(8,128)S(1)}, u32[]{:S(2)}, u32[]{:S(2)}) collective-permute-start(f32[2,8,32,256]{3,2,1,0:T(8,128)S(1)} %get-tuple-element.66), channel_id=1, source_target_pairs={{0,8},{8,0},{16,24},{24,16},{32,40},{40,32},{48,56},{56,48},{1,9},... | collective-permute-start | bytes 1572872 | tf_op jit(solution)/shard_map/ppermute | solution.py:36
  112.0 18.5 %collective-permute-start.11 = (f32[2,8,32,256]{3,2,1,0:T(8,128)S(1)}, f32[2,8,32,256]{3,2,1,0:T(8,128)S(1)}, u32[]{:S(2)}, u32[]{:S(2)}) collective-permute-start(f32[2,8,32,256]{3,2,1,0:T(8,128)S(1)} %get-tuple-element.67), channel_id=1, source_target_pairs={{8,16},{16,8},{24,32},{32,24},{40,48},{48,40},{9,17},{17,9},{25,33... | collective-permute-start | bytes 1572872 | tf_op jit(solution)/shard_map/ppermute | solution.py:37
  131.4 29.0 %collective-permute-start.14 = (f32[2,48,8,256]{3,2,1,0:T(8,128)S(1)}, f32[2,48,8,256]{3,2,1,0:T(8,128)S(1)}, u32[]{:S(2)}, u32[]{:S(2)}) collective-permute-start(f32[2,48,8,256]{3,2,1,0:T(8,128)S(1)} %get-tuple-element.68), channel_id=1, source_target_pairs={{0,1},{1,0},{2,3},{3,2},{4,5},{5,4},{6,7},{7,6},{8,9},{9,8},{10,11... | collective-permute-start | bytes 2359304 | tf_op jit(solution)/shard_map/ppermute | solution.py:36
  131.5 28.9 %collective-permute-start.15 = (f32[2,48,8,256]{3,2,1,0:T(8,128)S(1)}, f32[2,48,8,256]{3,2,1,0:T(8,128)S(1)}, u32[]{:S(2)}, u32[]{:S(2)}) collective-permute-start(f32[2,48,8,256]{3,2,1,0:T(8,128)S(1)} %get-tuple-element.69), channel_id=1, source_target_pairs={{1,2},{2,1},{3,4},{4,3},{5,6},{6,5},{9,10},{10,9},{11,12},{12,11},... | collective-permute-start | bytes 2359304 | tf_op jit(solution)/shard_map/ppermute | solution.py:37
  156.5 22.1 %collective-permute-start.16 = (f32[1,16,32,128]{3,2,1,0:T(8,128)S(1)}, f32[1,16,32,128]{3,2,1,0:T(8,128)S(1)}, u32[]{:S(2)}, u32[]{:S(2)}) collective-permute-start(f32[1,16,32,128]{3,2,1,0:T(8,128)S(1)} %get-tuple-element.74), channel_id=1, source_target_pairs={{0,8},{8,0},{16,24},{24,16},{32,40},{40,32},{48,56},{56,48},{1,9},... | collective-permute-start | bytes 786440 | tf_op jit(solution)/shard_map/ppermute | solution.py:36
  156.6 22.0 %collective-permute-start.17 = (f32[1,16,32,128]{3,2,1,0:T(8,128)S(1)}, f32[1,16,32,128]{3,2,1,0:T(8,128)S(1)}, u32[]{:S(2)}, u32[]{:S(2)}) collective-permute-start(f32[1,16,32,128]{3,2,1,0:T(8,128)S(1)} %get-tuple-element.75), channel_id=1, source_target_pairs={{8,16},{16,8},{24,32},{32,24},{40,48},{48,40},{9,17},{17,9},{25,33... | collective-permute-start | bytes 786440 | tf_op jit(solution)/shard_map/ppermute | solution.py:37
  178.6 43.0 %collective-permute-start.18 = (f32[32,32,256]{2,1,0:T(8,128)S(1)}, f32[32,32,256]{2,1,0:T(8,128)S(1)}, u32[]{:S(2)}, u32[]{:S(2)}) collective-permute-start(f32[32,32,256]{2,1,0:T(8,128)S(1)} %shard_map.114.ours), channel_id=1, source_target_pairs={{0,64},{64,0},{1,65},{65,1},{2,66},{66,2},{3,67},{67,3},{4,68},{68... | collective-permute-start | bytes 3145736 | tf_op jit(solution)/shard_map/ppermute | solution.py:557
  182.0 3.2 %collective-permute-start.19 = (f32[1,64,16,128]{3,2,1,0:T(8,128)S(1)}, f32[1,64,16,128]{3,2,1,0:T(8,128)S(1)}, u32[]{:S(2)}, u32[]{:S(2)}) collective-permute-start(f32[1,64,16,128]{3,2,1,0:T(8,128)S(1)} %get-tuple-element.81), channel_id=1, source_target_pairs={{0,1},{1,0},{2,3},{3,2},{4,5},{5,4},{6,7},{7,6},{8,9},{9,8},{10,11... | collective-permute-start | bytes 1572872 | tf_op jit(solution)/shard_map/ppermute | solution.py:36
  182.9 10.5 %collective-permute-start.20 = (f32[1,64,16,128]{3,2,1,0:T(8,128)S(1)}, f32[1,64,16,128]{3,2,1,0:T(8,128)S(1)}, u32[]{:S(2)}, u32[]{:S(2)}) collective-permute-start(f32[1,64,16,128]{3,2,1,0:T(8,128)S(1)} %get-tuple-element.82), channel_id=1, source_target_pairs={{1,2},{2,1},{3,4},{4,3},{5,6},{6,5},{9,10},{10,9},{11,12},{12,11},... | collective-permute-start | bytes 1572872 | tf_op jit(solution)/shard_map/ppermute | solution.py:37
  193.4 28.2 %copy-start.2 = (f32[32,32,256]{2,1,0:T(8,128)S(1)}, f32[32,32,256]{2,1,0:T(8,128)}, u32[]{:S(2)}) copy-start(f32[32,32,256]{2,1,0:T(8,128)} %coef.1) | copy-start | bytes 3145732
  193.4 28.2 %copy-start.13 = (f32[32,32,256]{2,1,0:T(8,128)S(1)}, f32[32,32,256]{2,1,0:T(8,128)}, u32[]{:S(2)}) copy-start(f32[32,32,256]{2,1,0:T(8,128)} %noise.1) | copy-start | bytes 3145732
  214.3 7.3 %collective-permute-start.21 = (f32[8,32,128]{2,1,0:T(8,128)S(1)}, f32[8,32,128]{2,1,0:T(8,128)S(1)}, u32[]{:S(2)}, u32[]{:S(2)}) collective-permute-start(f32[8,32,128]{2,1,0:T(8,128)S(1)} %shard_map.116.thin_ours), channel_id=1, source_target_pairs={{0,64},{64,0},{1,65},{65,1},{2,66},{66,2},{3,67},{67,3},{4,68},{68... | collective-permute-start | bytes 393224 | tf_op jit(solution)/shard_map/ppermute | solution.py:561
  (9 other events, 17.4 us)

commit v3 on v2

--- a/solution.py
+++ b/solution.py
@@ -14,9 +14,11 @@
 UNROLL = 8
 THIN = 32
 MARK = 64
+COEF_HALOS = 6
 THIN_UNROLL = 4
 VMEM_LIMIT = 48 * 1024 * 1024
 STRIP_VMEM_LIMIT = 16 * 1024 * 1024
+FIRST_VMEM_LIMIT = 60 * 1024 * 1024
 
 step_eta = 0.01
 prior_prec = 4.0
@@ -38,11 +40,10 @@
     )
 
 
-def strip_kernel(axis, width, count, parity, *refs):
+def strip_kernel(shape, axis, width, count, parity, *refs):
     fields, refs = refs[:count], refs[count:]
-    received, refs = refs[: 2 * axis], refs[2 * axis :]
-    sends, sems = refs[:2], refs[2]
-    rows, cols = fields[0].shape[:2]
+    received, sends, sems = refs[:-3], refs[-3:-1], refs[-1]
+    rows, cols = shape[:2]
     far = (rows, cols)[axis] - width
     even = parity[axis] == 0
     copies = []
@@ -50,51 +51,62 @@
     def copy(source, target):
         copies.append(pltpu.make_async_copy(source, target, sems.at[len(copies)]))
 
+    top = width + (rows if fields else 0)
+    places = [jnp.where(parity[0] == 0, *pair) for pair in ((top, 0), (0, top))]
     for send, start in zip(sends, (jnp.where(even, far, 0), jnp.where(even, 0, far))):
-        if axis == 1:
-            part = pl.ds(pl.multiple_of(start, 8), width)
-            above, below = rows + width, 0
-            places = [jnp.where(parity[0] == 0, *pair) for pair in ((above, below), (below, above))]
-        for index, field in enumerate(fields):
-            if axis == 0:
+        if axis == 0:
+            for index, field in enumerate(fields):
                 copy(field.at[pl.ds(start, width)], send.at[index])
-            else:
-                copy(field.at[:, part], send.at[index, pl.ds(width, rows)])
-                for strip, place in zip(received, places):
-                    copy(strip.at[index, :, part], send.at[index, pl.ds(place, width)])
+            continue
+        part = pl.ds(pl.multiple_of(start, 8), width)
+        for index in range(send.shape[0]):
+            if fields:
+                inner = pl.ds(width if received else 0, rows)
+                copy(fields[index].at[:, part], send.at[index, inner])
+            for strip, place in zip(received, places):
+                copy(strip.at[index, :, part], send.at[index, pl.ds(place, width)])
     run_copies(copies)
 
 
-def strips(parity, fields, axis, width, received=()):
-    rows, cols, depth = fields[0].shape
-    count = len(fields)
-    shape = (count, width, cols, depth) if axis == 0 else (count, rows + 2 * width, width, depth)
+def strips(parity, fields, axis, width, received=(), limit=None):
+    rows, cols, depth = fields[0].shape if fields else (0, received[0].shape[2], received[0].shape[3])
+    count = len(fields) if fields else received[0].shape[0]
+    height = rows + (2 * width if received else 0)
+    shape = (count, width, cols, depth) if axis == 0 else (count, height, width, depth)
     send = jax.ShapeDtypeStruct(shape, jnp.float32)
     anywhere = pl.BlockSpec(memory_space=pl.ANY)
+    copies = 2 * (len(fields) + count * len(received))
     return pl.pallas_call(
-        functools.partial(strip_kernel, axis, width, count),
-        in_specs=[pl.BlockSpec(memory_space=pltpu.SMEM)] + [anywhere] * (count + len(received)),
-        out_specs=[anywhere, anywhere],
+        functools.partial(strip_kernel, (rows, cols), axis, width, len(fields)),
+        in_specs=[pl.BlockSpec(memory_space=pltpu.SMEM)]
+        + [anywhere] * (len(fields) + len(received)),
+        out_specs=[pl.BlockSpec(memory_space=pltpu.VMEM)] * 2,
         out_shape=[send, send],
-        scratch_shapes=[pltpu.SemaphoreType.DMA(((2 + 4 * axis) * count,))],
-        compiler_params=pltpu.CompilerParams(vmem_limit_bytes=STRIP_VMEM_LIMIT),
+        scratch_shapes=[pltpu.SemaphoreType.DMA((copies,))],
+        compiler_params=pltpu.CompilerParams(vmem_limit_bytes=limit or STRIP_VMEM_LIMIT),
     )(parity, *fields, *received)
 
 
-def halo_places(parity, shape, width, pad):
+def halo_places(parity, shape, width, pad, halos):
     rows, cols = shape[:2]
     x_first = jnp.where(parity[0] == 0, rows + width, 0) + pad
     x_second = jnp.where(parity[0] == 0, 0, rows + width) + pad
-    y_first = pl.multiple_of(jnp.where(parity[1] == 0, cols + width, 0), 8)
-    y_second = pl.multiple_of(jnp.where(parity[1] == 0, 0, cols + width), 8)
-    inner, every = pl.ds(width, cols), pl.ds(pad, rows + 2 * width)
-    return (
-        (pl.ds(width + pad, rows), inner),
-        (pl.ds(x_first, width), inner),
-        (pl.ds(x_second, width), inner),
-        (every, pl.ds(y_first, width)),
-        (every, pl.ds(y_second, width)),
-    )
+    y_places = [
+        pl.ds(pl.multiple_of(jnp.where(parity[1] == 0, *pair), 8), width)
+        for pair in ((cols + width, 0), (0, cols + width))
+    ]
+    inner = pl.ds(width, cols)
+    every, middle = pl.ds(pad, rows + 2 * width), pl.ds(pad + width, rows)
+    ends = [(pl.ds(0, width), pl.ds(pad, width))]
+    ends += [(pl.ds(width, width), pl.ds(pad + width + rows, width))]
+    found = [(halos[0], (pl.ds(x_first, width), inner))]
+    found += [(halos[1], (pl.ds(x_second, width), inner))]
+    if len(halos) == 4:
+        return found + [(halo, (every, place)) for halo, place in zip(halos[2:], y_places)]
+    found += [(halo, (middle, place)) for halo, place in zip(halos[2:4], y_places)]
+    for halo, place in zip(halos[4:], y_places):
+        found += [(halo.at[part], (rows_at, place)) for part, rows_at in ends]
+    return found
 
 
 def run_copies(copies, between=None):
@@ -106,14 +118,12 @@
         copy.wait()
 
 
-def block_kernel(shape, adjoint, gather, parity, *refs):
+def block_kernel(shape, adjoint, gather, halo_count, first_part, parity, *refs):
     rows, cols, depth = shape
     own_refs, refs = refs[:3], refs[3:]
-    halo_refs, refs = refs[:8], refs[8:]
+    halo_refs, refs = refs[:halo_count], refs[halo_count:]
     if gather:
-        factor, grad_in, refs = refs[0], refs[1], refs[2:]
-    if gather and not adjoint:
-        surface_in, refs = refs[0], refs[1:]
+        factor, carried_in, refs = refs[0], refs[1], refs[2:]
     if gather:
         grad, refs = refs[0], refs[1:]
     else:
@@ -136,12 +146,13 @@
 
     @pl.when(turn_of == 0)
     def _():
-        places = halo_places(parity, shape, K, 1)
         copies = []
         for index, (own, target) in enumerate(zip(own_refs, (first, second, coef))):
-            halos = halo_refs[4:] if index == 2 else halo_refs[:4]
-            sources = [own] + [halo.at[index] for halo in halos]
-            for source, place in zip(sources, places):
+            halos = halo_refs[-COEF_HALOS:] if index == 2 else halo_refs[:-COEF_HALOS]
+            part = 2 if index == 2 else first_part + index
+            found = halo_places(parity, shape, K, 1, [halo.at[part] for halo in halos])
+            found += [(own, (pl.ds(edge, rows), pl.ds(K, cols)))]
+            for source, place in found:
                 copies.append(
                     pltpu.make_async_copy(source, target.at[place], sems.at[len(copies)])
                 )
@@ -151,9 +162,9 @@
                 field[0] = jnp.zeros(field.shape[1:], jnp.float32)
                 field[rows + 2 * K + 1] = jnp.zeros(field.shape[1:], jnp.float32)
             if gather:
-                grad[...] = grad_in[...]
+                grad[...] = carried_in[...] if adjoint else jnp.zeros_like(grad)
             if not adjoint:
-                surface[...] = surface_in[...] if gather else jnp.zeros_like(surface)
+                surface[...] = carried_in[...] if gather else jnp.zeros_like(surface)
 
         run_copies(copies, pads)
         if adjoint and not gather:
@@ -247,23 +258,21 @@
     return pl.BlockSpec(shape, lambda step: (0,) * len(shape))
 
 
-def run_block(parity, current, previous, coef, halos, coef_halos, adjoint, gather=None):
+def run_block(parity, current, previous, coef, halos, coef_halos, adjoint, gather=None, first_part=0):
     rows, cols, depth = coef.shape
     extended = (rows + 2 * K + 2, cols + 2 * K, depth)
     any_spec = pl.BlockSpec(memory_space=pltpu.HBM)
     field = jax.ShapeDtypeStruct(coef.shape, jnp.float32)
     strips = jax.ShapeDtypeStruct((2, K, cols, depth), jnp.float32)
     flat = (rows, cols, 128)
-    in_specs = [pl.BlockSpec(memory_space=pltpu.SMEM)] + [any_spec] * 11
+    in_specs = [pl.BlockSpec(memory_space=pltpu.SMEM)] + [any_spec] * (3 + len(halos) + COEF_HALOS)
     operands = [parity, current, previous, coef, *halos, *coef_halos]
     if gather is not None:
         operands += gather
         in_specs += [
             pl.BlockSpec((2,) + coef.shape, lambda step: (K // 2 - 1 - step, 0, 0, 0)),
-            whole(coef.shape),
+            whole(coef.shape if adjoint else flat),
         ]
-        if not adjoint:
-            in_specs += [whole(flat)]
         out_shape, out_specs = [field], [whole(coef.shape)]
     else:
         out_shape = [field, field, strips, strips]
@@ -276,13 +285,20 @@
         out_shape += [jax.ShapeDtypeStruct(flat, jnp.float32)]
         out_specs += [whole(flat)]
     return pl.pallas_call(
-        functools.partial(block_kernel, coef.shape, adjoint, gather is not None),
+        functools.partial(
+            block_kernel,
+            coef.shape,
+            adjoint,
+            gather is not None,
+            len(halos) + COEF_HALOS,
+            first_part,
+        ),
         grid=(K // 2,),
         in_specs=in_specs,
         out_specs=out_specs,
         out_shape=out_shape,
         scratch_shapes=[pltpu.VMEM(extended, jnp.float32)] * 3
-        + [pltpu.SemaphoreType.DMA((15,)), pltpu.SemaphoreType.DMA((6,))],
+        + [pltpu.SemaphoreType.DMA((27,)), pltpu.SemaphoreType.DMA((6,))],
         cost_estimate=pl.CostEstimate(flops=10**8, bytes_accessed=6 * 10**7, transcendentals=0),
         compiler_params=pltpu.CompilerParams(vmem_limit_bytes=VMEM_LIMIT),
     )(*operands)
@@ -308,12 +324,12 @@
 
     @pl.when(turn_of == 0)
     def _():
-        places = halo_places(parity, shape, STEPS, 0)
-        sources = [own] + [halo.at[0] for halo in halo_refs]
+        found = halo_places(parity, shape, STEPS, 0, [halo.at[0] for halo in halo_refs])
+        found += [(own, (pl.ds(STEPS, rows), pl.ds(STEPS, cols)))]
         run_copies(
             [
                 pltpu.make_async_copy(source, tile.at[place], sems.at[index])
-                for index, (source, place) in enumerate(zip(sources, places))
+                for index, (source, place) in enumerate(found)
             ]
         )
         first[...] = jnp.zeros_like(first)
@@ -521,42 +537,41 @@
     parity = jnp.stack([odd_x, odd_y]).astype(jnp.int32)
     after = lambda value, *earlier: lax.optimization_barrier((value, earlier))[0]
 
-    wave_fields = [wave_now[0], wave_prev[0], coef]
-    adjoint_fields = [adjoint_next[0], adjoint_after[0]]
-    sends = strips(parity, wave_fields, 0, K)
-    wave_halos = swap("gx", *sends)
-    counts, seen = receivers(after(observed, sends), recv_tile, recv_cell, rows * cols)
+    fields = [wave_now[0], wave_prev[0], coef, adjoint_next[0], adjoint_after[0]]
+    sends = strips(parity, fields, 0, K, limit=FIRST_VMEM_LIMIT)
+    halos = swap("gx", *sends)
+    early = after(parity, sends)
+    sends_y = strips(early, fields, 1, K)
+    halos += swap("gy", *sends_y)
+    counts, seen = receivers(after(observed, sends_y), recv_tile, recv_cell, rows * cols)
     speeds = jnp.pad(coef[:, :, :THIN], ((0, 0), (0, 0), (THIN, 128 - 2 * THIN)))
-    sends = strips(parity, wave_fields, 1, K, wave_halos)
-    wave_halos += swap("gy", *sends)
-    sends = strips(after(parity, sends, counts, seen, speeds), adjoint_fields, 0, K)
-    adjoint_halos = swap("gx", *sends)
-    sends = strips(parity, adjoint_fields, 1, K, adjoint_halos)
-    adjoint_halos += swap("gy", *sends)
-
-    wave = (after(parity, sends), *wave_fields, wave_halos, wave_halos)
+    sends = strips(after(parity, counts, seen, speeds), [], 1, K, halos[:2])
+    halos += swap("gy", *sends)
+
+    wave = (after(parity, sends), *fields[:3], halos, halos)
     now, then, *sends, laps_early, surface = run_block(*wave, False)
     wave_mid = swap("gx", *sends)
-    adjoint = (after(parity, sends), *adjoint_fields, coef, adjoint_halos, wave_halos)
-    later, latest, *late_sends, fields = run_block(*adjoint, True)
-    sends = strips(after(parity, late_sends), [now, then], 1, K, wave_mid)
+    sends_y = strips(after(parity, sends), [now, then], 1, K)
+    wave_mid += swap("gy", *sends_y)
+    adjoint = (after(parity, sends_y), *fields[3:], coef, halos, halos)
+    later, latest, *late_sends, ahead = run_block(*adjoint, True, first_part=3)
+    sends = strips(after(parity, late_sends), [], 1, K, wave_mid[:2])
     wave_mid += swap("gy", *sends)
     adjoint_mid = swap("gx", *after(late_sends, sends))
-    sends = strips(parity, [later, latest], 1, K, adjoint_mid)
-    adjoint_mid += swap("gy", *sends)
-    gradient = jnp.zeros(coef.shape, jnp.float32)
-    wave = (after(parity, sends), now, then, coef, wave_mid, wave_halos)
-    gradient, laps_late, surface = run_block(*wave, False, (fields, gradient, surface))
+    wave = (parity, now, then, coef, wave_mid, halos)
+    gradient, laps_late, surface = run_block(*wave, False, (ahead, surface))
     thin = counts * surface.reshape(rows * cols, 128) + seen
     thin = thin.reshape(rows, cols, 128) + speeds
+    sends = strips(after(parity, surface), [later, latest], 1, K, adjoint_mid)
+    adjoint_mid += swap("gy", *sends)
     sends = strips(parity, [thin], 0, STEPS)
     thin_halos = swap("gx", *sends)
-    adjoint = (after(parity, sends), later, latest, coef, adjoint_mid, wave_halos)
+    sends = strips(parity, [thin], 1, STEPS, thin_halos)
+    thin_halos += swap("gy", *sends)
+    adjoint = (after(parity, sends), later, latest, coef, adjoint_mid, halos)
     (gradient,) = run_block(*adjoint, True, (laps_early, gradient))
     shots = pairs(lax.axis_size("shot"), False)
     other = lax.ppermute(after(gradient, thin_halos), "shot", shots)
-    sends = strips(after(parity, gradient), [thin], 1, STEPS, thin_halos)
-    thin_halos += swap("gy", *sends)
     thin_gradient = run_thin(parity, thin, thin_halos, laps_early, laps_late)
     thin_other = lax.ppermute(thin_gradient, "shot", shots)
     return tuple(run_final(gradient, other, thin_gradient, thin_other, coef, noise))

time: 225 us -> 206 us (0.916)
  waiting for transfers between devices: 54.4 us -> 37.5 us
  local copies, waits for them, and re-layouts: 10.5 us -> 6.7 us
    ppermute x10, waiting for transfers between devices: 26.6 us -> 5.48 us  [swap(): lax.ppermute(first, axis, pairs(count, False))]
    all_to_all x1, waiting for transfers between devices: 0.01 us -> 11.3 us  [receivers(): lax.all_to_all(outgoing.reshape(tile_count, per_tile, 128), ('gx', 'gy'),...]
    ppermute x10, waiting for transfers between devices: 21.6 us -> 14.4 us  [swap(): lax.ppermute(second, axis, pairs(count, True))]
    pallas_call x8, Pallas kernels: 8.15 us -> 11 us  [strips(): pl.pallas_call(functools.partial(strip_kernel, (rows, cols), axis, width,...]
    unnamed x34 -> x38, local copies, waits for them, and re-layouts: 8.61 us -> 6.68 us
  transfers between devices with their start and end apart: 23 -> 23, of which waited for: 8 -> 6; matrix products, arithmetic and copies ran while one was open for 2% -> 1% of each run, Pallas kernels for 46% -> 41%
where the time goes in v3:
time: 206 us; the launch traced here: 205 us
  Pallas kernels  110 us (53%)
  starting transfers between devices  46.5 us (23%)
  waiting for transfers between devices  37.5 us (18%)
  local copies, waits for them, and re-layouts  6.7 us (3%)
    pallas_call x4, Pallas kernels, run_block(): pl.pallas_call(functools.partial(block_kernel, coef.shape, adjoint, gathe...  76 us
    ppermute x10, starting transfers between devices, swap(): lax.ppermute(second, axis, pairs(count, True))  30.9 us
    pallas_call x1, Pallas kernels, run_thin(): pl.pallas_call(functools.partial(thin_kernel, own.shape), grid=(STEPS //...  20.9 us
    ppermute x10, waiting for transfers between devices, swap(): lax.ppermute(second, axis, pairs(count, True))  14.4 us
    all_to_all x1, waiting for transfers between devices, receivers(): lax.all_to_all(outgoing.reshape(tile_count, per_tile, 128), ('gx', 'gy'),...  11.3 us
    pallas_call x8, Pallas kernels, strips(): pl.pallas_call(functools.partial(strip_kernel, (rows, cols), axis, width,...  11 us
    all_to_all x1, starting transfers between devices, receivers(): lax.all_to_all(outgoing.reshape(tile_count, per_tile, 128), ('gx', 'gy'),...  7.32 us
    unnamed x38, local copies, waits for them, and re-layouts  6.68 us
  transfers between devices with their start and end apart: 23, of which 6 were waited for; matrix products, arithmetic and copies ran while one was open for 1% of the time, Pallas kernels for 41%

profile of v3, /device:TPU:10, one launch (start us, length us, event | category | flops | bytes accessed | tf_op | source)
XLA Modules:
  0.0 204.8 jit_solution(13899023913693723510)
XLA Ops:
  1.3 4.0 %shard_map.104 = (f32[5,8,32,256]{3,2,1,0:T(8,128)}, f32[5,8,32,256]{3,2,1,0:T(8,128)}) custom-call(s32[2]{0:T(128)} %pad_add_fusion.parity, f32[32,32,256]{2,1,0:T(8,128)} %bitcast.16, f32[32,32,256]{2,1,0:T(8,128)} %bitcast.19, f32[32,32,256]{2,1,0:T(8,128)} %coef.1, f32[32,32,256]{2,1,0:T(8,128)} %bitcast.22, f32[32,32,256]{2,1,0:T(8,128)} %bitcast.25), custom_call_target="tpu_custom_call" | custom-call | tf_op jit(solution)/shard_map/pallas_call | solution.py:79
  5.4 2.0 collective-permute-start
  7.4 4.3 %collective-permute-start.1 = (f32[5,8,32,256]{3,2,1,0:T(8,128)}, f32[5,8,32,256]{3,2,1,0:T(8,128)S(1)}, u32[]{:S(2)}, u32[]{:S(2)}) collective-permute-start(f32[5,8,32,256]{3,2,1,0:T(8,128)} %get-tuple-element.45), channel_id=1, source_target_pairs={{8,16},{16,8},{24,32},{32,24},{40,48},{48,40},{9,17},{17,9},{25,33... | collective-permute-start | bytes 3932168 | tf_op jit(solution)/shard_map/ppermute | solution.py:39
  11.7 1.2 copy-done.2
  12.9 1.2 copy-done.4
  14.1 1.2 copy-done.6
  15.4 1.2 copy-done.7
  16.6 1.2 copy-done.9
  17.8 2.3 %shard_map.105 = (f32[5,32,8,256]{3,2,1,0:T(8,128)}, f32[5,32,8,256]{3,2,1,0:T(8,128)}) custom-call(s32[2]{0:T(128)S(1)} %copy-done.15, f32[32,32,256]{2,1,0:T(8,128)S(1)} %bitcast.17, f32[32,32,256]{2,1,0:T(8,128)S(1)} %bitcast.21, f32[32,32,256]{2,1,0:T(8,128)S(1)} %copy-done.2, f32[32,32,256]{2,1,0:T(8,128)S(1)} %bitcast.23, f32[32,32,256]{2,1,0:T(8,128)S(1)} %bitcast.27), custom_call_target="tpu_custom_call" | custom-call | tf_op jit(solution)/shard_map/pallas_call | solution.py:79
  20.3 2.5 %collective-permute-start.3 = (f32[5,32,8,256]{3,2,1,0:T(8,128)}, f32[5,32,8,256]{3,2,1,0:T(8,128)}, u32[]{:S(2)}, u32[]{:S(2)}) collective-permute-start(f32[5,32,8,256]{3,2,1,0:T(8,128)} %get-tuple-element.48), channel_id=1, source_target_pairs={{1,2},{2,1},{3,4},{4,3},{5,6},{6,5},{9,10},{10,9},{11,12},{12,11},... | collective-permute-start | bytes 3932168 | tf_op jit(solution)/shard_map/ppermute | solution.py:39
  24.1 7.3 %all-to-all-start = ((f32[64,2,128]{2,1,0:T(2,128)}), f32[64,2,128]{2,1,0:T(2,128)S(1)}, u32[]{:S(2)}, u32[]{:S(2)}) async-start(f32[64,2,128]{2,1,0:T(2,128)} %bitcast.8), calls=%async_computation | async-start | bytes 131072 | tf_op jit(solution)/shard_map/all_to_all | solution.py:512
  31.5 11.3 %all-to-all-done = f32[64,2,128]{2,1,0:T(2,128)S(1)} async-done(((f32[64,2,128]{2,1,0:T(2,128)}), f32[64,2,128]{2,1,0:T(2,128)S(1)}, u32[]{:S(2)}, u32[]{:S(2)}) %all-to-all-start) | async-done | bytes 65568 | tf_op jit(solution)/shard_map/all_to_all | solution.py:512
  45.0 3.0 %collective-permute-start.5 = (f32[5,16,8,256]{3,2,1,0:T(8,128)S(1)}, f32[5,16,8,256]{3,2,1,0:T(8,128)S(1)}, u32[]{:S(2)}, u32[]{:S(2)}) collective-permute-start(f32[5,16,8,256]{3,2,1,0:T(8,128)S(1)} %get-tuple-element.52), channel_id=1, source_target_pairs={{1,2},{2,1},{3,4},{4,3},{5,6},{6,5},{9,10},{10,9},{11,12},{12,11},... | collective-permute-start | bytes 1966088 | tf_op jit(solution)/shard_map/ppermute | solution.py:39
  48.1 8.8 %collective-permute-done.5.refs_8_.refs_14_.refs_12_ = f32[5,16,8,256]{3,2,1,0:T(8,128)S(1)} collective-permute-done((f32[5,16,8,256]{3,2,1,0:T(8,128)S(1)}, f32[5,16,8,256]{3,2,1,0:T(8,128)S(1)}, u32[]{:S(2)}, u32[]{:S(2)}) %collective-permute-start.5) | collective-permute-done | bytes 655392 | tf_op jit(solution)/shard_map/ppermute | solution.py:39
  56.9 19.1 %shard_map.107 = (f32[32,32,256]{2,1,0:T(8,128)S(1)}, f32[32,32,256]{2,1,0:T(8,128)S(1)}, f32[2,8,32,256]{3,2,1,0:T(8,128)S(1)}, f32[2,8,32,256]{3,2,1,0:T(8,128...) custom-call(s32[2]{0:T(128)S(1)} %copy-done.15, f32[32,32,256]{2,1,0:T(8,128)S(1)} %bitcast.18, ...), custom_call_target="tpu_custom_call" | custom-call | flops 100000000 | bytes 60000000 | tf_op jit(solution)/shard_map/pallas_call | solution.py:287
  76.9 4.5 %collective-permute-start.7 = (f32[2,8,32,256]{3,2,1,0:T(8,128)S(1)}, f32[2,8,32,256]{3,2,1,0:T(8,128)S(1)}, u32[]{:S(2)}, u32[]{:S(2)}) collective-permute-start(f32[2,8,32,256]{3,2,1,0:T(8,128)S(1)} %get-tuple-element.57), channel_id=1, source_target_pairs={{8,16},{16,8},{24,32},{32,24},{40,48},{48,40},{9,17},{17,9},{25,33... | collective-permute-start | bytes 1572872 | tf_op jit(solution)/shard_map/ppermute | solution.py:39
  82.3 2.6 %collective-permute-start.9 = (f32[2,32,8,256]{3,2,1,0:T(8,128)S(1)}, f32[2,32,8,256]{3,2,1,0:T(8,128)S(1)}, u32[]{:S(2)}, u32[]{:S(2)}) collective-permute-start(f32[2,32,8,256]{3,2,1,0:T(8,128)S(1)} %get-tuple-element.60), channel_id=1, source_target_pairs={{1,2},{2,1},{3,4},{4,3},{5,6},{6,5},{9,10},{10,9},{11,12},{12,11},... | collective-permute-start | bytes 1572872 | tf_op jit(solution)/shard_map/ppermute | solution.py:39
  84.9 19.0 %shard_map.109 = (f32[32,32,256]{2,1,0:T(8,128)S(1)}, f32[32,32,256]{2,1,0:T(8,128)S(1)}, f32[2,8,32,256]{3,2,1,0:T(8,128)S(1)}, f32[2,8,32,256]{3,2,1,0:T(8,128)S(1)}, f32[8,32,32,256]{3,2,1,0:T(8,128)}) custom-call(s32[2]{0:T(128)S(1)} %copy-done.15, f32[32,32,256]{2,1,0:T(8,128)S(1)} %bitcast.24, f32[32,32,256]{2,1,0:T(8,128)} %bitcast.26, ...), custom_call_target="tpu_custom_call" | custom-call | flops 100000000 | bytes 60000000 | tf_op jit(solution)/shard_map/pallas_call | solution.py:287
  105.5 2.3 %collective-permute-start.11 = (f32[2,16,8,256]{3,2,1,0:T(8,128)S(1)}, f32[2,16,8,256]{3,2,1,0:T(8,128)S(1)}, u32[]{:S(2)}, u32[]{:S(2)}) collective-permute-start(f32[2,16,8,256]{3,2,1,0:T(8,128)S(1)} %get-tuple-element.66), channel_id=1, source_target_pairs={{1,2},{2,1},{3,4},{4,3},{5,6},{6,5},{9,10},{10,9},{11,12},{12,11},... | collective-permute-start | bytes 786440 | tf_op jit(solution)/shard_map/ppermute | solution.py:39
  107.9 3.6 %collective-permute-start.15 = (f32[2,8,32,256]{3,2,1,0:T(8,128)S(1)}, f32[2,8,32,256]{3,2,1,0:T(8,128)S(1)}, u32[]{:S(2)}, u32[]{:S(2)}) collective-permute-start(f32[2,8,32,256]{3,2,1,0:T(8,128)S(1)} %get-tuple-element.78), channel_id=1, source_target_pairs={{8,16},{16,8},{24,32},{32,24},{40,48},{48,40},{9,17},{17,9},{25,33... | collective-permute-start | bytes 1572872 | tf_op jit(solution)/shard_map/ppermute | solution.py:39
  111.7 1.5 collective-permute-done.11.refs_8_
  113.2 19.9 %shard_map.111 = (f32[32,32,256]{2,1,0:T(8,128)S(1)}, f32[8,32,32,128]{3,2,1,0:T(8,128)}, f32[32,32,128]{2,1,0:T(8,128)S(1)}) custom-call(s32[2]{0:T(128)S(1)} %copy-done.15, f32[32,32,256]{2,1,0:T(8,128)} %copy-done.10, f32[32,32,256]{2,1,0:T(8,128)} %copy-done.11, f32[32,32,256]{2,1,0:T(8,128)} %coef.1, ...), custom_call_target="tpu_custom_call" | custom-call | flops 100000000 | bytes 60000000 | tf_op jit(solution)/shard_map/pallas_call | solution.py:287
  134.6 2.3 %collective-permute-start.17 = (f32[2,48,8,256]{3,2,1,0:T(8,128)S(1)}, f32[2,48,8,256]{3,2,1,0:T(8,128)S(1)}, u32[]{:S(2)}, u32[]{:S(2)}) collective-permute-start(f32[2,48,8,256]{3,2,1,0:T(8,128)S(1)} %get-tuple-element.81), channel_id=1, source_target_pairs={{1,2},{2,1},{3,4},{4,3},{5,6},{6,5},{9,10},{10,9},{11,12},{12,11},... | collective-permute-start | bytes 2359304 | tf_op jit(solution)/shard_map/ppermute | solution.py:39
  137.8 3.6 %collective-permute-start.13 = (f32[1,16,32,128]{3,2,1,0:T(8,128)S(1)}, f32[1,16,32,128]{3,2,1,0:T(8,128)S(1)}, u32[]{:S(2)}, u32[]{:S(2)}) collective-permute-start(f32[1,16,32,128]{3,2,1,0:T(8,128)S(1)} %get-tuple-element.71), channel_id=1, source_target_pairs={{8,16},{16,8},{24,32},{32,24},{40,48},{48,40},{9,17},{17,9},{25,33... | collective-permute-start | bytes 786440 | tf_op jit(solution)/shard_map/ppermute | solution.py:39
  141.4 5.5 %collective-permute-done.12.refs_1_.refs_0_ = f32[1,16,32,128]{3,2,1,0:T(8,128)S(1)} collective-permute-done((f32[1,16,32,128]{3,2,1,0:T(8,128)S(1)}, f32[1,16,32,128]{3,2,1,0:T(8,128)S(1)}, u32[]{:S(2)}, u32[]{:S(2)}) %collective-permute-start.12) | collective-permute-done | bytes 262176 | tf_op jit(solution)/shard_map/ppermute | solution.py:38
  146.9 4.0 %collective-permute-done.13.refs_2_.refs_1_ = f32[1,16,32,128]{3,2,1,0:T(8,128)S(1)} collective-permute-done((f32[1,16,32,128]{3,2,1,0:T(8,128)S(1)}, f32[1,16,32,128]{3,2,1,0:T(8,128)S(1)}, u32[]{:S(2)}, u32[]{:S(2)}) %collective-permute-start.13) | collective-permute-done | bytes 262176 | tf_op jit(solution)/shard_map/ppermute | solution.py:39
  151.7 2.1 %collective-permute-start.19 = (f32[1,64,16,128]{3,2,1,0:T(8,128)S(1)}, f32[1,64,16,128]{3,2,1,0:T(8,128)S(1)}, u32[]{:S(2)}, u32[]{:S(2)}) collective-permute-start(f32[1,64,16,128]{3,2,1,0:T(8,128)S(1)} %get-tuple-element.73), channel_id=1, source_target_pairs={{1,2},{2,1},{3,4},{4,3},{5,6},{6,5},{9,10},{10,9},{11,12},{12,11},... | collective-permute-start | bytes 1572872 | tf_op jit(solution)/shard_map/ppermute | solution.py:39
  153.9 18.0 %shard_map.115.ours = f32[32,32,256]{2,1,0:T(8,128)S(1)} custom-call(s32[2]{0:T(128)S(1)} %copy-done.15, f32[32,32,256]{2,1,0:T(8,128)S(1)} %get-tuple-element.75.refs_0_, f32[32,32,256]{2,1,0:T(8,128)} %copy-done.12, f32[32,32,256]{2,1,0:T(8,128)} %coef.1, f32[2,8,32,256]{3,2,1,0:T(8,128)S(1)} %collective-permute-done.14.refs_2_.refs_3_, ...), custom_call_target="tpu_custom_call" | custom-call | flops 100000000 | bytes 60000000 | tf_op jit(solution)/shard_map/pallas_call | solution.py:287
  171.9 2.7 %collective-permute-start.20 = (f32[32,32,256]{2,1,0:T(8,128)S(1)}, f32[32,32,256]{2,1,0:T(8,128)S(1)}, u32[]{:S(2)}, u32[]{:S(2)}) collective-permute-start(f32[32,32,256]{2,1,0:T(8,128)S(1)} %shard_map.115.ours), channel_id=1, source_target_pairs={{0,64},{64,0},{1,65},{65,1},{2,66},{66,2},{3,67},{67,3},{4,68},{68... | collective-permute-start | bytes 3145736 | tf_op jit(solution)/shard_map/ppermute | solution.py:574
  174.6 20.9 %shard_map.116.thin_ours = f32[8,32,128]{2,1,0:T(8,128)S(1)} custom-call(s32[2]{0:T(128)S(1)} %copy-done.15, f32[32,32,128]{2,1,0:T(8,128)S(1)} %pad_add_fusion.1.refs_0_.own, f32[1,16,32,128]{3,2,1,0:T(8,128)S(1)} %collective-permute-done.12.refs_1_.refs_0_, f32[1,16,32,128]{3,2,1,0:T(8,128)S(1)} %collective-permute-done.13.refs_2_.refs_1_, ...), custom_call_target="tpu_custom_call" | custom-call | flops 100000000 | bytes 50000000 | tf_op jit(solution)/shard_map/pallas_call | solution.py:422
  196.4 6.3 %collective-permute-done.21.thin_theirs = f32[8,32,128]{2,1,0:T(8,128)S(1)} collective-permute-done((f32[8,32,128]{2,1,0:T(8,128)S(1)}, f32[8,32,128]{2,1,0:T(8,128)S(1)}, u32[]{:S(2)}, u32[]{:S(2)}) %collective-permute-start.21) | collective-permute-done | bytes 131104 | tf_op jit(solution)/shard_map/ppermute | solution.py:576
  202.8 2.0 shard_map.117
  (83 shorter events, 11.8 us)
Async XLA Ops:
  1.3 10.4 %copy-start.15 = (s32[2]{0:T(128)S(1)}, s32[2]{0:T(128)}, u32[]{:S(2)}) copy-start(s32[2]{0:T(128)} %pad_add_fusion.parity) | copy-start | bytes 28
  5.4 38.0 %collective-permute-start = (f32[5,8,32,256]{3,2,1,0:T(8,128)}, f32[5,8,32,256]{3,2,1,0:T(8,128)S(1)}, u32[]{:S(2)}, u32[]{:S(2)}) collective-permute-start(f32[5,8,32,256]{3,2,1,0:T(8,128)} %get-tuple-element.44), channel_id=1, source_target_pairs={{0,8},{8,0},{16,24},{24,16},{32,40},{40,32},{48,56},{56,48},{1,9},... | collective-permute-start | bytes 3932168 | tf_op jit(solution)/shard_map/ppermute | solution.py:38
  7.4 36.0 %collective-permute-start.1 = (f32[5,8,32,256]{3,2,1,0:T(8,128)}, f32[5,8,32,256]{3,2,1,0:T(8,128)S(1)}, u32[]{:S(2)}, u32[]{:S(2)}) collective-permute-start(f32[5,8,32,256]{3,2,1,0:T(8,128)} %get-tuple-element.45), channel_id=1, source_target_pairs={{8,16},{16,8},{24,32},{32,24},{40,48},{48,40},{9,17},{17,9},{25,33... | collective-permute-start | bytes 3932168 | tf_op jit(solution)/shard_map/ppermute | solution.py:39
  17.8 5.4 %copy-start.18 = (s32[64]{0:T(128)S(1)}, s32[64]{0:T(128)}, u32[]{:S(2)}) copy-start(s32[64]{0:T(128)} %param.17) | copy-start | bytes 772
  20.2 27.9 %collective-permute-start.2 = (f32[5,32,8,256]{3,2,1,0:T(8,128)}, f32[5,32,8,256]{3,2,1,0:T(8,128)}, u32[]{:S(2)}, u32[]{:S(2)}) collective-permute-start(f32[5,32,8,256]{3,2,1,0:T(8,128)} %get-tuple-element.47), channel_id=1, source_target_pairs={{0,1},{1,0},{2,3},{3,2},{4,5},{5,4},{6,7},{7,6},{8,9},{9,8},{10,11... | collective-permute-start | bytes 3932168 | tf_op jit(solution)/shard_map/ppermute | solution.py:38
  20.3 27.8 %collective-permute-start.3 = (f32[5,32,8,256]{3,2,1,0:T(8,128)}, f32[5,32,8,256]{3,2,1,0:T(8,128)}, u32[]{:S(2)}, u32[]{:S(2)}) collective-permute-start(f32[5,32,8,256]{3,2,1,0:T(8,128)} %get-tuple-element.48), channel_id=1, source_target_pairs={{1,2},{2,1},{3,4},{4,3},{5,6},{6,5},{9,10},{10,9},{11,12},{12,11},... | collective-permute-start | bytes 3932168 | tf_op jit(solution)/shard_map/ppermute | solution.py:39
  24.1 18.6 %all-to-all-start = ((f32[64,2,128]{2,1,0:T(2,128)}), f32[64,2,128]{2,1,0:T(2,128)S(1)}, u32[]{:S(2)}, u32[]{:S(2)}) async-start(f32[64,2,128]{2,1,0:T(2,128)} %bitcast.8), calls=%async_computation | async-start | bytes 131072 | tf_op jit(solution)/shard_map/all_to_all | solution.py:512
  43.3 13.6 %copy-start.5 = (f32[1,32,32,256]{3,2,1,0:T(8,128)S(1)}, f32[1,32,32,256]{3,2,1,0:T(8,128)}, u32[]{:S(2)}) copy-start(f32[1,32,32,256]{3,2,1,0:T(8,128)} %param.10) | copy-start | bytes 3145732
  44.9 3.2 %collective-permute-start.4 = (f32[5,16,8,256]{3,2,1,0:T(8,128)S(1)}, f32[5,16,8,256]{3,2,1,0:T(8,128)S(1)}, u32[]{:S(2)}, u32[]{:S(2)}) collective-permute-start(f32[5,16,8,256]{3,2,1,0:T(8,128)S(1)} %get-tuple-element.51), channel_id=1, source_target_pairs={{0,1},{1,0},{2,3},{3,2},{4,5},{5,4},{6,7},{7,6},{8,9},{9,8},{10,11... | collective-permute-start | bytes 1966088 | tf_op jit(solution)/shard_map/ppermute | solution.py:38
  45.0 11.9 %collective-permute-start.5 = (f32[5,16,8,256]{3,2,1,0:T(8,128)S(1)}, f32[5,16,8,256]{3,2,1,0:T(8,128)S(1)}, u32[]{:S(2)}, u32[]{:S(2)}) collective-permute-start(f32[5,16,8,256]{3,2,1,0:T(8,128)S(1)} %get-tuple-element.52), channel_id=1, source_target_pairs={{1,2},{2,1},{3,4},{4,3},{5,6},{6,5},{9,10},{10,9},{11,12},{12,11},... | collective-permute-start | bytes 1966088 | tf_op jit(solution)/shard_map/ppermute | solution.py:39
  76.0 27.9 %copy-start.10 = (f32[32,32,256]{2,1,0:T(8,128)}, f32[32,32,256]{2,1,0:T(8,128)S(1)}, u32[]{:S(2)}) copy-start(f32[32,32,256]{2,1,0:T(8,128)S(1)} %get-tuple-element.54.refs_0_) | copy-start | bytes 3145732
  76.1 27.9 %copy-start.11 = (f32[32,32,256]{2,1,0:T(8,128)}, f32[32,32,256]{2,1,0:T(8,128)S(1)}, u32[]{:S(2)}) copy-start(f32[32,32,256]{2,1,0:T(8,128)S(1)} %get-tuple-element.55.refs_1_) | copy-start | bytes 3145732
  76.1 8.8 %copy-start.8 = (f32[1,32,32,256]{3,2,1,0:T(8,128)S(1)}, f32[1,32,32,256]{3,2,1,0:T(8,128)}, u32[]{:S(2)}) copy-start(f32[1,32,32,256]{3,2,1,0:T(8,128)} %param.12) | copy-start | bytes 3145732
  76.1 27.9 %collective-permute-start.6 = (f32[2,8,32,256]{3,2,1,0:T(8,128)S(1)}, f32[2,8,32,256]{3,2,1,0:T(8,128)S(1)}, u32[]{:S(2)}, u32[]{:S(2)}) collective-permute-start(f32[2,8,32,256]{3,2,1,0:T(8,128)S(1)} %get-tuple-element.56), channel_id=1, source_target_pairs={{0,8},{8,0},{16,24},{24,16},{32,40},{40,32},{48,56},{56,48},{1,9},... | collective-permute-start | bytes 1572872 | tf_op jit(solution)/shard_map/ppermute | solution.py:38
  76.9 27.1 %collective-permute-start.7 = (f32[2,8,32,256]{3,2,1,0:T(8,128)S(1)}, f32[2,8,32,256]{3,2,1,0:T(8,128)S(1)}, u32[]{:S(2)}, u32[]{:S(2)}) collective-permute-start(f32[2,8,32,256]{3,2,1,0:T(8,128)S(1)} %get-tuple-element.57), channel_id=1, source_target_pairs={{8,16},{16,8},{24,32},{32,24},{40,48},{48,40},{9,17},{17,9},{25,33... | collective-permute-start | bytes 1572872 | tf_op jit(solution)/shard_map/ppermute | solution.py:39
  82.1 25.8 %collective-permute-start.8 = (f32[2,32,8,256]{3,2,1,0:T(8,128)S(1)}, f32[2,32,8,256]{3,2,1,0:T(8,128)S(1)}, u32[]{:S(2)}, u32[]{:S(2)}) collective-permute-start(f32[2,32,8,256]{3,2,1,0:T(8,128)S(1)} %get-tuple-element.59), channel_id=1, source_target_pairs={{0,1},{1,0},{2,3},{3,2},{4,5},{5,4},{6,7},{7,6},{8,9},{9,8},{10,11... | collective-permute-start | bytes 1572872 | tf_op jit(solution)/shard_map/ppermute | solution.py:38
  82.3 29.4 %collective-permute-start.9 = (f32[2,32,8,256]{3,2,1,0:T(8,128)S(1)}, f32[2,32,8,256]{3,2,1,0:T(8,128)S(1)}, u32[]{:S(2)}, u32[]{:S(2)}) collective-permute-start(f32[2,32,8,256]{3,2,1,0:T(8,128)S(1)} %get-tuple-element.60), channel_id=1, source_target_pairs={{1,2},{2,1},{3,4},{4,3},{5,6},{6,5},{9,10},{10,9},{11,12},{12,11},... | collective-permute-start | bytes 1572872 | tf_op jit(solution)/shard_map/ppermute | solution.py:39
  104.0 29.3 %copy-start.12 = (f32[32,32,256]{2,1,0:T(8,128)}, f32[32,32,256]{2,1,0:T(8,128)S(1)}, u32[]{:S(2)}) copy-start(f32[32,32,256]{2,1,0:T(8,128)S(1)} %get-tuple-element.76.refs_1_) | copy-start | bytes 3145732
  104.7 6.9 %collective-permute-start.10 = (f32[2,16,8,256]{3,2,1,0:T(8,128)S(1)}, f32[2,16,8,256]{3,2,1,0:T(8,128)S(1)}, u32[]{:S(2)}, u32[]{:S(2)}) collective-permute-start(f32[2,16,8,256]{3,2,1,0:T(8,128)S(1)} %get-tuple-element.65), channel_id=1, source_target_pairs={{0,1},{1,0},{2,3},{3,2},{4,5},{5,4},{6,7},{7,6},{8,9},{9,8},{10,11... | collective-permute-start | bytes 786440 | tf_op jit(solution)/shard_map/ppermute | solution.py:38
  105.5 7.7 %collective-permute-start.11 = (f32[2,16,8,256]{3,2,1,0:T(8,128)S(1)}, f32[2,16,8,256]{3,2,1,0:T(8,128)S(1)}, u32[]{:S(2)}, u32[]{:S(2)}) collective-permute-start(f32[2,16,8,256]{3,2,1,0:T(8,128)S(1)} %get-tuple-element.66), channel_id=1, source_target_pairs={{1,2},{2,1},{3,4},{4,3},{5,6},{6,5},{9,10},{10,9},{11,12},{12,11},... | collective-permute-start | bytes 786440 | tf_op jit(solution)/shard_map/ppermute | solution.py:39
  107.8 25.5 %collective-permute-start.14 = (f32[2,8,32,256]{3,2,1,0:T(8,128)S(1)}, f32[2,8,32,256]{3,2,1,0:T(8,128)S(1)}, u32[]{:S(2)}, u32[]{:S(2)}) collective-permute-start(f32[2,8,32,256]{3,2,1,0:T(8,128)S(1)} %get-tuple-element.77), channel_id=1, source_target_pairs={{0,8},{8,0},{16,24},{24,16},{32,40},{40,32},{48,56},{56,48},{1,9},... | collective-permute-start | bytes 1572872 | tf_op jit(solution)/shard_map/ppermute | solution.py:38
  107.9 25.4 %collective-permute-start.15 = (f32[2,8,32,256]{3,2,1,0:T(8,128)S(1)}, f32[2,8,32,256]{3,2,1,0:T(8,128)S(1)}, u32[]{:S(2)}, u32[]{:S(2)}) collective-permute-start(f32[2,8,32,256]{3,2,1,0:T(8,128)S(1)} %get-tuple-element.78), channel_id=1, source_target_pairs={{8,16},{16,8},{24,32},{32,24},{40,48},{48,40},{9,17},{17,9},{25,33... | collective-permute-start | bytes 1572872 | tf_op jit(solution)/shard_map/ppermute | solution.py:39
  134.2 19.7 %collective-permute-start.16 = (f32[2,48,8,256]{3,2,1,0:T(8,128)S(1)}, f32[2,48,8,256]{3,2,1,0:T(8,128)S(1)}, u32[]{:S(2)}, u32[]{:S(2)}) collective-permute-start(f32[2,48,8,256]{3,2,1,0:T(8,128)S(1)} %get-tuple-element.80), channel_id=1, source_target_pairs={{0,1},{1,0},{2,3},{3,2},{4,5},{5,4},{6,7},{7,6},{8,9},{9,8},{10,11... | collective-permute-start | bytes 2359304 | tf_op jit(solution)/shard_map/ppermute | solution.py:38
  134.6 19.3 %collective-permute-start.17 = (f32[2,48,8,256]{3,2,1,0:T(8,128)S(1)}, f32[2,48,8,256]{3,2,1,0:T(8,128)S(1)}, u32[]{:S(2)}, u32[]{:S(2)}) collective-permute-start(f32[2,48,8,256]{3,2,1,0:T(8,128)S(1)} %get-tuple-element.81), channel_id=1, source_target_pairs={{1,2},{2,1},{3,4},{4,3},{5,6},{6,5},{9,10},{10,9},{11,12},{12,11},... | collective-permute-start | bytes 2359304 | tf_op jit(solution)/shard_map/ppermute | solution.py:39
  137.7 9.2 %collective-permute-start.12 = (f32[1,16,32,128]{3,2,1,0:T(8,128)S(1)}, f32[1,16,32,128]{3,2,1,0:T(8,128)S(1)}, u32[]{:S(2)}, u32[]{:S(2)}) collective-permute-start(f32[1,16,32,128]{3,2,1,0:T(8,128)S(1)} %get-tuple-element.70), channel_id=1, source_target_pairs={{0,8},{8,0},{16,24},{24,16},{32,40},{40,32},{48,56},{56,48},{1,9},... | collective-permute-start | bytes 786440 | tf_op jit(solution)/shard_map/ppermute | solution.py:38
  137.8 13.1 %collective-permute-start.13 = (f32[1,16,32,128]{3,2,1,0:T(8,128)S(1)}, f32[1,16,32,128]{3,2,1,0:T(8,128)S(1)}, u32[]{:S(2)}, u32[]{:S(2)}) collective-permute-start(f32[1,16,32,128]{3,2,1,0:T(8,128)S(1)} %get-tuple-element.71), channel_id=1, source_target_pairs={{8,16},{16,8},{24,32},{32,24},{40,48},{48,40},{9,17},{17,9},{25,33... | collective-permute-start | bytes 786440 | tf_op jit(solution)/shard_map/ppermute | solution.py:39
  151.6 20.3 %collective-permute-start.18 = (f32[1,64,16,128]{3,2,1,0:T(8,128)S(1)}, f32[1,64,16,128]{3,2,1,0:T(8,128)S(1)}, u32[]{:S(2)}, u32[]{:S(2)}) collective-permute-start(f32[1,64,16,128]{3,2,1,0:T(8,128)S(1)} %get-tuple-element.72), channel_id=1, source_target_pairs={{0,1},{1,0},{2,3},{3,2},{4,5},{5,4},{6,7},{7,6},{8,9},{9,8},{10,11... | collective-permute-start | bytes 1572872 | tf_op jit(solution)/shard_map/ppermute | solution.py:38
  151.7 20.1 %collective-permute-start.19 = (f32[1,64,16,128]{3,2,1,0:T(8,128)S(1)}, f32[1,64,16,128]{3,2,1,0:T(8,128)S(1)}, u32[]{:S(2)}, u32[]{:S(2)}) collective-permute-start(f32[1,64,16,128]{3,2,1,0:T(8,128)S(1)} %get-tuple-element.73), channel_id=1, source_target_pairs={{1,2},{2,1},{3,4},{4,3},{5,6},{6,5},{9,10},{10,9},{11,12},{12,11},... | collective-permute-start | bytes 1572872 | tf_op jit(solution)/shard_map/ppermute | solution.py:39
  171.9 30.9 %collective-permute-start.20 = (f32[32,32,256]{2,1,0:T(8,128)S(1)}, f32[32,32,256]{2,1,0:T(8,128)S(1)}, u32[]{:S(2)}, u32[]{:S(2)}) collective-permute-start(f32[32,32,256]{2,1,0:T(8,128)S(1)} %shard_map.115.ours), channel_id=1, source_target_pairs={{0,64},{64,0},{1,65},{65,1},{2,66},{66,2},{3,67},{67,3},{4,68},{68... | collective-permute-start | bytes 3145736 | tf_op jit(solution)/shard_map/ppermute | solution.py:574
  174.6 28.2 %copy-start.3 = (f32[32,32,256]{2,1,0:T(8,128)S(1)}, f32[32,32,256]{2,1,0:T(8,128)}, u32[]{:S(2)}) copy-start(f32[32,32,256]{2,1,0:T(8,128)} %coef.1) | copy-start | bytes 3145732
  174.6 28.2 %copy-start.13 = (f32[32,32,256]{2,1,0:T(8,128)S(1)}, f32[32,32,256]{2,1,0:T(8,128)}, u32[]{:S(2)}) copy-start(f32[32,32,256]{2,1,0:T(8,128)} %noise.1) | copy-start | bytes 3145732
  195.5 7.3 %collective-permute-start.21 = (f32[8,32,128]{2,1,0:T(8,128)S(1)}, f32[8,32,128]{2,1,0:T(8,128)S(1)}, u32[]{:S(2)}, u32[]{:S(2)}) collective-permute-start(f32[8,32,128]{2,1,0:T(8,128)S(1)} %shard_map.116.thin_ours), channel_id=1, source_target_pairs={{0,64},{64,0},{1,65},{65,1},{2,66},{66,2},{3,67},{67,3},{4,68},{68... | collective-permute-start | bytes 393224 | tf_op jit(solution)/shard_map/ppermute | solution.py:576
  (11 other events, 23.5 us)

commit v4 on v3

--- a/solution.py
+++ b/solution.py
@@ -11,7 +11,7 @@
 STEPS = 16
 DEPTH = 2
 K = 8
-UNROLL = 8
+UNROLL = 32
 THIN = 32
 MARK = 64
 COEF_HALOS = 6
@@ -182,11 +182,11 @@
             for g in range(groups)
         ]
 
-    def row(x, target, half, inside, below, centre, above):
+    def row(x, target, half, inside, below, centre, above, short):
         ups = [[pltpu.roll(c, 7, 0) for c in line_of] for line_of in centre]
         downs = [[pltpu.roll(c, 1, 0) for c in line_of] for line_of in centre]
         done = []
-        for g in range(groups):
+        for g in range(1, groups - 1) if short else range(groups):
             lefts = [pltpu.roll(c, 127, 1) for c in centre[g]]
             rights = [pltpu.roll(c, 1, 1) for c in centre[g]]
             for h in range(halves):
@@ -212,26 +212,44 @@
                 if not adjoint and h == 0:
                     surface[mine] = jnp.where(lane == DEPTH, fresh, pltpu.roll(surface[mine], 1, 1))
 
-    def sweep(source, target, half):
-        def rows_from(begin, count, unroll, inside):
-            def body(index, carried):
-                below, centre = carried
-                for offset in range(unroll):
-                    x = begin + index * unroll + offset
-                    above = load(source, x + 1)
-                    row(x, target, half, inside, below, centre, above)
-                    below, centre = centre, above
-                return below, centre
-
-            lax.fori_loop(0, count, body, (load(source, begin - 1), load(source, begin)))
-
-        count = K // 2 - turn_of - half
-        rows_from(edge - 2 * count, count, 2, False)
-        rows_from(edge, rows // UNROLL, UNROLL, True)
-        rows_from(edge + rows, count, 2, False)
-
-    sweep(first, second, 0)
-    sweep(second, first, 1)
+    def some_rows(source, target, half, first_row, many, inside, carried, short=False):
+        below, centre = carried
+        for x in range(many):
+            above = load(source, first_row + x + 1)
+            row(first_row + x, target, half, inside, below, centre, above, short)
+            below, centre = centre, above
+        return below, centre
+
+    def start_at(source, x):
+        return load(source, x - 1), load(source, x)
+
+    def halo_rows(source, target, half, count):
+        def body(index, carried):
+            for x in (edge - 2 * count + 2 * index, edge + rows + 2 * index):
+                some_rows(source, target, half, x, 2, False, start_at(source, x))
+            return carried
+
+        lax.fori_loop(0, count, body, 0)
+
+    def own_rows(source, target, half, short=False):
+        def body(index, carried):
+            x = edge + index * UNROLL
+            return some_rows(source, target, half, x, UNROLL, True, carried, short)
+
+        lax.fori_loop(0, rows // UNROLL, body, start_at(source, edge))
+
+    last = turn_of == K // 2 - 1
+    halo_rows(first, second, 0, K // 2 - turn_of)
+    own_rows(first, second, 0)
+
+    @pl.when(jnp.logical_not(last))
+    def _():
+        halo_rows(second, first, 1, K // 2 - 1 - turn_of)
+        own_rows(second, first, 1)
+
+    @pl.when(last)
+    def _():
+        own_rows(second, first, 1, True)
 
     if not gather:
 

time: 206 us -> 193 us (0.937)
  Pallas kernels: 110 us -> 97.1 us
    pallas_call x4, Pallas kernels: 76 us -> 63.2 us  [run_block(): pl.pallas_call(functools.partial(block_kernel, coef.shape, adjoint, gathe...]
  transfers between devices with their start and end apart: 23 -> 23, of which waited for: 6 -> 6; matrix products, arithmetic and copies ran while one was open for 1% -> 1% of each run, Pallas kernels for 41% -> 39%
where the time goes in v4:
time: 193 us; the launch traced here: 192 us
  Pallas kernels  97.1 us (50%)
  starting transfers between devices  46.5 us (24%)
  waiting for transfers between devices  37.3 us (19%)
  local copies, waits for them, and re-layouts  6.7 us (3%)
    pallas_call x4, Pallas kernels, run_block(): pl.pallas_call(functools.partial(block_kernel, coef.shape, adjoint, gathe...  63.2 us
    ppermute x10, starting transfers between devices, swap(): lax.ppermute(second, axis, pairs(count, True))  30.9 us
    pallas_call x1, Pallas kernels, run_thin(): pl.pallas_call(functools.partial(thin_kernel, own.shape), grid=(STEPS //...  20.9 us
    ppermute x10, waiting for transfers between devices, swap(): lax.ppermute(second, axis, pairs(count, True))  14.2 us
    all_to_all x1, waiting for transfers between devices, receivers(): lax.all_to_all(outgoing.reshape(tile_count, per_tile, 128), ('gx', 'gy'),...  11.3 us
    pallas_call x8, Pallas kernels, strips(): pl.pallas_call(functools.partial(strip_kernel, (rows, cols), axis, width,...  11 us
    all_to_all x1, starting transfers between devices, receivers(): lax.all_to_all(outgoing.reshape(tile_count, per_tile, 128), ('gx', 'gy'),...  7.32 us
    unnamed x38, local copies, waits for them, and re-layouts  6.68 us
  transfers between devices with their start and end apart: 23, of which 6 were waited for; matrix products, arithmetic and copies ran while one was open for 1% of the time, Pallas kernels for 39%

profile of v4, /device:TPU:10, one launch (start us, length us, event | category | flops | bytes accessed | tf_op | source)
XLA Modules:
  0.0 191.9 jit_solution(1085572997904301213)
XLA Ops:
  1.3 4.0 %shard_map.104 = (f32[5,8,32,256]{3,2,1,0:T(8,128)}, f32[5,8,32,256]{3,2,1,0:T(8,128)}) custom-call(s32[2]{0:T(128)} %pad_add_fusion.parity, f32[32,32,256]{2,1,0:T(8,128)} %bitcast.16, f32[32,32,256]{2,1,0:T(8,128)} %bitcast.19, f32[32,32,256]{2,1,0:T(8,128)} %coef.1, f32[32,32,256]{2,1,0:T(8,128)} %bitcast.22, f32[32,32,256]{2,1,0:T(8,128)} %bitcast.25), custom_call_target="tpu_custom_call" | custom-call | tf_op jit(solution)/shard_map/pallas_call | solution.py:79
  5.4 2.0 %collective-permute-start = (f32[5,8,32,256]{3,2,1,0:T(8,128)}, f32[5,8,32,256]{3,2,1,0:T(8,128)S(1)}, u32[]{:S(2)}, u32[]{:S(2)}) collective-permute-start(f32[5,8,32,256]{3,2,1,0:T(8,128)} %get-tuple-element.44), channel_id=1, source_target_pairs={{0,8},{8,0},{16,24},{24,16},{32,40},{40,32},{48,56},{56,48},{1,9},... | collective-permute-start | bytes 3932168 | tf_op jit(solution)/shard_map/ppermute | solution.py:38
  7.4 4.3 %collective-permute-start.1 = (f32[5,8,32,256]{3,2,1,0:T(8,128)}, f32[5,8,32,256]{3,2,1,0:T(8,128)S(1)}, u32[]{:S(2)}, u32[]{:S(2)}) collective-permute-start(f32[5,8,32,256]{3,2,1,0:T(8,128)} %get-tuple-element.45), channel_id=1, source_target_pairs={{8,16},{16,8},{24,32},{32,24},{40,48},{48,40},{9,17},{17,9},{25,33... | collective-permute-start | bytes 3932168 | tf_op jit(solution)/shard_map/ppermute | solution.py:39
  11.7 1.2 copy-done.2
  12.9 1.2 copy-done.4
  14.1 1.2 copy-done.6
  15.4 1.2 copy-done.7
  16.6 1.2 copy-done.9
  17.8 2.3 %shard_map.105 = (f32[5,32,8,256]{3,2,1,0:T(8,128)}, f32[5,32,8,256]{3,2,1,0:T(8,128)}) custom-call(s32[2]{0:T(128)S(1)} %copy-done.15, f32[32,32,256]{2,1,0:T(8,128)S(1)} %bitcast.17, f32[32,32,256]{2,1,0:T(8,128)S(1)} %bitcast.21, f32[32,32,256]{2,1,0:T(8,128)S(1)} %copy-done.2, f32[32,32,256]{2,1,0:T(8,128)S(1)} %bitcast.23, f32[32,32,256]{2,1,0:T(8,128)S(1)} %bitcast.27), custom_call_target="tpu_custom_call" | custom-call | tf_op jit(solution)/shard_map/pallas_call | solution.py:79
  20.3 2.5 %collective-permute-start.3 = (f32[5,32,8,256]{3,2,1,0:T(8,128)}, f32[5,32,8,256]{3,2,1,0:T(8,128)}, u32[]{:S(2)}, u32[]{:S(2)}) collective-permute-start(f32[5,32,8,256]{3,2,1,0:T(8,128)} %get-tuple-element.48), channel_id=1, source_target_pairs={{1,2},{2,1},{3,4},{4,3},{5,6},{6,5},{9,10},{10,9},{11,12},{12,11},... | collective-permute-start | bytes 3932168 | tf_op jit(solution)/shard_map/ppermute | solution.py:39
  24.1 7.3 %all-to-all-start = ((f32[64,2,128]{2,1,0:T(2,128)}), f32[64,2,128]{2,1,0:T(2,128)S(1)}, u32[]{:S(2)}, u32[]{:S(2)}) async-start(f32[64,2,128]{2,1,0:T(2,128)} %bitcast.8), calls=%async_computation | async-start | bytes 131072 | tf_op jit(solution)/shard_map/all_to_all | solution.py:530
  31.5 11.3 %all-to-all-done = f32[64,2,128]{2,1,0:T(2,128)S(1)} async-done(((f32[64,2,128]{2,1,0:T(2,128)}), f32[64,2,128]{2,1,0:T(2,128)S(1)}, u32[]{:S(2)}, u32[]{:S(2)}) %all-to-all-start) | async-done | bytes 65568 | tf_op jit(solution)/shard_map/all_to_all | solution.py:530
  45.0 3.0 %collective-permute-start.5 = (f32[5,16,8,256]{3,2,1,0:T(8,128)S(1)}, f32[5,16,8,256]{3,2,1,0:T(8,128)S(1)}, u32[]{:S(2)}, u32[]{:S(2)}) collective-permute-start(f32[5,16,8,256]{3,2,1,0:T(8,128)S(1)} %get-tuple-element.52), channel_id=1, source_target_pairs={{1,2},{2,1},{3,4},{4,3},{5,6},{6,5},{9,10},{10,9},{11,12},{12,11},... | collective-permute-start | bytes 1966088 | tf_op jit(solution)/shard_map/ppermute | solution.py:39
  48.1 8.8 %collective-permute-done.5.refs_8_.refs_14_.refs_12_ = f32[5,16,8,256]{3,2,1,0:T(8,128)S(1)} collective-permute-done((f32[5,16,8,256]{3,2,1,0:T(8,128)S(1)}, f32[5,16,8,256]{3,2,1,0:T(8,128)S(1)}, u32[]{:S(2)}, u32[]{:S(2)}) %collective-permute-start.5) | collective-permute-done | bytes 655392 | tf_op jit(solution)/shard_map/ppermute | solution.py:39
  56.9 15.9 %shard_map.107 = (f32[32,32,256]{2,1,0:T(8,128)S(1)}, f32[32,32,256]{2,1,0:T(8,128)S(1)}, f32[2,8,32,256]{3,2,1,0:T(8,128)S(1)}, f32[2,8,32,256]{3,2,1,0:T(8,128...) custom-call(s32[2]{0:T(128)S(1)} %copy-done.15, f32[32,32,256]{2,1,0:T(8,128)S(1)} %bitcast.18, ...), custom_call_target="tpu_custom_call" | custom-call | flops 100000000 | bytes 60000000 | tf_op jit(solution)/shard_map/pallas_call | solution.py:305
  73.7 4.5 %collective-permute-start.7 = (f32[2,8,32,256]{3,2,1,0:T(8,128)S(1)}, f32[2,8,32,256]{3,2,1,0:T(8,128)S(1)}, u32[]{:S(2)}, u32[]{:S(2)}) collective-permute-start(f32[2,8,32,256]{3,2,1,0:T(8,128)S(1)} %get-tuple-element.57), channel_id=1, source_target_pairs={{8,16},{16,8},{24,32},{32,24},{40,48},{48,40},{9,17},{17,9},{25,33... | collective-permute-start | bytes 1572872 | tf_op jit(solution)/shard_map/ppermute | solution.py:39
  79.1 2.6 %collective-permute-start.9 = (f32[2,32,8,256]{3,2,1,0:T(8,128)S(1)}, f32[2,32,8,256]{3,2,1,0:T(8,128)S(1)}, u32[]{:S(2)}, u32[]{:S(2)}) collective-permute-start(f32[2,32,8,256]{3,2,1,0:T(8,128)S(1)} %get-tuple-element.60), channel_id=1, source_target_pairs={{1,2},{2,1},{3,4},{4,3},{5,6},{6,5},{9,10},{10,9},{11,12},{12,11},... | collective-permute-start | bytes 1572872 | tf_op jit(solution)/shard_map/ppermute | solution.py:39
  81.7 15.7 %shard_map.109 = (f32[32,32,256]{2,1,0:T(8,128)S(1)}, f32[32,32,256]{2,1,0:T(8,128)S(1)}, f32[2,8,32,256]{3,2,1,0:T(8,128)S(1)}, f32[2,8,32,256]{3,2,1,0:T(8,128)S(1)}, f32[8,32,32,256]{3,2,1,0:T(8,128)}) custom-call(s32[2]{0:T(128)S(1)} %copy-done.15, f32[32,32,256]{2,1,0:T(8,128)S(1)} %bitcast.24, f32[32,32,256]{2,1,0:T(8,128)} %bitcast.26, ...), custom_call_target="tpu_custom_call" | custom-call | flops 100000000 | bytes 60000000 | tf_op jit(solution)/shard_map/pallas_call | solution.py:305
  98.9 2.4 %collective-permute-start.11 = (f32[2,16,8,256]{3,2,1,0:T(8,128)S(1)}, f32[2,16,8,256]{3,2,1,0:T(8,128)S(1)}, u32[]{:S(2)}, u32[]{:S(2)}) collective-permute-start(f32[2,16,8,256]{3,2,1,0:T(8,128)S(1)} %get-tuple-element.66), channel_id=1, source_target_pairs={{1,2},{2,1},{3,4},{4,3},{5,6},{6,5},{9,10},{10,9},{11,12},{12,11},... | collective-permute-start | bytes 786440 | tf_op jit(solution)/shard_map/ppermute | solution.py:39
  101.5 3.6 %collective-permute-start.15 = (f32[2,8,32,256]{3,2,1,0:T(8,128)S(1)}, f32[2,8,32,256]{3,2,1,0:T(8,128)S(1)}, u32[]{:S(2)}, u32[]{:S(2)}) collective-permute-start(f32[2,8,32,256]{3,2,1,0:T(8,128)S(1)} %get-tuple-element.78), channel_id=1, source_target_pairs={{8,16},{16,8},{24,32},{32,24},{40,48},{48,40},{9,17},{17,9},{25,33... | collective-permute-start | bytes 1572872 | tf_op jit(solution)/shard_map/ppermute | solution.py:39
  105.3 1.3 collective-permute-done.11.refs_8_
  106.6 16.6 %shard_map.111 = (f32[32,32,256]{2,1,0:T(8,128)S(1)}, f32[8,32,32,128]{3,2,1,0:T(8,128)}, f32[32,32,128]{2,1,0:T(8,128)S(1)}) custom-call(s32[2]{0:T(128)S(1)} %copy-done.15, f32[32,32,256]{2,1,0:T(8,128)} %copy-done.10, f32[32,32,256]{2,1,0:T(8,128)} %copy-done.11, f32[32,32,256]{2,1,0:T(8,128)} %coef.1, ...), custom_call_target="tpu_custom_call" | custom-call | flops 100000000 | bytes 60000000 | tf_op jit(solution)/shard_map/pallas_call | solution.py:305
  124.7 2.3 %collective-permute-start.17 = (f32[2,48,8,256]{3,2,1,0:T(8,128)S(1)}, f32[2,48,8,256]{3,2,1,0:T(8,128)S(1)}, u32[]{:S(2)}, u32[]{:S(2)}) collective-permute-start(f32[2,48,8,256]{3,2,1,0:T(8,128)S(1)} %get-tuple-element.81), channel_id=1, source_target_pairs={{1,2},{2,1},{3,4},{4,3},{5,6},{6,5},{9,10},{10,9},{11,12},{12,11},... | collective-permute-start | bytes 2359304 | tf_op jit(solution)/shard_map/ppermute | solution.py:39
  127.9 3.6 %collective-permute-start.13 = (f32[1,16,32,128]{3,2,1,0:T(8,128)S(1)}, f32[1,16,32,128]{3,2,1,0:T(8,128)S(1)}, u32[]{:S(2)}, u32[]{:S(2)}) collective-permute-start(f32[1,16,32,128]{3,2,1,0:T(8,128)S(1)} %get-tuple-element.71), channel_id=1, source_target_pairs={{8,16},{16,8},{24,32},{32,24},{40,48},{48,40},{9,17},{17,9},{25,33... | collective-permute-start | bytes 786440 | tf_op jit(solution)/shard_map/ppermute | solution.py:39
  131.6 5.5 %collective-permute-done.12.refs_1_.refs_0_ = f32[1,16,32,128]{3,2,1,0:T(8,128)S(1)} collective-permute-done((f32[1,16,32,128]{3,2,1,0:T(8,128)S(1)}, f32[1,16,32,128]{3,2,1,0:T(8,128)S(1)}, u32[]{:S(2)}, u32[]{:S(2)}) %collective-permute-start.12) | collective-permute-done | bytes 262176 | tf_op jit(solution)/shard_map/ppermute | solution.py:38
  137.0 4.0 %collective-permute-done.13.refs_2_.refs_1_ = f32[1,16,32,128]{3,2,1,0:T(8,128)S(1)} collective-permute-done((f32[1,16,32,128]{3,2,1,0:T(8,128)S(1)}, f32[1,16,32,128]{3,2,1,0:T(8,128)S(1)}, u32[]{:S(2)}, u32[]{:S(2)}) %collective-permute-start.13) | collective-permute-done | bytes 262176 | tf_op jit(solution)/shard_map/ppermute | solution.py:39
  141.9 1.9 collective-permute-start.19
  143.8 15.1 %shard_map.115.ours = f32[32,32,256]{2,1,0:T(8,128)S(1)} custom-call(s32[2]{0:T(128)S(1)} %copy-done.15, f32[32,32,256]{2,1,0:T(8,128)S(1)} %get-tuple-element.75.refs_0_, f32[32,32,256]{2,1,0:T(8,128)} %copy-done.12, f32[32,32,256]{2,1,0:T(8,128)} %coef.1, f32[2,8,32,256]{3,2,1,0:T(8,128)S(1)} %collective-permute-done.14.refs_2_.refs_3_, ...), custom_call_target="tpu_custom_call" | custom-call | flops 100000000 | bytes 60000000 | tf_op jit(solution)/shard_map/pallas_call | solution.py:305
  158.9 2.7 %collective-permute-start.20 = (f32[32,32,256]{2,1,0:T(8,128)S(1)}, f32[32,32,256]{2,1,0:T(8,128)S(1)}, u32[]{:S(2)}, u32[]{:S(2)}) collective-permute-start(f32[32,32,256]{2,1,0:T(8,128)S(1)} %shard_map.115.ours), channel_id=1, source_target_pairs={{0,64},{64,0},{1,65},{65,1},{2,66},{66,2},{3,67},{67,3},{4,68},{68... | collective-permute-start | bytes 3145736 | tf_op jit(solution)/shard_map/ppermute | solution.py:592
  161.7 20.9 %shard_map.116.thin_ours = f32[8,32,128]{2,1,0:T(8,128)S(1)} custom-call(s32[2]{0:T(128)S(1)} %copy-done.15, f32[32,32,128]{2,1,0:T(8,128)S(1)} %pad_add_fusion.1.refs_0_.own, f32[1,16,32,128]{3,2,1,0:T(8,128)S(1)} %collective-permute-done.12.refs_1_.refs_0_, f32[1,16,32,128]{3,2,1,0:T(8,128)S(1)} %collective-permute-done.13.refs_2_.refs_1_, ...), custom_call_target="tpu_custom_call" | custom-call | flops 100000000 | bytes 50000000 | tf_op jit(solution)/shard_map/pallas_call | solution.py:440
  183.5 6.3 %collective-permute-done.21.thin_theirs = f32[8,32,128]{2,1,0:T(8,128)S(1)} collective-permute-done((f32[8,32,128]{2,1,0:T(8,128)S(1)}, f32[8,32,128]{2,1,0:T(8,128)S(1)}, u32[]{:S(2)}, u32[]{:S(2)}) %collective-permute-start.21) | collective-permute-done | bytes 131104 | tf_op jit(solution)/shard_map/ppermute | solution.py:594
  189.8 2.0 %shard_map.117 = (f32[32,32,256]{2,1,0:T(8,128)}, f32[32,32,256]{2,1,0:T(8,128)}) custom-call(f32[32,32,256]{2,1,0:T(8,128)S(1)} %shard_map.115.ours, f32[32,32,256]{2,1,0:T(8,128)S(1)} %collective-permute-done.20.theirs, f32[8,32,128]{2,1,0:T(8,128)S(1)} %shard_map.116.thin_ours, f32[8,32,128]{2,1,0:T(8,128)S(1)} %collective-permute-done.21.thin_theirs, ...), custom_call_target="tpu_custom_call" | custom-call | tf_op jit(solution)/shard_map/pallas_call | solution.py:497
  (83 shorter events, 11.8 us)
Async XLA Ops:
  1.3 10.4 %copy-start.15 = (s32[2]{0:T(128)S(1)}, s32[2]{0:T(128)}, u32[]{:S(2)}) copy-start(s32[2]{0:T(128)} %pad_add_fusion.parity) | copy-start | bytes 28
  5.4 38.0 %collective-permute-start = (f32[5,8,32,256]{3,2,1,0:T(8,128)}, f32[5,8,32,256]{3,2,1,0:T(8,128)S(1)}, u32[]{:S(2)}, u32[]{:S(2)}) collective-permute-start(f32[5,8,32,256]{3,2,1,0:T(8,128)} %get-tuple-element.44), channel_id=1, source_target_pairs={{0,8},{8,0},{16,24},{24,16},{32,40},{40,32},{48,56},{56,48},{1,9},... | collective-permute-start | bytes 3932168 | tf_op jit(solution)/shard_map/ppermute | solution.py:38
  7.4 36.0 %collective-permute-start.1 = (f32[5,8,32,256]{3,2,1,0:T(8,128)}, f32[5,8,32,256]{3,2,1,0:T(8,128)S(1)}, u32[]{:S(2)}, u32[]{:S(2)}) collective-permute-start(f32[5,8,32,256]{3,2,1,0:T(8,128)} %get-tuple-element.45), channel_id=1, source_target_pairs={{8,16},{16,8},{24,32},{32,24},{40,48},{48,40},{9,17},{17,9},{25,33... | collective-permute-start | bytes 3932168 | tf_op jit(solution)/shard_map/ppermute | solution.py:39
  17.8 5.4 %copy-start.18 = (s32[64]{0:T(128)S(1)}, s32[64]{0:T(128)}, u32[]{:S(2)}) copy-start(s32[64]{0:T(128)} %param.17) | copy-start | bytes 772
  20.2 27.9 %collective-permute-start.2 = (f32[5,32,8,256]{3,2,1,0:T(8,128)}, f32[5,32,8,256]{3,2,1,0:T(8,128)}, u32[]{:S(2)}, u32[]{:S(2)}) collective-permute-start(f32[5,32,8,256]{3,2,1,0:T(8,128)} %get-tuple-element.47), channel_id=1, source_target_pairs={{0,1},{1,0},{2,3},{3,2},{4,5},{5,4},{6,7},{7,6},{8,9},{9,8},{10,11... | collective-permute-start | bytes 3932168 | tf_op jit(solution)/shard_map/ppermute | solution.py:38
  20.3 27.8 %collective-permute-start.3 = (f32[5,32,8,256]{3,2,1,0:T(8,128)}, f32[5,32,8,256]{3,2,1,0:T(8,128)}, u32[]{:S(2)}, u32[]{:S(2)}) collective-permute-start(f32[5,32,8,256]{3,2,1,0:T(8,128)} %get-tuple-element.48), channel_id=1, source_target_pairs={{1,2},{2,1},{3,4},{4,3},{5,6},{6,5},{9,10},{10,9},{11,12},{12,11},... | collective-permute-start | bytes 3932168 | tf_op jit(solution)/shard_map/ppermute | solution.py:39
  24.1 18.6 %all-to-all-start = ((f32[64,2,128]{2,1,0:T(2,128)}), f32[64,2,128]{2,1,0:T(2,128)S(1)}, u32[]{:S(2)}, u32[]{:S(2)}) async-start(f32[64,2,128]{2,1,0:T(2,128)} %bitcast.8), calls=%async_computation | async-start | bytes 131072 | tf_op jit(solution)/shard_map/all_to_all | solution.py:530
  43.3 13.6 %copy-start.5 = (f32[1,32,32,256]{3,2,1,0:T(8,128)S(1)}, f32[1,32,32,256]{3,2,1,0:T(8,128)}, u32[]{:S(2)}) copy-start(f32[1,32,32,256]{3,2,1,0:T(8,128)} %param.10) | copy-start | bytes 3145732
  44.9 3.2 %collective-permute-start.4 = (f32[5,16,8,256]{3,2,1,0:T(8,128)S(1)}, f32[5,16,8,256]{3,2,1,0:T(8,128)S(1)}, u32[]{:S(2)}, u32[]{:S(2)}) collective-permute-start(f32[5,16,8,256]{3,2,1,0:T(8,128)S(1)} %get-tuple-element.51), channel_id=1, source_target_pairs={{0,1},{1,0},{2,3},{3,2},{4,5},{5,4},{6,7},{7,6},{8,9},{9,8},{10,11... | collective-permute-start | bytes 1966088 | tf_op jit(solution)/shard_map/ppermute | solution.py:38
  45.0 11.9 %collective-permute-start.5 = (f32[5,16,8,256]{3,2,1,0:T(8,128)S(1)}, f32[5,16,8,256]{3,2,1,0:T(8,128)S(1)}, u32[]{:S(2)}, u32[]{:S(2)}) collective-permute-start(f32[5,16,8,256]{3,2,1,0:T(8,128)S(1)} %get-tuple-element.52), channel_id=1, source_target_pairs={{1,2},{2,1},{3,4},{4,3},{5,6},{6,5},{9,10},{10,9},{11,12},{12,11},... | collective-permute-start | bytes 1966088 | tf_op jit(solution)/shard_map/ppermute | solution.py:39
  72.9 24.5 %copy-start.10 = (f32[32,32,256]{2,1,0:T(8,128)}, f32[32,32,256]{2,1,0:T(8,128)S(1)}, u32[]{:S(2)}) copy-start(f32[32,32,256]{2,1,0:T(8,128)S(1)} %get-tuple-element.54.refs_0_) | copy-start | bytes 3145732
  72.9 24.5 %copy-start.11 = (f32[32,32,256]{2,1,0:T(8,128)}, f32[32,32,256]{2,1,0:T(8,128)S(1)}, u32[]{:S(2)}) copy-start(f32[32,32,256]{2,1,0:T(8,128)S(1)} %get-tuple-element.55.refs_1_) | copy-start | bytes 3145732
  72.9 8.8 %copy-start.8 = (f32[1,32,32,256]{3,2,1,0:T(8,128)S(1)}, f32[1,32,32,256]{3,2,1,0:T(8,128)}, u32[]{:S(2)}) copy-start(f32[1,32,32,256]{3,2,1,0:T(8,128)} %param.12) | copy-start | bytes 3145732
  72.9 24.5 %collective-permute-start.6 = (f32[2,8,32,256]{3,2,1,0:T(8,128)S(1)}, f32[2,8,32,256]{3,2,1,0:T(8,128)S(1)}, u32[]{:S(2)}, u32[]{:S(2)}) collective-permute-start(f32[2,8,32,256]{3,2,1,0:T(8,128)S(1)} %get-tuple-element.56), channel_id=1, source_target_pairs={{0,8},{8,0},{16,24},{24,16},{32,40},{40,32},{48,56},{56,48},{1,9},... | collective-permute-start | bytes 1572872 | tf_op jit(solution)/shard_map/ppermute | solution.py:38
  73.7 23.7 %collective-permute-start.7 = (f32[2,8,32,256]{3,2,1,0:T(8,128)S(1)}, f32[2,8,32,256]{3,2,1,0:T(8,128)S(1)}, u32[]{:S(2)}, u32[]{:S(2)}) collective-permute-start(f32[2,8,32,256]{3,2,1,0:T(8,128)S(1)} %get-tuple-element.57), channel_id=1, source_target_pairs={{8,16},{16,8},{24,32},{32,24},{40,48},{48,40},{9,17},{17,9},{25,33... | collective-permute-start | bytes 1572872 | tf_op jit(solution)/shard_map/ppermute | solution.py:39
  78.9 22.6 %collective-permute-start.8 = (f32[2,32,8,256]{3,2,1,0:T(8,128)S(1)}, f32[2,32,8,256]{3,2,1,0:T(8,128)S(1)}, u32[]{:S(2)}, u32[]{:S(2)}) collective-permute-start(f32[2,32,8,256]{3,2,1,0:T(8,128)S(1)} %get-tuple-element.59), channel_id=1, source_target_pairs={{0,1},{1,0},{2,3},{3,2},{4,5},{5,4},{6,7},{7,6},{8,9},{9,8},{10,11... | collective-permute-start | bytes 1572872 | tf_op jit(solution)/shard_map/ppermute | solution.py:38
  79.1 26.2 %collective-permute-start.9 = (f32[2,32,8,256]{3,2,1,0:T(8,128)S(1)}, f32[2,32,8,256]{3,2,1,0:T(8,128)S(1)}, u32[]{:S(2)}, u32[]{:S(2)}) collective-permute-start(f32[2,32,8,256]{3,2,1,0:T(8,128)S(1)} %get-tuple-element.60), channel_id=1, source_target_pairs={{1,2},{2,1},{3,4},{4,3},{5,6},{6,5},{9,10},{10,9},{11,12},{12,11},... | collective-permute-start | bytes 1572872 | tf_op jit(solution)/shard_map/ppermute | solution.py:39
  97.4 26.1 %copy-start.12 = (f32[32,32,256]{2,1,0:T(8,128)}, f32[32,32,256]{2,1,0:T(8,128)S(1)}, u32[]{:S(2)}) copy-start(f32[32,32,256]{2,1,0:T(8,128)S(1)} %get-tuple-element.76.refs_1_) | copy-start | bytes 3145732
  98.2 7.1 %collective-permute-start.10 = (f32[2,16,8,256]{3,2,1,0:T(8,128)S(1)}, f32[2,16,8,256]{3,2,1,0:T(8,128)S(1)}, u32[]{:S(2)}, u32[]{:S(2)}) collective-permute-start(f32[2,16,8,256]{3,2,1,0:T(8,128)S(1)} %get-tuple-element.65), channel_id=1, source_target_pairs={{0,1},{1,0},{2,3},{3,2},{4,5},{5,4},{6,7},{7,6},{8,9},{9,8},{10,11... | collective-permute-start | bytes 786440 | tf_op jit(solution)/shard_map/ppermute | solution.py:38
  98.9 7.7 %collective-permute-start.11 = (f32[2,16,8,256]{3,2,1,0:T(8,128)S(1)}, f32[2,16,8,256]{3,2,1,0:T(8,128)S(1)}, u32[]{:S(2)}, u32[]{:S(2)}) collective-permute-start(f32[2,16,8,256]{3,2,1,0:T(8,128)S(1)} %get-tuple-element.66), channel_id=1, source_target_pairs={{1,2},{2,1},{3,4},{4,3},{5,6},{6,5},{9,10},{10,9},{11,12},{12,11},... | collective-permute-start | bytes 786440 | tf_op jit(solution)/shard_map/ppermute | solution.py:39
  101.4 22.1 %collective-permute-start.14 = (f32[2,8,32,256]{3,2,1,0:T(8,128)S(1)}, f32[2,8,32,256]{3,2,1,0:T(8,128)S(1)}, u32[]{:S(2)}, u32[]{:S(2)}) collective-permute-start(f32[2,8,32,256]{3,2,1,0:T(8,128)S(1)} %get-tuple-element.77), channel_id=1, source_target_pairs={{0,8},{8,0},{16,24},{24,16},{32,40},{40,32},{48,56},{56,48},{1,9},... | collective-permute-start | bytes 1572872 | tf_op jit(solution)/shard_map/ppermute | solution.py:38
  101.5 22.0 %collective-permute-start.15 = (f32[2,8,32,256]{3,2,1,0:T(8,128)S(1)}, f32[2,8,32,256]{3,2,1,0:T(8,128)S(1)}, u32[]{:S(2)}, u32[]{:S(2)}) collective-permute-start(f32[2,8,32,256]{3,2,1,0:T(8,128)S(1)} %get-tuple-element.78), channel_id=1, source_target_pairs={{8,16},{16,8},{24,32},{32,24},{40,48},{48,40},{9,17},{17,9},{25,33... | collective-permute-start | bytes 1572872 | tf_op jit(solution)/shard_map/ppermute | solution.py:39
  124.3 19.5 %collective-permute-start.16 = (f32[2,48,8,256]{3,2,1,0:T(8,128)S(1)}, f32[2,48,8,256]{3,2,1,0:T(8,128)S(1)}, u32[]{:S(2)}, u32[]{:S(2)}) collective-permute-start(f32[2,48,8,256]{3,2,1,0:T(8,128)S(1)} %get-tuple-element.80), channel_id=1, source_target_pairs={{0,1},{1,0},{2,3},{3,2},{4,5},{5,4},{6,7},{7,6},{8,9},{9,8},{10,11... | collective-permute-start | bytes 2359304 | tf_op jit(solution)/shard_map/ppermute | solution.py:38
  124.7 19.1 %collective-permute-start.17 = (f32[2,48,8,256]{3,2,1,0:T(8,128)S(1)}, f32[2,48,8,256]{3,2,1,0:T(8,128)S(1)}, u32[]{:S(2)}, u32[]{:S(2)}) collective-permute-start(f32[2,48,8,256]{3,2,1,0:T(8,128)S(1)} %get-tuple-element.81), channel_id=1, source_target_pairs={{1,2},{2,1},{3,4},{4,3},{5,6},{6,5},{9,10},{10,9},{11,12},{12,11},... | collective-permute-start | bytes 2359304 | tf_op jit(solution)/shard_map/ppermute | solution.py:39
  127.8 9.2 %collective-permute-start.12 = (f32[1,16,32,128]{3,2,1,0:T(8,128)S(1)}, f32[1,16,32,128]{3,2,1,0:T(8,128)S(1)}, u32[]{:S(2)}, u32[]{:S(2)}) collective-permute-start(f32[1,16,32,128]{3,2,1,0:T(8,128)S(1)} %get-tuple-element.70), channel_id=1, source_target_pairs={{0,8},{8,0},{16,24},{24,16},{32,40},{40,32},{48,56},{56,48},{1,9},... | collective-permute-start | bytes 786440 | tf_op jit(solution)/shard_map/ppermute | solution.py:38
  127.9 13.1 %collective-permute-start.13 = (f32[1,16,32,128]{3,2,1,0:T(8,128)S(1)}, f32[1,16,32,128]{3,2,1,0:T(8,128)S(1)}, u32[]{:S(2)}, u32[]{:S(2)}) collective-permute-start(f32[1,16,32,128]{3,2,1,0:T(8,128)S(1)} %get-tuple-element.71), channel_id=1, source_target_pairs={{8,16},{16,8},{24,32},{32,24},{40,48},{48,40},{9,17},{17,9},{25,33... | collective-permute-start | bytes 786440 | tf_op jit(solution)/shard_map/ppermute | solution.py:39
  141.8 17.1 %collective-permute-start.18 = (f32[1,64,16,128]{3,2,1,0:T(8,128)S(1)}, f32[1,64,16,128]{3,2,1,0:T(8,128)S(1)}, u32[]{:S(2)}, u32[]{:S(2)}) collective-permute-start(f32[1,64,16,128]{3,2,1,0:T(8,128)S(1)} %get-tuple-element.72), channel_id=1, source_target_pairs={{0,1},{1,0},{2,3},{3,2},{4,5},{5,4},{6,7},{7,6},{8,9},{9,8},{10,11... | collective-permute-start | bytes 1572872 | tf_op jit(solution)/shard_map/ppermute | solution.py:38
  141.9 17.0 %collective-permute-start.19 = (f32[1,64,16,128]{3,2,1,0:T(8,128)S(1)}, f32[1,64,16,128]{3,2,1,0:T(8,128)S(1)}, u32[]{:S(2)}, u32[]{:S(2)}) collective-permute-start(f32[1,64,16,128]{3,2,1,0:T(8,128)S(1)} %get-tuple-element.73), channel_id=1, source_target_pairs={{1,2},{2,1},{3,4},{4,3},{5,6},{6,5},{9,10},{10,9},{11,12},{12,11},... | collective-permute-start | bytes 1572872 | tf_op jit(solution)/shard_map/ppermute | solution.py:39
  158.9 30.9 %collective-permute-start.20 = (f32[32,32,256]{2,1,0:T(8,128)S(1)}, f32[32,32,256]{2,1,0:T(8,128)S(1)}, u32[]{:S(2)}, u32[]{:S(2)}) collective-permute-start(f32[32,32,256]{2,1,0:T(8,128)S(1)} %shard_map.115.ours), channel_id=1, source_target_pairs={{0,64},{64,0},{1,65},{65,1},{2,66},{66,2},{3,67},{67,3},{4,68},{68... | collective-permute-start | bytes 3145736 | tf_op jit(solution)/shard_map/ppermute | solution.py:592
  161.7 28.2 %copy-start.3 = (f32[32,32,256]{2,1,0:T(8,128)S(1)}, f32[32,32,256]{2,1,0:T(8,128)}, u32[]{:S(2)}) copy-start(f32[32,32,256]{2,1,0:T(8,128)} %coef.1) | copy-start | bytes 3145732
  161.7 28.2 %copy-start.13 = (f32[32,32,256]{2,1,0:T(8,128)S(1)}, f32[32,32,256]{2,1,0:T(8,128)}, u32[]{:S(2)}) copy-start(f32[32,32,256]{2,1,0:T(8,128)} %noise.1) | copy-start | bytes 3145732
  182.5 7.3 %collective-permute-start.21 = (f32[8,32,128]{2,1,0:T(8,128)S(1)}, f32[8,32,128]{2,1,0:T(8,128)S(1)}, u32[]{:S(2)}, u32[]{:S(2)}) collective-permute-start(f32[8,32,128]{2,1,0:T(8,128)S(1)} %shard_map.116.thin_ours), channel_id=1, source_target_pairs={{0,64},{64,0},{1,65},{65,1},{2,66},{66,2},{3,67},{67,3},{4,68},{68... | collective-permute-start | bytes 393224 | tf_op jit(solution)/shard_map/ppermute | solution.py:594
  (11 other events, 23.5 us)
